TPU v7x, 32 devices: a whole 2x2x4 slice. The times are simulated.
32 devices in a mesh: dp: 8 (over z, x), tensor: 4 (over y, core).
Axes of the slice: x: 2, y: 2, z: 4, core: 2. Of those that a mesh axis runs over, the one named last changes fastest.
Arguments:
- tokens: bfloat16 [4096, 2048], P(('dp', 'tensor')), may hold values from -6 to 6
- norm_gain1: float32 [2048], P(('dp', 'tensor')), may hold values from 0.5 to 1.5
- norm_gain2: float32 [2048], P(('dp', 'tensor')), may hold values from 0.5 to 1.5
- att_router: float32 [2048, 4], P(('dp', 'tensor')), may hold values from -0.09375 to 0.09375
- query_maps: float32 [4, 2048, 2048], P(None, 'dp', 'tensor'), may hold values from -0.125 to 0.125
- kv_maps: float32 [2, 2048, 2048], P(None, 'dp', 'tensor'), may hold values from -0.125 to 0.125
- out_maps: float32 [4, 2048, 2048], P(None, 'dp', 'tensor'), may hold values from -0.5 to 0.5
- ffn_router: float32 [2048, 4], P(('dp', 'tensor')), may hold values from -0.09375 to 0.09375
- ffn_maps: float32 [12, 2048, 5632], P(None, 'dp', 'tensor'), may hold values from -0.125 to 0.125
- att_route: int32 [4096, 2], P('dp'), may hold values from 0 to 3, all different within a row; in each aligned block of 512 rows (0 to 511, 512 to 1023, ...) at most 352 rows name the same one
- ffn_route: int32 [4096, 2], P('dp'), may hold values from 0 to 3, all different within a row; in each aligned block of 512 rows (0 to 511, 512 to 1023, ...) at most 352 rows name the same one
- parents: int32 [32], P('dp'), may hold values from 0 to 2, as said below
- cotangent: bfloat16 [4096, 2048], P(('dp', 'tensor')), may hold values from -6 to 6
Outputs:
- mixed: bfloat16 [4096, 2048], P(('dp', 'tensor'))
- input_grad: bfloat16 [4096, 2048], P(('dp', 'tensor'))
- gain1_grad: float32 [2048], P(('dp', 'tensor'))
- gain2_grad: float32 [2048], P(('dp', 'tensor'))
- att_router_grad: float32 [2048, 4], P(('dp', 'tensor'))
- query_grad: float32 [4, 2048, 2048], P(None, 'dp', 'tensor')
- kv_grad: float32 [2, 2048, 2048], P(None, 'dp', 'tensor')
- out_grad: float32 [4, 2048, 2048], P(None, 'dp', 'tensor')
- ffn_router_grad: float32 [2048, 4], P(('dp', 'tensor'))
- ffn_grad: float32 [12, 2048, 5632], P(None, 'dp', 'tensor')
Inputs may be any that keep to these rules, and one draw needn't show every extreme that they name: `parents`: within each tree segment 0 has entry 0; every other segment's parent is an earlier segment of the same tree, and the last segment's parent is the one just before it. `att_route`: each row names two different experts; among the 512 rows of one tree no expert is named by more than 352 rows, a bound that some block reaches. `ffn_route`: each row names two different experts; among the 512 rows of one tree no expert is named by more than 352 rows, a bound that some block reaches.
All inputs are finite; a program needn't handle non-finite values.
Results may differ from a plain program's by a relative error of at most 0.02.
Values may be sent and summed in bfloat16 or wider, within the bound.
No kernel may reach another device: no remote copies, remote signals or barrier semaphores. Data moves between devices by JAX's collectives and lax.ppermute only.
A program may use at most 576 MiB of HBM per device.

v0:
```python
import jax
import jax.numpy as jnp
from jax import lax
from jax.sharding import PartitionSpec as P

HS = 128
TOPK = 2
SEG = 128


epsilon = 1e-05
rope_base = 10000.0
highest = lax.Precision.HIGHEST


def tree_tables(parent_row, segment_size):
    count_seg = parent_row.shape[0]
    group_len = count_seg * segment_size
    segment = jnp.arange(count_seg, dtype=jnp.int32)

    def climb(depth_step, carried):
        reached, current = carried
        current = jnp.where(current > 0, parent_row[current], jnp.zeros_like(current))
        return (reached | (current[:, None] == segment[None, :]), current)

    reached, current = lax.fori_loop(
        0, count_seg, climb, (segment[:, None] == segment[None, :], segment)
    )
    depth_count = jnp.sum(reached.astype(jnp.float32), axis=1) - 1.0
    offsets = jnp.arange(segment_size, dtype=jnp.float32)
    positions = (depth_count[:, None] * segment_size + offsets[None, :]).reshape(-1)
    ancestor = jnp.repeat(jnp.repeat(reached, segment_size, axis=0), segment_size, axis=1)
    token_order = jnp.arange(group_len, dtype=jnp.int32)
    return (positions, ancestor & (token_order[None, :] <= token_order[:, None]))


def rope_tables(positions, head_size):
    half_size = head_size // 2
    frequency = rope_base ** (-2.0 * jnp.arange(half_size, dtype=jnp.float32) / head_size)
    angles = positions[:, None] * frequency[None, :]
    cosines = jnp.cos(angles)
    sines = jnp.sin(angles)
    return (jnp.concatenate([cosines, cosines], axis=-1), jnp.concatenate([sines, sines], axis=-1))


def rotate(vectors, cosines, sines):
    half_size = vectors.shape[-1] // 2
    turned = jnp.concatenate([-vectors[..., half_size:], vectors[..., :half_size]], axis=-1)
    return vectors * cosines + turned * sines


def rms_forward(rows_in, gain_full):
    scale_rows = lax.rsqrt(jnp.mean(rows_in * rows_in, axis=-1, keepdims=True) + epsilon)
    return (rows_in * scale_rows * gain_full, scale_rows)


def rms_backward(rows_in, scale_rows, gain_full, upstream):
    normal_rows = rows_in * scale_rows
    weighted = upstream * gain_full
    rows_grad = scale_rows * (
        weighted - normal_rows * jnp.mean(weighted * normal_rows, axis=-1, keepdims=True)
    )
    return (rows_grad, jnp.sum(upstream * normal_rows, axis=0))


def route_gates(normed_low, router_full, route_rows):
    experts = router_full.shape[1]
    chosen_map = (
        route_rows[:, :, None] == jnp.arange(experts, dtype=jnp.int32)[None, None, :]
    ).astype(jnp.float32)
    logits = jnp.dot(normed_low.astype(jnp.float32), router_full, precision=highest)
    chosen = jnp.einsum("tse,te->ts", chosen_map, logits, precision=highest)
    row_max = jnp.max(chosen, axis=-1, keepdims=True)
    exponent = jnp.exp(chosen - row_max)
    return (exponent / jnp.sum(exponent, axis=-1, keepdims=True), chosen_map)


def gates_backward(gate_probs, chosen_map, normed_low, router_full, upstream):
    inner_grad = gate_probs * (upstream - jnp.sum(gate_probs * upstream, axis=-1, keepdims=True))
    logit_grad = jnp.einsum("ts,tse->te", inner_grad, chosen_map, precision=highest)
    router_grad = jnp.einsum(
        "td,te->de", normed_low.astype(jnp.float32), logit_grad, precision=highest
    )
    normed_grad = jnp.einsum("te,de->td", logit_grad, router_full, precision=highest)
    return (router_grad, normed_grad)


def dispatch_tables(route_rows, experts, capacity):
    flat_route = route_rows.reshape(-1)
    total_slots = flat_route.shape[0]
    onehot = (flat_route[:, None] == jnp.arange(experts, dtype=jnp.int32)[None, :]).astype(
        jnp.int32
    )
    places = jnp.sum((jnp.cumsum(onehot, axis=0) - 1) * onehot, axis=1)
    table = (
        jnp.full((experts, capacity), total_slots, jnp.int32)
        .at[flat_route, places]
        .set(jnp.arange(total_slots, dtype=jnp.int32))
    )
    return (flat_route * capacity + places, table)


def with_blank(rows_in):
    return jnp.concatenate([rows_in, jnp.zeros((1,) + rows_in.shape[1:], rows_in.dtype)], axis=0)


def collect(buffer, slot_where):
    flat_rows = buffer.reshape(-1, buffer.shape[-1])
    return flat_rows[slot_where].reshape(slot_where.shape[0] // 2, 2, buffer.shape[-1])


def attend(query_block, keys_group, values_group, allow_block):
    score_scale = query_block.shape[-1] ** (-0.5)
    scores = (
        jnp.einsum("bshd,khd->shbk", query_block, keys_group, preferred_element_type=jnp.float32)
        * score_scale
    )
    scores = jnp.where(allow_block[None, None], scores, -1e30)
    row_max = jnp.max(scores, axis=-1, keepdims=True)
    exponent = jnp.exp(scores - row_max)
    total_sum = jnp.sum(exponent, axis=-1, keepdims=True)
    probs_low = (exponent / total_sum).astype(jnp.bfloat16)
    attended = jnp.einsum(
        "shbk,khd->bshd", probs_low, values_group, preferred_element_type=jnp.float32
    )
    return (attended.astype(jnp.bfloat16), (row_max + jnp.log(total_sum))[..., 0])


def attend_back(query_block, keys_group, values_group, allow_block, log_total, grad_block):
    score_scale = query_block.shape[-1] ** (-0.5)
    scores = (
        jnp.einsum("bshd,khd->shbk", query_block, keys_group, preferred_element_type=jnp.float32)
        * score_scale
    )
    scores = jnp.where(allow_block[None, None], scores, -1e30)
    probs_full = jnp.exp(scores - log_total[..., None])
    prob_grad = jnp.einsum(
        "bshd,khd->shbk", grad_block, values_group, preferred_element_type=jnp.float32
    )
    score_grad = (
        probs_full * (prob_grad - jnp.sum(probs_full * prob_grad, axis=-1, keepdims=True))
    ).astype(jnp.bfloat16)
    query_grad = (
        jnp.einsum("shbk,khd->bshd", score_grad, keys_group, preferred_element_type=jnp.float32)
        * score_scale
    )
    key_grad = (
        jnp.einsum("shbk,bshd->khd", score_grad, query_block, preferred_element_type=jnp.float32)
        * score_scale
    )
    value_grad = jnp.einsum(
        "shbk,bshd->khd",
        probs_full.astype(jnp.bfloat16),
        grad_block,
        preferred_element_type=jnp.float32,
    )
    return (query_grad, key_grad, value_grad)


def attention_forward(queries, keys_group, values_group, allowed):
    group_len = keys_group.shape[0]
    block_rows = min(512, group_len)
    blocks = group_len // block_rows

    def one_block(pieces):
        query_block, allow_block = pieces
        return attend(query_block, keys_group, values_group, allow_block)

    attended, log_total = lax.map(
        one_block,
        (
            queries.reshape((blocks, block_rows) + queries.shape[1:]),
            allowed.reshape(blocks, block_rows, group_len),
        ),
    )
    return (attended.reshape(queries.shape), log_total)


def attention_backward(queries, keys_group, values_group, allowed, log_total, grad_heads):
    group_len = keys_group.shape[0]
    block_rows = min(512, group_len)
    blocks = group_len // block_rows

    def one_block(carried, pieces):
        query_block, allow_block, total_block, grad_block = pieces
        query_grad, key_grad, value_grad = attend_back(
            query_block, keys_group, values_group, allow_block, total_block, grad_block
        )
        return ((carried[0] + key_grad, carried[1] + value_grad), query_grad)

    zeros_kv = jnp.zeros(keys_group.shape, jnp.float32)
    sums_kv, query_grad = lax.scan(
        one_block,
        (zeros_kv, zeros_kv),
        (
            queries.reshape((blocks, block_rows) + queries.shape[1:]),
            allowed.reshape(blocks, block_rows, group_len),
            log_total,
            grad_heads.reshape((blocks, block_rows) + grad_heads.shape[1:]),
        ),
    )
    return (query_grad.reshape(queries.shape), sums_kv[0], sums_kv[1])


def attention_maps(query_maps, kv_maps, out_maps):
    return (
        lax.all_gather(query_maps.astype(jnp.bfloat16), "dp", axis=1, tiled=True),
        lax.all_gather(kv_maps.astype(jnp.bfloat16), "dp", axis=1, tiled=True),
        lax.all_gather(out_maps.astype(jnp.bfloat16), "dp", axis=1, tiled=True),
    )


def expert_maps(ffn_maps):
    gathered = lax.all_gather(ffn_maps.astype(jnp.bfloat16), "dp", axis=1, tiled=True)
    experts = gathered.shape[0] // 3
    return (gathered[:experts], gathered[experts : 2 * experts], gathered[2 * experts :])


def local(
    tokens,
    norm_gain1,
    norm_gain2,
    att_router,
    query_maps,
    kv_maps,
    out_maps,
    ffn_router,
    ffn_maps,
    att_route,
    ffn_route,
    parents,
    cotangent,
):
    local_rows = tokens.shape[0]
    group_len = att_route.shape[0]
    row_start = lax.axis_index("tensor") * local_rows
    gain_first, gain_second, router_att, router_ffn = (
        lax.all_gather(norm_gain1, ("dp", "tensor"), axis=0, tiled=True),
        lax.all_gather(norm_gain2, ("dp", "tensor"), axis=0, tiled=True),
        lax.all_gather(att_router, ("dp", "tensor"), axis=0, tiled=True),
        lax.all_gather(ffn_router, ("dp", "tensor"), axis=0, tiled=True),
    )
    positions, allowed = tree_tables(parents, SEG)
    cosines, sines = rope_tables(positions, HS)
    cos_four, sin_four = (cosines[:, None, None, :], sines[:, None, None, :])
    cos_three, sin_three = (cosines[:, None, :], sines[:, None, :])
    att_experts = query_maps.shape[0]
    ffn_experts = ffn_maps.shape[0] // 3
    capacity_att = TOPK * group_len // att_experts * 11 // 8
    capacity_ffn = TOPK * group_len // ffn_experts * 11 // 8
    wide_rows = tokens.astype(jnp.float32)
    normed_first, scale_first = rms_forward(wide_rows, gain_first)
    first_low = normed_first.astype(jnp.bfloat16)
    probs_att, chosen_att = route_gates(
        first_low, router_att, lax.dynamic_slice_in_dim(att_route, row_start, local_rows, 0)
    )
    rows_att, gates_att = (
        lax.all_gather(first_low, "tensor", axis=0, tiled=True),
        lax.all_gather(probs_att.astype(jnp.bfloat16), "tensor", axis=0, tiled=True),
    )
    where_att, table_att = dispatch_tables(att_route, att_experts, capacity_att)
    query_w, kv_w, out_w = attention_maps(query_maps, kv_maps, out_maps)
    expert_rows_att = with_blank(rows_att)[table_att // 2]
    query_buf = jnp.einsum(
        "ecd,edf->ecf", expert_rows_att, query_w, preferred_element_type=jnp.float32
    )
    query_raw = collect(query_buf, where_att)
    kv_raw = jnp.einsum("td,jdf->jtf", rows_att, kv_w, preferred_element_type=jnp.float32)
    heads_here = kv_w.shape[2] // HS
    queries = rotate(query_raw.reshape(group_len, TOPK, heads_here, HS), cos_four, sin_four).astype(
        jnp.bfloat16
    )
    keys_group = rotate(kv_raw[0].reshape(group_len, heads_here, HS), cos_three, sin_three).astype(
        jnp.bfloat16
    )
    values_group = kv_raw[1].reshape(group_len, heads_here, HS).astype(jnp.bfloat16)
    attended, log_total = attention_forward(queries, keys_group, values_group, allowed)
    slot_rows = with_blank(attended.reshape(group_len * TOPK, -1))[table_att]
    branch_att = jnp.einsum("ecf,edf->ecd", slot_rows, out_w, preferred_element_type=jnp.float32)
    gates_att_wide = gates_att.astype(jnp.float32)
    partial_att = jnp.sum(gates_att_wide[:, :, None] * collect(branch_att, where_att), axis=1)
    middle = wide_rows + lax.psum_scatter(partial_att, "tensor", scatter_dimension=0, tiled=True)
    normed_second, scale_second = rms_forward(middle, gain_second)
    second_low = normed_second.astype(jnp.bfloat16)
    probs_ffn, chosen_ffn = route_gates(
        second_low, router_ffn, lax.dynamic_slice_in_dim(ffn_route, row_start, local_rows, 0)
    )
    rows_ffn, gates_ffn = (
        lax.all_gather(second_low, "tensor", axis=0, tiled=True),
        lax.all_gather(probs_ffn.astype(jnp.bfloat16), "tensor", axis=0, tiled=True),
    )
    where_ffn, table_ffn = dispatch_tables(ffn_route, ffn_experts, capacity_ffn)
    gate_w, up_w, down_w = expert_maps(ffn_maps)
    expert_rows_ffn = with_blank(rows_ffn)[table_ffn // 2]
    gate_h = jnp.einsum("ecd,edf->ecf", expert_rows_ffn, gate_w, preferred_element_type=jnp.float32)
    up_h = jnp.einsum("ecd,edf->ecf", expert_rows_ffn, up_w, preferred_element_type=jnp.float32)
    sigmoid_h = jax.nn.sigmoid(gate_h)
    silu_h = gate_h * sigmoid_h
    activated = (silu_h * up_h).astype(jnp.bfloat16)
    branch_ffn = jnp.einsum("ecf,edf->ecd", activated, down_w, preferred_element_type=jnp.float32)
    gates_ffn_wide = gates_ffn.astype(jnp.float32)
    partial_ffn = jnp.sum(gates_ffn_wide[:, :, None] * collect(branch_ffn, where_ffn), axis=1)
    mixed = (
        middle
        + lax.psum_scatter(
            partial_ffn.astype(jnp.bfloat16), "tensor", scatter_dimension=0, tiled=True
        ).astype(jnp.float32)
    ).astype(jnp.bfloat16)
    grad_out = cotangent.astype(jnp.float32)
    grad_rows_ffn = lax.all_gather(cotangent, "tensor", axis=0, tiled=True)
    gate_w, up_w, down_w = expert_maps(ffn_maps)
    grad_buf_ffn = with_blank(grad_rows_ffn)[table_ffn // 2].astype(jnp.float32)
    gate_buf_ffn = with_blank(gates_ffn_wide.reshape(-1))[table_ffn]
    grad_branch_ffn = (gate_buf_ffn[..., None] * grad_buf_ffn).astype(jnp.bfloat16)
    gate_part_ffn = collect(jnp.sum(grad_buf_ffn * branch_ffn, axis=-1)[..., None], where_ffn)[
        ..., 0
    ]
    act_grad = jnp.einsum(
        "ecd,edf->ecf", grad_branch_ffn, down_w, preferred_element_type=jnp.float32
    )
    gate_grad = (act_grad * up_h * sigmoid_h * (1.0 + gate_h * (1.0 - sigmoid_h))).astype(
        jnp.bfloat16
    )
    up_grad = (act_grad * silu_h).astype(jnp.bfloat16)
    expert_grad = jnp.concatenate(
        [
            jnp.einsum(
                "ecd,ecf->edf", expert_rows_ffn, gate_grad, preferred_element_type=jnp.float32
            ),
            jnp.einsum(
                "ecd,ecf->edf", expert_rows_ffn, up_grad, preferred_element_type=jnp.float32
            ),
            jnp.einsum(
                "ecd,ecf->edf", grad_branch_ffn, activated, preferred_element_type=jnp.float32
            ),
        ],
        axis=0,
    )
    back_ffn = jnp.einsum(
        "ecf,edf->ecd", gate_grad, gate_w, preferred_element_type=jnp.float32
    ) + jnp.einsum("ecf,edf->ecd", up_grad, up_w, preferred_element_type=jnp.float32)
    part_ffn = jnp.sum(collect(back_ffn, where_ffn), axis=1)
    second_grad, gate_grad_ffn = (
        lax.psum_scatter(part_ffn, "tensor", scatter_dimension=0, tiled=True),
        lax.psum_scatter(gate_part_ffn, "tensor", scatter_dimension=0, tiled=True),
    )
    router_ffn_grad, extra_ffn = gates_backward(
        probs_ffn, chosen_ffn, second_low, router_ffn, gate_grad_ffn
    )
    middle_norm_grad, gain_second_grad = rms_backward(
        middle, scale_second, gain_second, second_grad + extra_ffn
    )
    middle_grad = grad_out + middle_norm_grad
    ffn_grad = lax.psum_scatter(
        expert_grad.astype(jnp.bfloat16), "dp", scatter_dimension=1, tiled=True
    ).astype(jnp.float32)
    grad_rows_att = lax.all_gather(middle_grad.astype(jnp.bfloat16), "tensor", axis=0, tiled=True)
    query_w, kv_w, out_w = attention_maps(query_maps, kv_maps, out_maps)
    grad_buf_att = with_blank(grad_rows_att)[table_att // 2].astype(jnp.float32)
    gate_buf_att = with_blank(gates_att_wide.reshape(-1))[table_att]
    grad_branch_att = (gate_buf_att[..., None] * grad_buf_att).astype(jnp.bfloat16)
    gate_part_att = collect(jnp.sum(grad_buf_att * branch_att, axis=-1)[..., None], where_att)[
        ..., 0
    ]
    grad_slot = jnp.einsum(
        "ecd,edf->ecf", grad_branch_att, out_w, preferred_element_type=jnp.float32
    ).astype(jnp.bfloat16)
    out_grad_full = jnp.einsum(
        "ecd,ecf->edf", grad_branch_att, slot_rows, preferred_element_type=jnp.float32
    )
    grad_heads = collect(grad_slot, where_att).reshape(group_len, TOPK, heads_here, HS)
    query_grad_raw, key_grad_raw, value_grad_raw = attention_backward(
        queries, keys_group, values_group, allowed, log_total, grad_heads
    )
    query_rows_grad = (
        rotate(query_grad_raw, cos_four, -sin_four)
        .reshape(group_len * TOPK, -1)
        .astype(jnp.bfloat16)
    )
    key_rows_grad = (
        rotate(key_grad_raw, cos_three, -sin_three).reshape(group_len, -1).astype(jnp.bfloat16)
    )
    value_rows_grad = value_grad_raw.reshape(group_len, -1).astype(jnp.bfloat16)
    query_slot_grad = with_blank(query_rows_grad)[table_att]
    query_grad_full = jnp.einsum(
        "ecd,ecf->edf", expert_rows_att, query_slot_grad, preferred_element_type=jnp.float32
    )
    back_query = jnp.sum(
        collect(
            jnp.einsum(
                "ecf,edf->ecd", query_slot_grad, query_w, preferred_element_type=jnp.float32
            ),
            where_att,
        ),
        axis=1,
    )
    kv_rows_grad = jnp.stack([key_rows_grad, value_rows_grad])
    kv_grad_full = jnp.einsum(
        "td,jtf->jdf", rows_att, kv_rows_grad, preferred_element_type=jnp.float32
    )
    back_kv = jnp.einsum("jtf,jdf->td", kv_rows_grad, kv_w, preferred_element_type=jnp.float32)
    first_grad, gate_grad_att = (
        lax.psum_scatter(
            (back_query + back_kv).astype(jnp.bfloat16), "tensor", scatter_dimension=0, tiled=True
        ).astype(jnp.float32),
        lax.psum_scatter(
            gate_part_att.astype(jnp.bfloat16), "tensor", scatter_dimension=0, tiled=True
        ).astype(jnp.float32),
    )
    router_att_grad, extra_att = gates_backward(
        probs_att, chosen_att, first_low, router_att, gate_grad_att
    )
    wide_norm_grad, gain_first_grad = rms_backward(
        wide_rows, scale_first, gain_first, first_grad + extra_att
    )
    input_grad = (middle_grad + wide_norm_grad).astype(jnp.bfloat16)
    query_grad, kv_grad, out_grad = (
        lax.psum_scatter(
            query_grad_full.astype(jnp.bfloat16), "dp", scatter_dimension=1, tiled=True
        ).astype(jnp.float32),
        lax.psum_scatter(
            kv_grad_full.astype(jnp.bfloat16), "dp", scatter_dimension=1, tiled=True
        ).astype(jnp.float32),
        lax.psum_scatter(
            out_grad_full.astype(jnp.bfloat16), "dp", scatter_dimension=1, tiled=True
        ).astype(jnp.float32),
    )
    gain1_grad, gain2_grad, att_router_grad, ffn_router_grad = (
        lax.psum_scatter(gain_first_grad, ("dp", "tensor"), scatter_dimension=0, tiled=True),
        lax.psum_scatter(gain_second_grad, ("dp", "tensor"), scatter_dimension=0, tiled=True),
        lax.psum_scatter(router_att_grad, ("dp", "tensor"), scatter_dimension=0, tiled=True),
        lax.psum_scatter(router_ffn_grad, ("dp", "tensor"), scatter_dimension=0, tiled=True),
    )
    return (
        mixed,
        input_grad,
        gain1_grad,
        gain2_grad,
        att_router_grad,
        query_grad,
        kv_grad,
        out_grad,
        ffn_router_grad,
        ffn_grad,
    )


def solution(mesh):
    placed = (
        P(("dp", "tensor"), None),
        P(("dp", "tensor")),
        P(("dp", "tensor")),
        P(("dp", "tensor"), None),
        P(None, "dp", "tensor"),
        P(None, "dp", "tensor"),
        P(None, "dp", "tensor"),
        P(("dp", "tensor"), None),
        P(None, "dp", "tensor"),
        P("dp", None),
        P("dp", None),
        P("dp"),
        P(("dp", "tensor"), None),
    )
    return jax.shard_map(
        local,
        mesh=mesh,
        in_specs=placed,
        out_specs=(
            P(("dp", "tensor"), None),
            P(("dp", "tensor"), None),
            P(("dp", "tensor")),
            P(("dp", "tensor")),
            P(("dp", "tensor"), None),
            P(None, "dp", "tensor"),
            P(None, "dp", "tensor"),
            P(None, "dp", "tensor"),
            P(("dp", "tensor"), None),
            P(None, "dp", "tensor"),
        ),
        check_vma=False,
    )
```

profile of v0, /device:TPU:0, one launch (start us, length us, event | category | flops | bytes accessed | tf_op | source)
XLA Modules:
  0.0 3970.6 jit_solution(15597208861068143022)
XLA Ops:
  10.4 42.1 %all-reduce.11 = (f32[2048]{0:T(1024)S(1)}, f32[2048]{0:T(1024)S(1)}) all-reduce(f32[2048]{0:T(1024)S(1)} %dynamic-update-slice, f32[2048]{0:T(1024)S(1)} %dynamic-update-slice.1), channel_id=1, replica_groups=mesh['dp'=8,'tensor'=4] {'dp','tensor'}, use_global_device_ids=true, to_apply=%add.6 | all-reduce | flops 4096 | bytes 32768
  74.5 41.0 %all-gather = f32[32,64,4]{1,2,0:T(4,128)S(1)} all-gather(f32[1,64,4]{1,2,0:T(4,128)S(1)} %bitcast.273), channel_id=1, replica_groups=mesh['dp'=8,'tensor'=4] {'dp','tensor'}, dimensions={0}, use_global_device_ids=true | all-gather | bytes 33792 | tf_op jit(solution)/shard_map/all_gather | solution.py:240
  134.6 20.3 all-gather.13.cloned.1.call-done
  161.5 119.3 %all-gather.15.cloned.1.call-done = bf16[4,2048,512]{2,1,0:T(8,128)(2,1)} async-done(((bf16[4,256,512]{2,1,0:T(8,128)(2,1)}), bf16[4,2048,512]{2,1,0:T(8,128)(2,1)}) %all-gather.15.cloned.1.call-update) | async-done | bytes 8388624 | tf_op jit(solution)/shard_map/all_gather | solution.py:207
  312.6 94.0 %all-gather.17.cloned.1.call-done = bf16[4,2048,512]{2,1,0:T(8,128)(2,1)} async-done(((bf16[4,256,512]{2,1,0:T(8,128)(2,1)}), bf16[4,2048,512]{2,1,0:T(8,128)(2,1)}) %all-gather.17.cloned.1.call-update) | async-done | bytes 8388624 | tf_op jit(solution)/shard_map/all_gather | solution.py:209
  418.2 13.2 gather_fusion.4
  442.2 15.5 multiply_reduce_fusion.1
  458.3 42.2 %reduce-scatter.17.cloned.1.call-done = f32[128,2048]{1,0:T(8,128)} async-done(((f32[512,2048]{1,0:T(8,128)}), f32[128,2048]{1,0:T(8,128)}) %reduce-scatter.17.cloned.1.call-update) | async-done | bytes 1048592 | tf_op jit(solution)/shard_map/reduce_scatter | solution.py:282
  518.2 41.0 %all-gather.1 = f32[32,64,4]{1,2,0:T(4,128)S(1)} all-gather(f32[1,64,4]{1,2,0:T(4,128)S(1)} %bitcast.274), channel_id=1, replica_groups=mesh['dp'=8,'tensor'=4] {'dp','tensor'}, dimensions={0}, use_global_device_ids=true | all-gather | bytes 33792 | tf_op jit(solution)/shard_map/all_gather | solution.py:241
  593.2 1264.5 %all-gather.21.cloned.1.call-done = bf16[12,2048,1408]{2,1,0:T(8,128)(2,1)} async-done(((bf16[12,256,1408]{2,1,0:T(8,128)(2,1)}), bf16[12,2048,1408]{2,1,0:T(8,128)(2,1)}) %all-gather.21.cloned.1.call-update) | async-done | bytes 69206032 | tf_op jit(solution)/shard_map/all_gather | solution.py:214
  1857.7 17.5 fusion.9
  1875.2 16.4 fusion.3
  1891.6 23.6 multiply_convert_fusion.1
  1915.2 18.7 fusion.16
  1941.1 16.7 fusion.7
  1957.8 19.5 fusion.30
  1977.3 13.3 gather_fusion.9
  2017.5 41.6 %reduce-scatter.21.cloned.1.call-done = f32[128,2048]{1,0:T(8,128)} async-done(((f32[512,2048]{1,0:T(8,128)}), f32[128,2048]{1,0:T(8,128)}) %reduce-scatter.21.cloned.1.call-update) | async-done | bytes 1048592 | tf_op jit(solution)/shard_map/reduce_scatter | solution.py:344
  2072.5 14.6 all-gather.25.cloned.1.call-done
  2162.4 13.3 gather_fusion.15
  2190.6 13.3 reduce_sum.212
  2239.3 15.0 multiply_reduce_fusion
  2283.3 20.5 convolution_convert_fusion.1
  2303.8 20.4 convolution_convert_fusion.2
  2324.2 20.6 convolution_convert_fusion
  2344.8 47.6 %pad_maximum_fusion = bf16[12,2048,1408]{2,1,0:T(8,128)(2,1)} fusion(bf16[4,2048,1408]{2,1,0:T(8,128)(2,1)} %convolution_convert_fusion, bf16[4,2048,1408]{2,1,0:T(8,128)(2,1)} %convolution_convert_fusion.1, bf16[4,2048,1408]{2,1,0:T(8,128)(2,1)} %convolution_convert_fusion.2), kind=kLoop, calls=%fused_computation.25 | loop fusion | flops 69206016 | bytes 138412032 | tf_op jit(solution)/shard_map/concatenate | solution.py:325
  2401.7 28.9 reduce-scatter.25.cloned.1.call-done
  2433.9 39.4 all-reduce.10
  2477.4 79.9 %reduce-scatter.31.cloned.1.call-done = bf16[2,256,512]{1,2,0:T(8,128)(2,1)} async-done(((bf16[2,2048,512]{1,2,0:T(8,128)(2,1)}), bf16[2,256,512]{1,2,0:T(8,128)(2,1)}) %reduce-scatter.31.cloned.1.call-update) | async-done | bytes 524304 | tf_op jit(solution)/shard_map/reduce_scatter | solution.py:421
  2559.5 151.5 %reduce-scatter.29.cloned.1.call-done = bf16[4,256,512]{2,1,0:T(8,128)(2,1)} async-done(((bf16[4,2048,512]{2,1,0:T(8,128)(2,1)}), bf16[4,256,512]{2,1,0:T(8,128)(2,1)}) %reduce-scatter.29.cloned.1.call-update) | async-done | bytes 1048592 | tf_op jit(solution)/shard_map/reduce_scatter | solution.py:418
  2713.8 149.3 %reduce-scatter.33.cloned.1.call-done = bf16[4,256,512]{2,1,0:T(8,128)(2,1)} async-done(((bf16[4,2048,512]{2,1,0:T(8,128)(2,1)}), bf16[4,256,512]{2,1,0:T(8,128)(2,1)}) %reduce-scatter.33.cloned.1.call-update) | async-done | bytes 1048592 | tf_op jit(solution)/shard_map/reduce_scatter | solution.py:424
  2865.9 1085.9 %reduce-scatter.35.cloned.1.call-done = bf16[12,256,1408]{2,1,0:T(8,128)(2,1)} async-done(((bf16[12,2048,1408]{2,1,0:T(8,128)(2,1)}), bf16[12,256,1408]{2,1,0:T(8,128)(2,1)}) %reduce-scatter.35.cloned.1.call-update) | async-done | bytes 8650768 | tf_op jit(solution)/shard_map/reduce_scatter | solution.py:354
  (451 shorter events, 396.4 us)
Async XLA Ops:
  7.2 118.2 %all-gather.11.cloned.1.call-start = ((), (), s32[]{:S(2)}) async-start(), calls=%async_computation.12 | async-start | bytes 2621440 | tf_op jit(solution)/shard_map/all_gather | solution.py:258
  52.5 449.5 %copy-start.48 = (f32[2048]{0:T(1024)}, f32[2048]{0:T(1024)S(1)}, u32[]{:S(2)}) copy-start(f32[2048]{0:T(1024)S(1)} %get-tuple-element.148) | copy-start | bytes 24580
  54.6 100.3 %all-gather.13.cloned.1.call-start = ((), (), s32[]{:S(2)}) async-start(), calls=%async_computation.13 | async-start | bytes 4718592 | tf_op jit(solution)/shard_map/all_gather | solution.py:208
  56.9 223.9 %all-gather.15.cloned.1.call-start = ((), (), s32[]{:S(2)}) async-start(), calls=%async_computation.14 | async-start | bytes 9437184 | tf_op jit(solution)/shard_map/all_gather | solution.py:207
  59.7 346.9 %all-gather.17.cloned.1.call-start = ((), (), s32[]{:S(2)}) async-start(), calls=%async_computation.15 | async-start | bytes 9437184 | tf_op jit(solution)/shard_map/all_gather | solution.py:209
  60.8 439.7 %reduce-scatter.17.cloned.1.call-start = ((), (), s32[]{:S(2)}) async-start(), calls=%async_computation.16 | async-start | bytes 5242880 | tf_op jit(solution)/shard_map/reduce_scatter | solution.py:282
  123.7 183.7 %copy-start.53 = (s32[2048]{0:T(1024)}, s32[2048]{0:T(1024)S(1)}, u32[]{:S(2)}) copy-start(s32[2048]{0:T(1024)S(1)} %pad_clamp_fusion.3) | copy-start | bytes 24580
  125.3 292.9 %copy-start.43 = (s32[1024]{0:T(1024)}, s32[1024]{0:T(1024)S(1)}, u32[]{:S(2)}) copy-start(s32[1024]{0:T(1024)S(1)} %broadcast_clamp_fusion.1) | copy-start | bytes 12292
  161.5 137.3 %copy-start.17 = (bf16[512,4,128,1]{0,2,3,1:T(8,128)(2,1)}, bf16[512,4,128,1]{0,2,3,1:T(8,128)(2,1)S(1)}, u32[]{:S(2)}) copy-start(bf16[512,4,128,1]{0,2,3,1:T(8,128)(2,1)S(1)} %fusion.76) | copy-start | bytes 1572868
  312.6 105.7 %copy-start.9 = (bf16[1408,512]{1,0:T(8,128)(2,1)}, bf16[1408,512]{1,0:T(8,128)(2,1)S(1)}, u32[]{:S(2)}) copy-start(bf16[1408,512]{1,0:T(8,128)(2,1)S(1)} %gather_fusion.3) | copy-start | bytes 4325380
  457.7 101.8 %all-gather.23.cloned.1.call-start = ((), (), s32[]{:S(2)}) async-start(), calls=%async_computation.20 | async-start | bytes 2621440 | tf_op jit(solution)/shard_map/all_gather | solution.py:310
  458.3 126.2 %all-gather.19.cloned.1.call-start = ((), (), s32[]{:S(2)}) async-start(), calls=%async_computation.17 | async-start | bytes 2621440 | tf_op jit(solution)/shard_map/all_gather | solution.py:289
  504.0 1353.8 %all-gather.21.cloned.1.call-start = ((), (), s32[]{:S(2)}) async-start(), calls=%async_computation.18 | async-start | bytes 77856768 | tf_op jit(solution)/shard_map/all_gather | solution.py:214
  513.6 1501.1 %reduce-scatter.23.cloned.1.call-start = ((), (), s32[]{:S(2)}) async-start(), calls=%async_computation.22 | async-start | bytes 327680 | tf_op jit(solution)/shard_map/reduce_scatter | solution.py:345
  559.5 1417.8 %copy-start.64 = (s32[1024]{0:T(1024)}, s32[1024]{0:T(1024)S(1)}, u32[]{:S(2)}) copy-start(s32[1024]{0:T(1024)S(1)} %broadcast_clamp_fusion) | copy-start | bytes 12292
  584.5 1290.7 %copy-start.84 = (f32[4,352]{1,0:T(4,128)}, f32[4,352]{1,0:T(4,128)S(1)}, u32[]{:S(2)}) copy-start(f32[4,352]{1,0:T(4,128)S(1)} %reshape.505) | copy-start | bytes 16900
  1941.1 118.0 %reduce-scatter.21.cloned.1.call-start = ((), (), s32[]{:S(2)}) async-start(), calls=%async_computation.21 | async-start | bytes 5242880 | tf_op jit(solution)/shard_map/reduce_scatter | solution.py:344
  2014.5 72.6 %all-gather.25.cloned.1.call-start = ((), (), s32[]{:S(2)}) async-start(), calls=%async_computation.23 | async-start | bytes 2621440 | tf_op jit(solution)/shard_map/all_gather | solution.py:357
  2064.3 139.6 %reduce-scatter.27.cloned.1.call-start = ((), (), s32[]{:S(2)}) async-start(), calls=%async_computation.25 | async-start | bytes 163840 | tf_op jit(solution)/shard_map/reduce_scatter | solution.py:406
  2110.7 281.9 %reduce-scatter.39.cloned.1.call-start = ((), (), s32[]{:S(2)}) async-start(), calls=%async_computation.31 | async-start | bytes 1081344
  2112.4 287.9 %reduce-scatter.37.cloned.1.call-start = ((), (), s32[]{:S(2)}) async-start(), calls=%async_computation.30 | async-start | bytes 1081344
  2208.2 222.5 %reduce-scatter.25.cloned.1.call-start = ((), (), s32[]{:S(2)}) async-start(), calls=%async_computation.24 | async-start | bytes 2621440 | tf_op jit(solution)/shard_map/reduce_scatter | solution.py:403
  2215.4 259.1 %reduce-scatter.19.cloned.1.call-start = ((), (), s32[]{:S(2)}) async-start(), calls=%async_computation.19 | async-start | bytes 2621440 | tf_op jit(solution)/shard_map/reduce_scatter | solution.py:305
  2254.4 302.9 %reduce-scatter.31.cloned.1.call-start = ((), (), s32[]{:S(2)}) async-start(), calls=%async_computation.27 | async-start | bytes 4718592 | tf_op jit(solution)/shard_map/reduce_scatter | solution.py:421
  2260.5 450.5 %reduce-scatter.29.cloned.1.call-start = ((), (), s32[]{:S(2)}) async-start(), calls=%async_computation.26 | async-start | bytes 9437184 | tf_op jit(solution)/shard_map/reduce_scatter | solution.py:418
  2271.0 592.1 %reduce-scatter.33.cloned.1.call-start = ((), (), s32[]{:S(2)}) async-start(), calls=%async_computation.28 | async-start | bytes 9437184 | tf_op jit(solution)/shard_map/reduce_scatter | solution.py:424
  2283.3 1668.6 %reduce-scatter.35.cloned.1.call-start = ((), (), s32[]{:S(2)}) async-start(), calls=%async_computation.29 | async-start | bytes 77856768 | tf_op jit(solution)/shard_map/reduce_scatter | solution.py:354
  2392.4 82.1 %copy-start.4 = (f32[128,2048]{1,0:T(8,128)S(1)}, f32[128,2048]{1,0:T(8,128)}, u32[]{:S(2)}) copy-start(f32[128,2048]{1,0:T(8,128)} %copy-done.2) | copy-start | bytes 3145732
  2392.4 82.1 %copy-start.8 = (f32[128,2048]{1,0:T(8,128)S(1)}, f32[128,2048]{1,0:T(8,128)}, u32[]{:S(2)}) copy-start(f32[128,2048]{1,0:T(8,128)} %copy-done.7) | copy-start | bytes 3145732
  2392.4 82.1 %copy-start.20 = (bf16[128,2048]{1,0:T(8,128)(2,1)S(1)}, bf16[128,2048]{1,0:T(8,128)(2,1)}, u32[]{:S(2)}) copy-start(bf16[128,2048]{1,0:T(8,128)(2,1)} %param.27) | copy-start | bytes 1572868
  2392.5 82.1 %copy-start.50 = (f32[2048]{0:T(1024)S(1)}, f32[2048]{0:T(1024)}, u32[]{:S(2)}) copy-start(f32[2048]{0:T(1024)} %copy-done.48) | copy-start | bytes 24580
  2392.5 82.1 %copy-start.81 = (f32[128]{0:T(128)S(1)}, f32[128]{0:T(128)}, u32[]{:S(2)}) copy-start(f32[128]{0:T(128)} %copy-done.79) | copy-start | bytes 1540
  (86 other events, 1542.2 us)
Sparse Core Ops, SparseCore 0:
  54.7 22.4 all-gather.10
  79.7 75.0 all-gather.12
  157.7 123.0 all-gather.14
  283.4 123.0 all-gather.16
  457.8 42.6 reduce-scatter.16
  502.0 22.6 all-gather.22
  526.9 22.8 all-gather.18
  551.4 1306.2 all-gather.20
  1941.2 19.9 reduce-scatter.22
  2014.6 44.4 reduce-scatter.20
  2064.5 22.5 all-gather.24
  2110.8 19.5 reduce-scatter.26
  2132.6 134.7 reduce-scatter.38
  2269.6 130.6 reduce-scatter.36
  2403.3 27.3 reduce-scatter.24
  2433.7 31.5 reduce-scatter.18
  2468.8 88.4 reduce-scatter.30
  2561.8 149.1 reduce-scatter.28
  2714.6 148.4 reduce-scatter.32
  2867.3 1084.4 reduce-scatter.34
where the time goes:
time: 3980 us; the launch traced here: 3970 us
  waiting for transfers between devices  3100 us (78%)
  matrix products  284 us (7%)
  local copies, waits for them, and re-layouts  225 us (6%)
  blocking collectives  174 us (4%)
  other arithmetic  171 us (4%)
    all_gather x1, waiting for transfers between devices, expert_maps(): lax.all_gather(ffn_maps.astype(jnp.bfloat16), 'dp', axis=1, tiled=True)  1260 us
    reduce_scatter x1, waiting for transfers between devices, local(): lax.psum_scatter(expert_grad.astype(jnp.bfloat16), 'dp', scatter_dimensio...  1090 us
    reduce_scatter x1, waiting for transfers between devices, local(): lax.psum_scatter(query_grad_full.astype(jnp.bfloat16), 'dp', scatter_dime...  152 us
    reduce_scatter x1, waiting for transfers between devices, local(): lax.psum_scatter(out_grad_full.astype(jnp.bfloat16), 'dp', scatter_dimens...  149 us
    all_gather x1, waiting for transfers between devices, attention_maps(): lax.all_gather(query_maps.astype(jnp.bfloat16), 'dp', axis=1, tiled=True)  119 us
    all_gather x1, waiting for transfers between devices, attention_maps(): lax.all_gather(out_maps.astype(jnp.bfloat16), 'dp', axis=1, tiled=True)  94 us
    unnamed x2, blocking collectives  81.6 us
    reduce_scatter x1, waiting for transfers between devices, local(): lax.psum_scatter(kv_grad_full.astype(jnp.bfloat16), 'dp', scatter_dimensi...  79.9 us
  transfers between devices with their start and end apart: 20, of which 13 were waited for; matrix products, arithmetic and copies ran while one was open for 12% of the time, Pallas kernels for 0%

commit v1 on v0

v1 whole, which is shorter than its diff:
```python
import functools

import jax
import jax.numpy as jnp
from jax import lax
from jax.experimental import pallas as pl
from jax.experimental.pallas import tpu as pltpu
from jax.sharding import Mesh, PartitionSpec as P

EXPERTS = 4
HS = 128
SEG = 128
SIDE = 128
epsilon = 1e-05
rope_base = 10000.0
f32 = jnp.float32
bf16 = jnp.bfloat16
ALL = ("zz", "xx", "tensor")
GROUP = ("zz", "tensor")
VMEM = 60 * 1024 * 1024


def dot(a, b):
    return lax.dot_general(a, b, (((1,), (0,)), ((), ())), preferred_element_type=f32)


def dot_nt(a, b):
    return lax.dot_general(a, b, (((1,), (1,)), ((), ())), preferred_element_type=f32)


def dot_tn(a, b):
    return lax.dot_general(a, b, (((0,), (0,)), ((), ())), preferred_element_type=f32)


def lanes(rows):
    return lax.broadcasted_iota(jnp.int32, (rows, SIDE), 1).astype(f32)


def put(columns, rows):
    lane = lanes(rows)
    out = jnp.zeros((rows, SIDE), f32)
    for place, column in columns.items():
        out = jnp.where(lane == place, column, out)
    return out


def norm_scale(rows):
    return lax.rsqrt(jnp.mean(rows * rows, axis=-1, keepdims=True) + epsilon)


def gate_probs(low, router_parts, route0, route1):
    rows = low.shape[0]
    parts = dot(low, router_parts)
    lane = lanes(rows)
    logits = (
        parts
        + pltpu.roll(parts, SIDE - EXPERTS, 1)
        + pltpu.roll(parts, SIDE - 2 * EXPERTS, 1)
    )
    c0 = jnp.sum(jnp.where(lane == route0, logits, 0.0), axis=1, keepdims=True)
    c1 = jnp.sum(jnp.where(lane == route1, logits, 0.0), axis=1, keepdims=True)
    top = jnp.maximum(c0, c1)
    e0 = jnp.exp(c0 - top)
    e1 = jnp.exp(c1 - top)
    total = e0 + e1
    return put({0: e0 / total, 1: e1 / total}, rows)


def choose(wide, route):
    out = wide[:, :HS]
    for e in range(1, EXPERTS):
        out = jnp.where(route == e, wide[:, e * HS : (e + 1) * HS], out)
    return out


def spread(slots, routes):
    blocks = []
    for e in range(EXPERTS):
        block = jnp.where(routes[0] == e, slots[0], 0.0)
        blocks.append(block + jnp.where(routes[1] == e, slots[1], 0.0))
    return blocks


def rope_rows(depth, table_ref):
    segments = table_ref.shape[0] // SEG
    out = table_ref[0:SEG, :]
    for d in range(1, segments):
        out = jnp.where(depth == d, table_ref[d * SEG : (d + 1) * SEG, :], out)
    return out


def allow_mask(side, seg):
    rows = side[seg * SEG : (seg + 1) * SEG]
    blocks = [jnp.broadcast_to(rows[:, 2 + b : 3 + b], (SEG, SEG)) for b in range(seg)]
    later = lax.broadcasted_iota(jnp.int32, (SEG, SEG), 1)
    here = lax.broadcasted_iota(jnp.int32, (SEG, SEG), 0)
    blocks.append((later <= here).astype(f32))
    mask = jnp.concatenate(blocks, axis=1) if seg else blocks[0]
    return jnp.concatenate([mask, mask], axis=0)


def weights_of(queries, keys, mask):
    scores = dot_nt(queries, keys) * (HS**-0.5)
    scores = jnp.where(mask > 0.5, scores, -1e30)
    top = jnp.max(scores, axis=-1, keepdims=True)
    exponent = jnp.exp(scores - top)
    return exponent / jnp.sum(exponent, axis=-1, keepdims=True)


def pack_kernel(where_ref, parents_ref, tok_ref, att_ref, ffn_ref, out_ref):
    rows = tok_ref.shape[0]
    dim = tok_ref.shape[1]
    out_ref[:, :dim] = tok_ref[...]
    segments = parents_ref.shape[0]
    current = where_ref[0]
    reached = [current == b for b in range(segments)]
    for step in range(segments - 1):
        parent = parents_ref[jnp.maximum(current, 0)]
        current = jnp.where(current > 0, parent, 0)
        reached = [r | (current == b) for b, r in enumerate(reached)]
    flags = [jnp.where(r, 1.0, 0.0) for r in reached]
    depth = functools.reduce(lambda a, b: a + b, flags) - 1.0
    att = att_ref[...].astype(f32)
    ffn = ffn_ref[...].astype(f32)
    columns = {0: att[:, 0:1], 1: att[:, 1:2], 6: depth, 7: ffn[:, 0:1], 8: ffn[:, 1:2]}
    for b in range(segments):
        columns[2 + b] = flags[b]
    out_ref[:, dim:] = put(columns, rows).astype(bf16)


def att_fwd_kernel(
    tok_ref, w_ref, router_ref, gain_ref, cos_ref, sin_ref, part_ref, x_ref, keep_ref, gate_ref
):
    dim = x_ref.shape[1]
    rows = x_ref.shape[0]
    side = tok_ref[:, dim:].astype(f32)
    wide = tok_ref[:, :dim].astype(f32)
    x = (wide * norm_scale(wide) * gain_ref[...]).astype(bf16)
    x_ref[...] = x
    qkv_width = (EXPERTS + 2) * HS
    qkv = dot(x, w_ref[:, :qkv_width])
    routes = (side[:, 0:1], side[:, 1:2])
    probs = gate_probs(x, router_ref[...], routes[0], routes[1])
    gate_ref[...] = probs
    gates = probs.astype(bf16).astype(f32)
    segments = rows // SEG
    cos, sin = [], []
    for a in range(segments):
        depth = side[a * SEG : (a + 1) * SEG, 6:7]
        cos.append(rope_rows(depth, cos_ref))
        sin.append(rope_rows(depth, sin_ref))
    cos = jnp.concatenate(cos, axis=0)
    sin = jnp.concatenate(sin, axis=0)

    def turn(v):
        return (v * cos + pltpu.roll(v, HS // 2, 1) * sin).astype(bf16)

    q = [turn(choose(qkv, r)) for r in routes]
    k = turn(qkv[:, EXPERTS * HS : (EXPERTS + 1) * HS])
    v = qkv[:, (EXPERTS + 1) * HS :].astype(bf16)
    heads = [[], []]
    for a in range(segments):
        here = slice(a * SEG, (a + 1) * SEG)
        upto = (a + 1) * SEG
        qa = jnp.concatenate([q[0][here], q[1][here]], axis=0)
        p = weights_of(qa, k[:upto], allow_mask(side, a))
        o = dot(p.astype(bf16), v[:upto]).astype(bf16)
        heads[0].append(o[:SEG])
        heads[1].append(o[SEG:])
    heads = [jnp.concatenate(h, axis=0) for h in heads]
    for i, piece in enumerate([q[0], q[1], k, v, heads[0], heads[1]]):
        keep_ref[:, i * HS : (i + 1) * HS] = piece
    gated = [gates[:, s : s + 1] * heads[s].astype(f32) for s in range(2)]
    z = jnp.concatenate([b.astype(bf16) for b in spread(gated, routes)], axis=1)
    part_ref[...] = dot_nt(z, w_ref[:, qkv_width:]).astype(bf16)


def att_bwd_kernel(
    c_ref, w_ref, keep_ref, gate_ref, side_ref, cos_ref, sin_ref, back_ref, grad_ref, z_ref
):
    dim = c_ref.shape[1]
    rows = c_ref.shape[0]
    qkv_width = (EXPERTS + 2) * HS
    side = side_ref[...].astype(f32)
    routes = (side[:, 0:1], side[:, 1:2])
    gates = gate_ref[...].astype(bf16).astype(f32)
    g = dot(c_ref[...], w_ref[:, qkv_width:])
    q = [keep_ref[:, :HS], keep_ref[:, HS : 2 * HS]]
    k = keep_ref[:, 2 * HS : 3 * HS]
    v = keep_ref[:, 3 * HS : 4 * HS]
    heads = [keep_ref[:, 4 * HS : 5 * HS].astype(f32), keep_ref[:, 5 * HS :].astype(f32)]
    chosen = [choose(g, r) for r in routes]
    parts = [jnp.sum(heads[s] * chosen[s], axis=1, keepdims=True) for s in range(2)]
    hg = [(gates[:, s : s + 1] * chosen[s]).astype(bf16) for s in range(2)]
    gated = [gates[:, s : s + 1] * heads[s] for s in range(2)]
    for e, block in enumerate(spread(gated, routes)):
        z_ref[:, e * HS : (e + 1) * HS] = block.astype(bf16)
    segments = rows // SEG
    dk = [jnp.zeros((SEG, HS), f32) for _ in range(segments)]
    dv = [jnp.zeros((SEG, HS), f32) for _ in range(segments)]
    dq = [[], []]
    for a in range(segments):
        here = slice(a * SEG, (a + 1) * SEG)
        upto = (a + 1) * SEG
        qa = jnp.concatenate([q[0][here], q[1][here]], axis=0)
        ha = jnp.concatenate([hg[0][here], hg[1][here]], axis=0)
        p = weights_of(qa, k[:upto], allow_mask(side, a))
        pg = dot_nt(ha, v[:upto])
        sg = (p * (pg - jnp.sum(p * pg, axis=-1, keepdims=True))).astype(bf16)
        dqa = dot(sg, k[:upto]) * (HS**-0.5)
        dq[0].append(dqa[:SEG])
        dq[1].append(dqa[SEG:])
        dka = dot_tn(sg, qa) * (HS**-0.5)
        dva = dot_tn(p.astype(bf16), ha)
        for b in range(a + 1):
            dk[b] = dk[b] + dka[b * SEG : (b + 1) * SEG]
            dv[b] = dv[b] + dva[b * SEG : (b + 1) * SEG]
    cos, sin = [], []
    for a in range(segments):
        depth = side[a * SEG : (a + 1) * SEG, 6:7]
        cos.append(rope_rows(depth, cos_ref))
        sin.append(rope_rows(depth, sin_ref))
    cos = jnp.concatenate(cos, axis=0)
    sin = jnp.concatenate(sin, axis=0)

    def unturn(v):
        return v * cos - pltpu.roll(v, HS // 2, 1) * sin

    dq = [unturn(jnp.concatenate(d, axis=0)) for d in dq]
    blocks = spread(dq, routes) + [unturn(jnp.concatenate(dk, axis=0)), jnp.concatenate(dv, axis=0)]
    grad = jnp.concatenate([b.astype(bf16) for b in blocks], axis=1)
    grad_ref[...] = grad
    back_ref[:, :dim] = dot_nt(grad, w_ref[:, :qkv_width]).astype(bf16)
    back_ref[:, dim:] = put({0: parts[0], 1: parts[1]}, rows).astype(bf16)


def mid_kernel(rs_ref, packed_ref, gain_ref, router_ref, out_ref, middle_ref, gate_ref):
    rows, dim = rs_ref.shape
    side = packed_ref[:, dim:].astype(f32)
    middle = packed_ref[:, :dim].astype(f32) + rs_ref[...].astype(f32)
    middle_ref[...] = middle
    low = (middle * norm_scale(middle) * gain_ref[...]).astype(bf16)
    out_ref[:, :dim] = low
    probs = gate_probs(low, router_ref[...], side[:, 7:8], side[:, 8:9])
    gate_ref[...] = probs
    out_ref[:, dim:] = put(
        {0: probs[:, 0:1], 1: probs[:, 1:2], 2: side[:, 7:8], 3: side[:, 8:9]}, rows
    ).astype(bf16)


def norm_back_kernel(
    route_at, where_ref, rsb_ref, rows_ref, base_ref, gain_ref, router_ref, gate_ref, side_ref,
    *out_refs
):
    count, dim = rows_ref.shape
    grad = rsb_ref[:, :dim].astype(f32)
    gp = rsb_ref[:, dim:].astype(f32)
    side = side_ref[...].astype(f32)
    p0, p1 = gate_ref[:, 0:1], gate_ref[:, 1:2]
    q0, q1 = gp[:, 0:1], gp[:, 1:2]
    inner = p0 * q0 + p1 * q1
    i0, i1 = p0 * (q0 - inner), p1 * (q1 - inner)
    rows = rows_ref[...].astype(f32)
    scale = norm_scale(rows)
    normal = rows * scale
    gain = gain_ref[...]
    low = (normal * gain).astype(bf16).astype(f32)
    route0, route1 = side[:, route_at : route_at + 1], side[:, route_at + 1 : route_at + 2]
    parts = []
    for e in range(EXPERTS):
        logit_grad = jnp.where(route0 == e, i0, 0.0) + jnp.where(route1 == e, i1, 0.0)
        grad = grad + logit_grad * router_ref[e : e + 1, :]
        parts.append(jnp.sum(logit_grad * low, axis=0, keepdims=True))
    parts.append(jnp.sum(grad * normal, axis=0, keepdims=True))
    parts.append(jnp.zeros((8 - len(parts), dim), f32))
    out_refs[0][...] = jnp.concatenate(parts, axis=0)
    weighted = grad * gain
    total = base_ref[...].astype(f32) + scale * (
        weighted - normal * jnp.mean(weighted * normal, axis=-1, keepdims=True)
    )
    for ref in out_refs[1:]:
        ref[...] = total.astype(ref.dtype)


def ffn_kernel(
    where_ref, x_ref, c_ref, wg_ref, wu_ref, wd_ref, back_ref, a_ref, gg_ref, ug_ref
):
    rows, dim = c_ref.shape
    side = x_ref[:, dim:].astype(f32)
    mine = where_ref[0].astype(f32)
    in0, in1 = side[:, 2:3] == mine, side[:, 3:4] == mine
    coef = jnp.where(in0, side[:, 0:1], 0.0) + jnp.where(in1, side[:, 1:2], 0.0)
    x = x_ref[:, :dim]
    gate = dot(x, wg_ref[...])
    up = dot(x, wu_ref[...])
    act_grad = dot(c_ref[...], wd_ref[...])
    sig = jax.nn.sigmoid(gate)
    silu = gate * sig
    act = (silu * up).astype(bf16).astype(f32)
    part = jnp.sum(act * act_grad, axis=-1, keepdims=True)
    a_ref[...] = (act * coef).astype(bf16)
    act_grad = act_grad * coef
    gg = (act_grad * up * sig * (1.0 + gate * (1.0 - sig))).astype(bf16)
    ug = (act_grad * silu).astype(bf16)
    gg_ref[...] = gg
    ug_ref[...] = ug
    back_ref[:, :dim] = (dot_nt(gg, wg_ref[...]) + dot_nt(ug, wu_ref[...])).astype(bf16)
    back_ref[:, dim:] = put(
        {0: jnp.where(in0, part, 0.0), 1: jnp.where(in1, part, 0.0)}, rows
    ).astype(bf16)


def params():
    return pltpu.CompilerParams(vmem_limit_bytes=VMEM)


def cost(flops, nbytes):
    return pl.CostEstimate(flops=int(flops), bytes_accessed=int(nbytes), transcendentals=0)


def shape(dims, dtype):
    return jax.ShapeDtypeStruct(dims, dtype)


def whole(array):
    zeros = (0,) * array.ndim
    return pl.BlockSpec(array.shape, lambda *unused: zeros)


def router_parts(router):
    high = lax.reduce_precision(router, 8, 7)
    rest = router - high
    middle = lax.reduce_precision(rest, 8, 7)
    low = rest - middle
    parts = jnp.concatenate([high, middle, low], axis=1)
    return jnp.pad(parts, ((0, 0), (0, SIDE - parts.shape[1]))).astype(bf16)


def shift(value, axis, step, size):
    return lax.ppermute(value, axis, [(i, (i + step) % size) for i in range(size)])


def local(
    tokens, norm_gain1, norm_gain2, att_router, query_maps, kv_maps, out_maps, ffn_router,
    ffn_maps, att_route, ffn_route, parents, cotangent,
):
    rows, dim = tokens.shape
    group_len = att_route.shape[0]
    zz, xx, tt = lax.axis_index("zz"), lax.axis_index("xx"), lax.axis_index("tensor")
    zs, xs, ts = lax.axis_size("zz"), lax.axis_size("xx"), lax.axis_size("tensor")
    here = jnp.stack([tt]).astype(jnp.int32)
    total = rows * zs * ts
    wide_cols = dim + SIDE

    def bring_rows(pieces):
        got = [pieces(0)] + [None] * (zs - 1)
        for k in (1, 3, 2):
            got[k] = shift(pieces(k), "zz", k, zs)
        part, width = got[0].shape
        if xs == 2:
            full = jnp.zeros((zs, xs, part, width), bf16)
            for k in (0, 1, 3, 2):
                source = (zz - k) % zs
                full = lax.dynamic_update_slice(full, got[k][None, None], (source, xx, 0, 0))
                other = shift(got[k], "xx", 1, 2)
                full = lax.dynamic_update_slice(full, other[None, None], (source, 1 - xx, 0, 0))
        else:
            half = jnp.zeros((zs, part, width), bf16)
            for k in range(zs):
                half = lax.dynamic_update_slice(half, got[k][None], ((zz - k) % zs, 0, 0))
            full = lax.all_gather(half, "xx", axis=1)
        return full.reshape(zs * xs * part, width)

    def return_rows(grad):
        width = grad.shape[1]
        grad = grad.reshape(zs, xs, -1, width)
        part = grad.shape[2]
        if xs != 2:
            summed = lax.psum_scatter(
                grad.transpose(1, 0, 2, 3), "xx", scatter_dimension=0, tiled=False
            )
        out = [None] * zs
        for k in (2, 1, 3, 0):
            target = (zz + k) % zs
            if xs == 2:
                sent = lax.dynamic_slice(grad, (target, 1 - xx, 0, 0), (1, 1, part, width))
                kept = lax.dynamic_slice(grad, (target, xx, 0, 0), (1, 1, part, width))
                piece = kept.astype(f32) + shift(sent, "xx", 1, 2).astype(f32)
                piece = piece.astype(bf16)[0, 0]
            else:
                piece = lax.dynamic_index_in_dim(summed, target, 0, keepdims=False)
            out[k] = shift(piece, "zz", k, zs) if k else piece
        return out

    packed = pl.pallas_call(
        pack_kernel,
        grid_spec=pltpu.PrefetchScalarGridSpec(
            num_scalar_prefetch=2,
            grid=(1,),
            in_specs=[
                pl.BlockSpec((rows, dim), lambda i, w, p: (0, 0)),
                pl.BlockSpec((rows, 2), lambda i, w, p: (w[0], 0)),
                pl.BlockSpec((rows, 2), lambda i, w, p: (w[0], 0)),
            ],
            out_specs=pl.BlockSpec((rows, wide_cols), lambda i, w, p: (0, 0)),
        ),
        out_shape=shape((rows, wide_cols), bf16),
        compiler_params=params(),
        name="pack",
    )(here, parents, tokens, att_route, ffn_route)
    group_tokens = lax.all_gather(packed, GROUP, axis=0, tiled=True)

    small = jnp.concatenate(
        [norm_gain1[None], norm_gain2[None], att_router.T, ffn_router.T], axis=0
    )
    small = lax.all_gather(small.reshape(1, -1), ALL, axis=0, tiled=True)
    small = small.reshape(-1, 2 + 2 * EXPERTS, norm_gain1.shape[0])
    small = small.transpose(1, 0, 2).reshape(2 + 2 * EXPERTS, dim)
    gain1, gain2 = small[0:1], small[1:2]
    router1 = jnp.pad(small[2 : 2 + EXPERTS], ((0, 8 - EXPERTS), (0, 0)))
    router2 = jnp.pad(small[2 + EXPERTS :], ((0, 8 - EXPERTS), (0, 0)))
    parts1 = router_parts(small[2 : 2 + EXPERTS].T)
    parts2 = router_parts(small[2 + EXPERTS :].T)

    maps = jnp.concatenate([query_maps, kv_maps, out_maps], axis=0).astype(bf16)
    count = maps.shape[0]
    part = maps.shape[1]
    by_head = maps.reshape(count, part, zs, HS).transpose(2, 1, 0, 3).reshape(zs, part, count * HS)
    w_att = bring_rows(
        lambda k: lax.dynamic_index_in_dim(by_head, (zz + k) % zs, 0, keepdims=False)
    )

    def expert_rows(kind):
        def piece(k):
            index = kind * EXPERTS + (zz + k) % zs
            return lax.dynamic_index_in_dim(ffn_maps, index, 0, keepdims=False).astype(bf16)

        return bring_rows(piece)

    w_gate, w_up, w_down = expert_rows(0), expert_rows(1), expert_rows(2)
    group_cot = lax.all_gather(cotangent, GROUP, axis=0, tiled=True)

    half = HS // 2
    frequency = rope_base ** (-2.0 * jnp.arange(half, dtype=f32) / HS)
    angles = jnp.arange(group_len, dtype=f32)[:, None] * frequency[None, :]
    cosines, sines = jnp.cos(angles), jnp.sin(angles)
    cos = jnp.concatenate([cosines, cosines], axis=1)
    sin = jnp.concatenate([-sines, sines], axis=1)

    trees = total // group_len
    block = lambda width: pl.BlockSpec((group_len, width), lambda i: (i, 0))
    part_att, x1, kept, gate1 = pl.pallas_call(
        att_fwd_kernel,
        grid=(trees,),
        in_specs=[
            block(wide_cols), whole(w_att), whole(parts1), whole(gain1), whole(cos), whole(sin)
        ],
        out_specs=[block(dim), block(dim), block(6 * HS), block(SIDE)],
        out_shape=[
            shape((total, dim), bf16), shape((total, dim), bf16), shape((total, 6 * HS), bf16),
            shape((total, SIDE), f32),
        ],
        compiler_params=params(),
        cost_estimate=cost(2 * total * dim * 11 * HS, 6 * total * dim),
        name="att_fwd",
    )(group_tokens, w_att, parts1, gain1, cos, sin)
    sum_att = lax.psum_scatter(part_att, GROUP, scatter_dimension=0, tiled=True)

    packed2, middle, gate2 = pl.pallas_call(
        mid_kernel,
        out_shape=[shape((rows, wide_cols), bf16), shape((rows, dim), f32), shape((rows, SIDE), f32)],
        compiler_params=params(),
        name="mid",
    )(sum_att, packed, gain2, parts2)
    x2 = lax.all_gather(packed2, GROUP, axis=0, tiled=True)

    width = w_gate.shape[1]
    step = 256
    rows_of = lambda w: pl.BlockSpec((step, w), lambda i, s: (i, 0))
    fixed = lambda: pl.BlockSpec(
        (dim, width), lambda i, s: (0, 0), pipeline_mode=pl.Buffered(buffer_count=1)
    )
    back2, act, gate_grad, up_grad = pl.pallas_call(
        ffn_kernel,
        grid_spec=pltpu.PrefetchScalarGridSpec(
            num_scalar_prefetch=1,
            grid=(total // step,),
            in_specs=[rows_of(wide_cols), rows_of(dim), fixed(), fixed(), fixed()],
            out_specs=[rows_of(wide_cols), rows_of(width), rows_of(width), rows_of(width)],
        ),
        out_shape=[shape((total, wide_cols), bf16)] + [shape((total, width), bf16)] * 3,
        compiler_params=params(),
        cost_estimate=cost(2 * total * dim * 5 * width, 6 * dim * width + 12 * total * dim),
        name="ffn",
    )(jnp.stack([zz]).astype(jnp.int32), x2, group_cot, w_gate, w_up, w_down)
    sum_back2 = lax.psum_scatter(back2, GROUP, scatter_dimension=0, tiled=True)

    part_ffn = dot_nt(act, w_down).astype(bf16)
    mixed = (
        middle + lax.psum_scatter(part_ffn, GROUP, scatter_dimension=0, tiled=True).astype(f32)
    ).astype(bf16)

    def norm_back(route_at, rsb, wide_rows, base, gain, router, gate, gate_at, outs, name):
        def pick(a):
            return pl.BlockSpec(a.shape, lambda i, w: (0,) * a.ndim)

        return pl.pallas_call(
            functools.partial(norm_back_kernel, route_at),
            grid_spec=pltpu.PrefetchScalarGridSpec(
                num_scalar_prefetch=1,
                grid=(1,),
                in_specs=[
                    pick(rsb), pl.BlockSpec((rows, dim), lambda i, w: (0, 0)), pick(base), pick(gain), pick(router),
                    pl.BlockSpec((rows, SIDE), lambda i, w: (w[0], 0)),
                    pl.BlockSpec((rows, SIDE), lambda i, w: (0, dim // SIDE)),
                ],
                out_specs=[pl.BlockSpec((8, dim), lambda i, w: (0, 0))]
                + [pl.BlockSpec((rows, dim), lambda i, w: (0, 0)) for _ in outs],
            ),
            out_shape=[shape((8, dim), f32)] + [shape((rows, dim), d) for d in outs],
            compiler_params=params(),
            name=name,
        )(gate_at, rsb, wide_rows, base, gain, router, gate, packed)

    zero = jnp.zeros((1,), jnp.int32)
    parts_ffn, middle_grad, att_cot = norm_back(
        7, sum_back2, middle, cotangent, gain2, router2, gate2, zero, [f32, bf16], "mid_back"
    )
    group_att_cot = lax.all_gather(att_cot, GROUP, axis=0, tiled=True)

    x2_low = x2[:, :dim]
    ffn_out = jnp.zeros(ffn_maps.shape, f32)
    for kind, grad in (
        (2, dot_tn(group_cot, act)), (0, dot_tn(x2_low, gate_grad)), (1, dot_tn(x2_low, up_grad))
    ):
        for k, piece in enumerate(return_rows(grad.astype(bf16))):
            index = kind * EXPERTS + (zz - k) % zs
            ffn_out = lax.dynamic_update_slice(ffn_out, piece.astype(f32)[None], (index, 0, 0))

    back1, grad_qkv, z = pl.pallas_call(
        att_bwd_kernel,
        grid=(trees,),
        in_specs=[
            block(dim), whole(w_att), block(6 * HS), block(SIDE),
            pl.BlockSpec((group_len, SIDE), lambda i: (i, dim // SIDE)), whole(cos), whole(sin),
        ],
        out_specs=[block(wide_cols), block(6 * HS), block(EXPERTS * HS)],
        out_shape=[
            shape((total, wide_cols), bf16), shape((total, 6 * HS), bf16),
            shape((total, EXPERTS * HS), bf16),
        ],
        compiler_params=params(),
        cost_estimate=cost(2 * total * dim * 11 * HS, 6 * total * dim),
        name="att_bwd",
    )(group_att_cot, w_att, kept, gate1, group_tokens, cos, sin)
    sum_back1 = lax.psum_scatter(back1, GROUP, scatter_dimension=0, tiled=True)

    grad_att = jnp.concatenate(
        [dot_tn(x1, grad_qkv).astype(bf16), dot_tn(group_att_cot, z).astype(bf16)], axis=1
    )
    gathered = jnp.zeros((zs, part, count * HS), bf16)
    for k, piece in enumerate(return_rows(grad_att)):
        gathered = lax.dynamic_update_slice(gathered, piece[None], ((zz - k) % zs, 0, 0))
    maps_grad = (
        gathered.reshape(zs, part, count, HS).transpose(2, 1, 0, 3).reshape(maps.shape).astype(f32)
    )

    parts_att, input_grad = norm_back(
        0, sum_back1, tokens, middle_grad, gain1, router1, gate1,
        (zz * ts + tt)[None].astype(jnp.int32), [bf16], "input_back",
    )

    def small_sum(parts):
        parts = parts.reshape(8, zs * xs * ts, -1).transpose(1, 0, 2)
        devices = parts.shape[0]
        summed = lax.psum_scatter(
            parts.reshape(devices, -1), ALL, scatter_dimension=0, tiled=True
        ).reshape(8, -1)
        return summed[EXPERTS], summed[:EXPERTS].T

    gain2_grad, ffn_router_grad = small_sum(parts_ffn)
    gain1_grad, att_router_grad = small_sum(parts_att)
    queries = query_maps.shape[0]
    keys = kv_maps.shape[0]
    return (
        mixed,
        input_grad,
        gain1_grad,
        gain2_grad,
        att_router_grad,
        maps_grad[:queries],
        maps_grad[queries : queries + keys],
        maps_grad[queries + keys :],
        ffn_router_grad,
        ffn_out,
    )


def solution(mesh):
    dp, tensor = mesh.shape["dp"], mesh.shape["tensor"]
    fine = Mesh(mesh.devices.reshape(EXPERTS, dp // EXPERTS, tensor), ALL)
    dps = ("zz", "xx")
    rows, flat, maps = P(ALL, None), P(ALL), P(None, dps, "tensor")
    placed = (
        rows, flat, flat, rows, maps, maps, maps, rows, maps, P(dps, None), P(dps, None), P(dps), rows
    )
    return jax.shard_map(
        local,
        mesh=fine,
        in_specs=placed,
        out_specs=(rows, rows, flat, flat, rows, maps, maps, maps, rows, maps),
        check_vma=False,
    )
```

time: 3980 us -> 1600 us (0.40)
  waiting for transfers between devices: 3100 us -> 866 us
  starting transfers between devices: 1 us -> 211 us
  matrix products: 284 us -> 86.2 us
  Pallas kernels: 0 us -> 150 us
  other arithmetic: 171 us -> 31.5 us
  local copies, waits for them, and re-layouts: 225 us -> 129 us
  blocking collectives: 174 us -> 101 us
    all_gather x8 -> x4, waiting for transfers between devices: 1510 us -> 0.01 us  [the longest x1 0.01 us: local(): group_tokens = lax.all_gather(packed, GROUP, axis=0, tiled=True)]
    reduce_scatter x10 -> x4, waiting for transfers between devices: 1580 us -> 227 us  [the longest x1 122 us: local(): sum_back2 = lax.psum_scatter(back2, GROUP, scatter_dimension=0, tiled=True)]
    ppermute x0 -> x56, waiting for transfers between devices: none -> 508 us  [shift(): lax.ppermute(value, axis, [(i, (i + step) % size) for i in range(size)])]
    ppermute x0 -> x56, starting transfers between devices: none -> 210 us  [shift(): lax.ppermute(value, axis, [(i, (i + step) % size) for i in range(size)])]
    dot_general x32 -> x6, matrix products: 280 us -> 86.2 us  [the longest x5 67.7 us: dot_tn(): lax.dot_general(a, b, (((0,), (0,)), ((), ())), preferred_element_type=f32)]
    pallas_call x0 -> x7, Pallas kernels: none -> 150 us  [the longest x1 77.5 us: local(): pl.pallas_call(ffn_kernel, grid_spec=pltpu.PrefetchScalarGridSpec(num_sca...]
    gather x22 -> x0, local copies, waits for them, and re-layouts: 132 us -> none  [the longest x8 75.1 us: collect(): flat_rows[slot_where].reshape(slot_where.shape[0] // 2, 2, buffer.shape[-1])]
    unnamed x22 -> x10, waiting for transfers between devices: 7.06 us -> 131 us
  transfers between devices with their start and end apart: 20 -> 65, of which waited for: 13 -> 31; matrix products, arithmetic and copies ran while one was open for 12% -> 15% of each run, Pallas kernels for 0% -> 2%
where the time goes in v1:
time: 1600 us; the launch traced here: 1590 us
  waiting for transfers between devices  866 us (54%)
  starting transfers between devices  211 us (13%)
  Pallas kernels  150 us (9%)
  local copies, waits for them, and re-layouts  129 us (8%)
  blocking collectives  101 us (6%)
  matrix products  86.2 us (5%)
  other arithmetic  31.5 us (2%)
    ppermute x56, waiting for transfers between devices, shift(): lax.ppermute(value, axis, [(i, (i + step) % size) for i in range(size)])  508 us
    ppermute x56, starting transfers between devices, shift(): lax.ppermute(value, axis, [(i, (i + step) % size) for i in range(size)])  210 us
    unnamed x10, waiting for transfers between devices  131 us
    reduce_scatter x1, waiting for transfers between devices, local(): sum_back2 = lax.psum_scatter(back2, GROUP, scatter_dimension=0, tiled=True)  122 us
    reduce_scatter x1, waiting for transfers between devices, local(): sum_att = lax.psum_scatter(part_att, GROUP, scatter_dimension=0, tiled=True)  105 us
    all_gather x1, blocking collectives, local(): small = lax.all_gather(small.reshape(1, -1), ALL, axis=0, tiled=True)  101 us
    pallas_call x1, Pallas kernels, local(): pl.pallas_call(ffn_kernel, grid_spec=pltpu.PrefetchScalarGridSpec(num_sca...  77.5 us
    dot_general x5, matrix products, dot_tn(): lax.dot_general(a, b, (((0,), (0,)), ((), ())), preferred_element_type=f32)  67.7 us
  transfers between devices with their start and end apart: 65, of which 31 were waited for; matrix products, arithmetic and copies ran while one was open for 15% of the time, Pallas kernels for 2%

profile of v1, /device:TPU:0, one launch (start us, length us, event | category | flops | bytes accessed | tf_op | source)
XLA Modules:
  0.0 1589.8 jit_solution(1270710565468231557)
XLA Ops:
  32.6 101.4 %all-gather = f32[32,1,640]{2,1,0:T(1,128)S(1)} all-gather(f32[1,1,640]{2,1,0:T(1,128)S(1)} %reshape.208), channel_id=1, replica_groups=mesh['zz'=4,'xx'=2,'tensor'=4] {'zz','xx','tensor'}, dimensions={0}, use_global_device_ids=true | all-gather | bytes 84480 | tf_op jit(solution)/shard_map/all_gather | solution.py:416
  142.7 22.6 %collective-permute-start.2 = (bf16[256,1280]{1,0:T(8,128)(2,1)}, bf16[256,1280]{1,0:T(8,128)(2,1)S(1)}, u32[]{:S(2)}, u32[]{:S(2)}) collective-permute-start(bf16[256,1280]{1,0:T(8,128)(2,1)} %collective-permute-done.1), channel_id=1, source_target_pairs={{0,4},{4,0},{1,5},{5,1},{2,6},{6,2},{3,7},{7,3},{8,12},{12,8},{9,1... | collective-permute-start | bytes 1966088 | tf_op jit(solution)/shard_map/ppermute | solution.py:340
  209.7 29.1 %att_fwd.1 = (bf16[2048,2048]{1,0:T(8,128)(2,1)}, bf16[2048,2048]{1,0:T(8,128)(2,1)}, bf16[2048,768]{1,0:T(8,128)(2,1)}, f32[2048,128]{1,0:T(8,128)}) custom-call(bf16[2048,2176]{1,0:T(8,128)(2,1)} %all-gather.6.cloned.1.call-done.tok_ref.side_ref, bf16[2048,1280]{1,0:T(8,128)(2,1)} %bitcast.18.w_ref, bf16[2048,128]{1,0:T(8,128)(2,1)} %pad.16.clone.router_ref, ...), custom_call_target="tpu_custom_call" | custom-call | flops 11811160064 | bytes 25165824 | tf_op jit(solution)/shard_map/att_fwd/pallas_call | solution.py:452
  241.6 104.7 %reduce-scatter.5.cloned.1.call-done.rs_ref = bf16[128,2048]{1,0:T(8,128)(2,1)} async-done(((bf16[2048,2048]{1,0:T(8,128)(2,1)}), bf16[128,2048]{1,0:T(8,128)(2,1)}) %reduce-scatter.5.cloned.1.call-update) | async-done | bytes 524304 | tf_op jit(solution)/shard_map/reduce_scatter | solution.py:467
  393.9 16.0 %collective-permute-start.17 = (bf16[256,1408]{1,0:T(8,128)(2,1)S(1)}, bf16[256,1408]{1,0:T(8,128)(2,1)S(1)}, u32[]{:S(2)}, u32[]{:S(2)}) collective-permute-start(bf16[256,1408]{1,0:T(8,128)(2,1)S(1)} %get-tuple-element.78), channel_id=1, source_target_pairs={{0,24},{8,0},{16,8},{24,16},{1,25},{9,1},{17,9},{25,17},{2,26},{10... | collective-permute-start | bytes 2162696 | tf_op jit(solution)/shard_map/ppermute | solution.py:340
  412.7 60.1 %collective-permute-done.15 = bf16[256,1408]{1,0:T(8,128)(2,1)S(1)} collective-permute-done((bf16[256,1408]{1,0:T(8,128)(2,1)S(1)}, bf16[256,1408]{1,0:T(8,128)(2,1)S(1)}, u32[]{:S(2)}, u32[]{:S(2)}) %collective-permute-start.15) | collective-permute-done | bytes 720928 | tf_op jit(solution)/shard_map/ppermute | solution.py:340
  472.9 29.0 %collective-permute-start.22 = (bf16[256,1408]{1,0:T(8,128)(2,1)S(1)}, bf16[256,1408]{1,0:T(8,128)(2,1)S(1)}, u32[]{:S(2)}, u32[]{:S(2)}) collective-permute-start(bf16[256,1408]{1,0:T(8,128)(2,1)S(1)} %copy-done.5), channel_id=1, source_target_pairs={{0,8},{8,16},{16,24},{24,0},{1,9},{9,17},{17,25},{25,1},{2,10},{10... | collective-permute-start | bytes 2162696 | tf_op jit(solution)/shard_map/ppermute | solution.py:340
  505.4 27.8 %collective-permute-done.22 = bf16[256,1408]{1,0:T(8,128)(2,1)S(1)} collective-permute-done((bf16[256,1408]{1,0:T(8,128)(2,1)S(1)}, bf16[256,1408]{1,0:T(8,128)(2,1)S(1)}, u32[]{:S(2)}, u32[]{:S(2)}) %collective-permute-start.22) | collective-permute-done | bytes 720928 | tf_op jit(solution)/shard_map/ppermute | solution.py:340
  543.8 14.3 collective-permute-done.11
  563.7 13.4 collective-permute-done.16
  580.7 35.9 %collective-permute-done.19 = bf16[256,1408]{1,0:T(8,128)(2,1)S(1)} collective-permute-done((bf16[256,1408]{1,0:T(8,128)(2,1)S(1)}, bf16[256,1408]{1,0:T(8,128)(2,1)S(1)}, u32[]{:S(2)}, u32[]{:S(2)}) %collective-permute-start.19) | collective-permute-done | bytes 720928 | tf_op jit(solution)/shard_map/ppermute | solution.py:340
  618.7 33.3 %collective-permute-done.26 = bf16[256,1408]{1,0:T(8,128)(2,1)S(1)} collective-permute-done((bf16[256,1408]{1,0:T(8,128)(2,1)S(1)}, bf16[256,1408]{1,0:T(8,128)(2,1)S(1)}, u32[]{:S(2)}, u32[]{:S(2)}) %collective-permute-start.26) | collective-permute-done | bytes 720928 | tf_op jit(solution)/shard_map/ppermute | solution.py:340
  657.8 13.3 collective-permute-done.25
  685.5 77.5 %ffn.1 = (bf16[2048,2176]{1,0:T(8,128)(2,1)}, bf16[2048,1408]{1,0:T(8,128)(2,1)}, bf16[2048,1408]{1,0:T(8,128)(2,1)}, bf16[2048,1408]{1,0:T(8,128)(2,1)}) custom-call(s32[1]{0:T(128)} %bitcast.26.where_ref, bf16[2048,2176]{1,0:T(8,128)(2,1)} %all-gather.8.cloned.1.call-done.x_ref, bf16[2048,2048]{1,0:T(8,128)(2,1)} %all-gather.10.cloned.1.call-done.c_ref, ...), custom_call_target="tpu_custom_call" | custom-call | flops 59055800320 | bytes 67633152 | tf_op jit(solution)/shard_map/ffn/pallas_call | solution.py:483
  763.7 122.4 %reduce-scatter.9.cloned.1.call-done.rsb_ref = bf16[128,2176]{1,0:T(8,128)(2,1)} async-done(((bf16[2048,2176]{1,0:T(8,128)(2,1)}), bf16[128,2176]{1,0:T(8,128)(2,1)}) %reduce-scatter.9.cloned.1.call-update) | async-done | bytes 557072 | tf_op jit(solution)/shard_map/reduce_scatter | solution.py:496
  890.6 18.5 %convolution_convert_fusion = bf16[2048,2048]{1,0:T(8,128)(2,1)} fusion(bf16[2048,1408]{1,0:T(8,128)(2,1)} %get-tuple-element.32, bf16[2048,1408]{1,0:T(8,128)(2,1)} %bitcast.65.wd_ref), kind=kOutput, calls=%fused_computation | convolution fusion | flops 11815354368 | bytes 19922944 | tf_op jit(solution)/shard_map/dot_general | solution.py:28
  909.9 17.9 %fusion.2 = bf16[2048,1408]{0,1:T(8,128)(2,1)} fusion(bf16[2048,1408]{1,0:T(8,128)(2,1)} %get-tuple-element.32, bf16[2048,2048]{1,0:T(8,128)(2,1)} %all-gather.10.cloned.1.call-done.c_ref), kind=kOutput, calls=%fused_computation.6 | convolution fusion | flops 11814043648 | bytes 19922944 | tf_op jit(solution)/shard_map/dot_general | solution.py:32
  942.6 17.3 %convolution_convert_fusion.2 = bf16[2048,1408]{1,0:T(8,128)(2,1)S(1)} fusion(bf16[2048,1408]{1,0:T(8,128)(2,1)} %get-tuple-element.46, bf16[2048,2176]{1,0:T(8,128)(2,1)} %all-gather.8.cloned.1.call-done.x_ref), kind=kOutput, calls=%fused_computation.2 | convolution fusion | flops 11814043648 | bytes 19922944 | tf_op jit(solution)/shard_map/dot_general | solution.py:32
  963.2 17.5 %convolution_convert_fusion.1 = bf16[2048,1408]{1,0:T(8,128)(2,1)S(1)} fusion(bf16[2048,1408]{1,0:T(8,128)(2,1)} %get-tuple-element.47, bf16[2048,2176]{1,0:T(8,128)(2,1)} %all-gather.8.cloned.1.call-done.x_ref), kind=kOutput, calls=%fused_computation.1 | convolution fusion | flops 11814043648 | bytes 19922944 | tf_op jit(solution)/shard_map/dot_general | solution.py:32
  990.5 14.0 collective-permute-done.47
  1021.4 14.0 collective-permute-done.43
  1052.2 14.0 collective-permute-done.52
  1067.9 13.8 collective-permute-done.50
  1085.2 29.3 %att_bwd.1 = (bf16[2048,2176]{1,0:T(8,128)(2,1)}, bf16[2048,768]{1,0:T(8,128)(2,1)}, bf16[2048,512]{1,0:T(8,128)(2,1)}) custom-call(bf16[2048,2048]{1,0:T(8,128)(2,1)} %all-gather.12.cloned.1.call-done.c_ref, bf16[2048,1280]{1,0:T(8,128)(2,1)} %bitcast.18.w_ref, bf16[2048,768]{1,0:T(8,128)(2,1)} %get-tuple-element.36.keep_ref, ...), custom_call_target="tpu_custom_call" | custom-call | flops 11811160064 | bytes 25165824 | tf_op jit(solution)/shard_map/att_bwd/pallas_call | solution.py:540
  1123.7 28.4 %collective-permute-done.41 = bf16[256,1408]{1,0:T(8,128)(2,1)} collective-permute-done((bf16[256,1408]{1,0:T(8,128)(2,1)}, bf16[256,1408]{1,0:T(8,128)(2,1)}, u32[]{:S(2)}, u32[]{:S(2)}) %collective-permute-start.41) | collective-permute-done | bytes 720928 | tf_op jit(solution)/shard_map/ppermute | solution.py:340
  1153.4 27.8 %collective-permute-start.51 = (bf16[256,1408]{1,0:T(8,128)(2,1)S(1)}, bf16[256,1408]{1,0:T(8,128)(2,1)S(1)}, u32[]{:S(2)}, u32[]{:S(2)}) collective-permute-start(bf16[256,1408]{1,0:T(8,128)(2,1)S(1)} %copy-done.8), channel_id=1, source_target_pairs={{0,8},{8,16},{16,24},{24,0},{1,9},{9,17},{17,25},{25,1},{2,10},{10... | collective-permute-start | bytes 2162696 | tf_op jit(solution)/shard_map/ppermute | solution.py:340
  1184.4 63.8 %collective-permute-done.46 = bf16[256,1408]{1,0:T(8,128)(2,1)S(1)} collective-permute-done((bf16[256,1408]{1,0:T(8,128)(2,1)S(1)}, bf16[256,1408]{1,0:T(8,128)(2,1)S(1)}, u32[]{:S(2)}, u32[]{:S(2)}) %collective-permute-start.46) | collective-permute-done | bytes 720928 | tf_op jit(solution)/shard_map/ppermute | solution.py:340
  1284.1 13.0 collective-permute-done.53
  1312.2 14.0 collective-permute-done.29
  1340.2 43.7 %collective-permute-start.30 = (bf16[256,1280]{1,0:T(8,128)(2,1)}, bf16[256,1280]{1,0:T(8,128)(2,1)}, u32[]{:S(2)}, u32[]{:S(2)}) collective-permute-start(bf16[256,1280]{1,0:T(8,128)(2,1)} %get-tuple-element.109), channel_id=1, source_target_pairs={{0,8},{8,16},{16,24},{24,0},{1,9},{9,17},{17,25},{25,1},{2,10},{10... | collective-permute-start | bytes 1966088 | tf_op jit(solution)/shard_map/ppermute | solution.py:340
  1400.7 14.9 collective-permute-done.32
  1448.7 131.0 %all-reduce.9.cloned.1.call-done = (f32[32,512]{1,0:T(8,128)}, f32[32,512]{1,0:T(8,128)}) async-done(((f32[32,512]{1,0:T(8,128)}, f32[32,512]{1,0:T(8,128)}), (f32[32,512]{1,0:T(8,128)}, f32[32,512]{1,0:T(8,128)})) %all-reduce.9.cloned.1.call-update) | async-done | bytes 131088
  (292 shorter events, 381.4 us)
Async XLA Ops:
  7.2 202.5 %all-gather.6.cloned.1.call-start = ((), (), s32[]{:S(2)}) async-start(), calls=%async_computation.4 | async-start | bytes 9469952 | tf_op jit(solution)/shard_map/all_gather | solution.py:411
  13.1 333.2 %reduce-scatter.5.cloned.1.call-start = ((), (), s32[]{:S(2)}) async-start(), calls=%async_computation.5 | async-start | bytes 8912896 | tf_op jit(solution)/shard_map/reduce_scatter | solution.py:467
  20.1 147.1 %collective-permute-start = (bf16[256,1280]{1,0:T(8,128)(2,1)S(1)}, bf16[256,1280]{1,0:T(8,128)(2,1)}, u32[]{:S(2)}, u32[]{:S(2)}) collective-permute-start(bf16[256,1280]{1,0:T(8,128)(2,1)S(1)} %bitcast.246), channel_id=1, source_target_pairs={{0,4},{4,0},{1,5},{5,1},{2,6},{6,2},{3,7},{7,3},{8,12},{12,8},{9,1... | collective-permute-start | bytes 1966088 | tf_op jit(solution)/shard_map/ppermute | solution.py:340
  25.4 117.3 %collective-permute-start.1 = (bf16[256,1280]{1,0:T(8,128)(2,1)}, bf16[256,1280]{1,0:T(8,128)(2,1)}, u32[]{:S(2)}, u32[]{:S(2)}) collective-permute-start(bf16[256,1280]{1,0:T(8,128)(2,1)} %bitcast.9), channel_id=1, source_target_pairs={{0,8},{8,16},{16,24},{24,0},{1,9},{9,17},{17,25},{25,1},{2,10},{10... | collective-permute-start | bytes 1966088 | tf_op jit(solution)/shard_map/ppermute | solution.py:340
  29.1 136.1 %collective-permute-start.3 = (bf16[256,1280]{1,0:T(8,128)(2,1)}, bf16[256,1280]{1,0:T(8,128)(2,1)}, u32[]{:S(2)}, u32[]{:S(2)}) collective-permute-start(bf16[256,1280]{1,0:T(8,128)(2,1)} %bitcast.12), channel_id=1, source_target_pairs={{0,24},{8,0},{16,8},{24,16},{1,25},{9,1},{17,9},{25,17},{2,26},{10... | collective-permute-start | bytes 1966088 | tf_op jit(solution)/shard_map/ppermute | solution.py:340
  31.6 133.7 %collective-permute-start.5 = (bf16[256,1280]{1,0:T(8,128)(2,1)S(1)}, bf16[256,1280]{1,0:T(8,128)(2,1)S(1)}, u32[]{:S(2)}, u32[]{:S(2)}) collective-permute-start(bf16[256,1280]{1,0:T(8,128)(2,1)S(1)} %bitcast.250), channel_id=1, source_target_pairs={{0,16},{8,24},{16,0},{24,8},{1,17},{9,25},{17,1},{25,9},{2,18},{10... | collective-permute-start | bytes 1966088 | tf_op jit(solution)/shard_map/ppermute | solution.py:340
  238.7 446.8 %all-gather.10.cloned.1.call-start = ((), (), s32[]{:S(2)}) async-start(), calls=%async_computation.7 | async-start | bytes 8912896 | tf_op jit(solution)/shard_map/all_gather | solution.py:441
  239.5 446.0 %all-gather.8.cloned.1.call-start = ((), (), s32[]{:S(2)}) async-start(), calls=%async_computation.6 | async-start | bytes 9469952 | tf_op jit(solution)/shard_map/all_gather | solution.py:475
  349.3 536.8 %reduce-scatter.9.cloned.1.call-start = ((), (), s32[]{:S(2)}) async-start(), calls=%async_computation.9 | async-start | bytes 9469952 | tf_op jit(solution)/shard_map/reduce_scatter | solution.py:496
  361.3 178.1 %collective-permute-start.10 = (bf16[256,1408]{1,0:T(8,128)(2,1)}, bf16[256,1408]{1,0:T(8,128)(2,1)S(1)}, u32[]{:S(2)}, u32[]{:S(2)}) collective-permute-start(bf16[256,1408]{1,0:T(8,128)(2,1)} %get-tuple-element.81), channel_id=1, source_target_pairs={{0,24},{8,0},{16,8},{24,16},{1,25},{9,1},{17,9},{25,17},{2,26},{10... | collective-permute-start | bytes 2162696 | tf_op jit(solution)/shard_map/ppermute | solution.py:340
  363.4 197.3 %collective-permute-start.12 = (bf16[256,1408]{1,0:T(8,128)(2,1)}, bf16[256,1408]{1,0:T(8,128)(2,1)S(1)}, u32[]{:S(2)}, u32[]{:S(2)}) collective-permute-start(bf16[256,1408]{1,0:T(8,128)(2,1)} %get-tuple-element.80), channel_id=1, source_target_pairs={{0,16},{8,24},{16,0},{24,8},{1,17},{9,25},{17,1},{25,9},{2,18},{10... | collective-permute-start | bytes 2162696 | tf_op jit(solution)/shard_map/ppermute | solution.py:340
  380.0 92.8 %collective-permute-start.15 = (bf16[256,1408]{1,0:T(8,128)(2,1)S(1)}, bf16[256,1408]{1,0:T(8,128)(2,1)S(1)}, u32[]{:S(2)}, u32[]{:S(2)}) collective-permute-start(bf16[256,1408]{1,0:T(8,128)(2,1)S(1)} %copy-done.7), channel_id=1, source_target_pairs={{0,8},{8,16},{16,24},{24,0},{1,9},{9,17},{17,25},{25,1},{2,10},{10... | collective-permute-start | bytes 2162696 | tf_op jit(solution)/shard_map/ppermute | solution.py:340
  393.9 169.5 %collective-permute-start.17 = (bf16[256,1408]{1,0:T(8,128)(2,1)S(1)}, bf16[256,1408]{1,0:T(8,128)(2,1)S(1)}, u32[]{:S(2)}, u32[]{:S(2)}) collective-permute-start(bf16[256,1408]{1,0:T(8,128)(2,1)S(1)} %get-tuple-element.78), channel_id=1, source_target_pairs={{0,24},{8,0},{16,8},{24,16},{1,25},{9,1},{17,9},{25,17},{2,26},{10... | collective-permute-start | bytes 2162696 | tf_op jit(solution)/shard_map/ppermute | solution.py:340
  410.9 91.9 %collective-permute-start.21 = (bf16[256,1408]{1,0:T(8,128)(2,1)S(1)}, bf16[256,1408]{1,0:T(8,128)(2,1)S(1)}, u32[]{:S(2)}, u32[]{:S(2)}) collective-permute-start(bf16[256,1408]{1,0:T(8,128)(2,1)S(1)} %copy-done.6), channel_id=1, source_target_pairs={{0,4},{4,0},{1,5},{5,1},{2,6},{6,2},{3,7},{7,3},{8,12},{12,8},{9,1... | collective-permute-start | bytes 2162696 | tf_op jit(solution)/shard_map/ppermute | solution.py:340
  533.2 83.5 %collective-permute-start.19 = (bf16[256,1408]{1,0:T(8,128)(2,1)S(1)}, bf16[256,1408]{1,0:T(8,128)(2,1)S(1)}, u32[]{:S(2)}, u32[]{:S(2)}) collective-permute-start(bf16[256,1408]{1,0:T(8,128)(2,1)S(1)} %get-tuple-element.77), channel_id=1, source_target_pairs={{0,16},{8,24},{16,0},{24,8},{1,17},{9,25},{17,1},{25,9},{2,18},{10... | collective-permute-start | bytes 2162696 | tf_op jit(solution)/shard_map/ppermute | solution.py:340
  539.4 78.4 %collective-permute-start.24 = (bf16[256,1408]{1,0:T(8,128)(2,1)S(1)}, bf16[256,1408]{1,0:T(8,128)(2,1)S(1)}, u32[]{:S(2)}, u32[]{:S(2)}) collective-permute-start(bf16[256,1408]{1,0:T(8,128)(2,1)S(1)} %get-tuple-element.83), channel_id=1, source_target_pairs={{0,24},{8,0},{16,8},{24,16},{1,25},{9,1},{17,9},{25,17},{2,26},{10... | collective-permute-start | bytes 2162696 | tf_op jit(solution)/shard_map/ppermute | solution.py:340
  560.7 91.3 %collective-permute-start.26 = (bf16[256,1408]{1,0:T(8,128)(2,1)S(1)}, bf16[256,1408]{1,0:T(8,128)(2,1)S(1)}, u32[]{:S(2)}, u32[]{:S(2)}) collective-permute-start(bf16[256,1408]{1,0:T(8,128)(2,1)S(1)} %get-tuple-element.72), channel_id=1, source_target_pairs={{0,16},{8,24},{16,0},{24,8},{1,17},{9,25},{17,1},{25,9},{2,18},{10... | collective-permute-start | bytes 2162696 | tf_op jit(solution)/shard_map/ppermute | solution.py:340
  563.4 109.6 %collective-permute-start.13 = (bf16[256,1408]{1,0:T(8,128)(2,1)S(1)}, bf16[256,1408]{1,0:T(8,128)(2,1)S(1)}, u32[]{:S(2)}, u32[]{:S(2)}) collective-permute-start(bf16[256,1408]{1,0:T(8,128)(2,1)S(1)} %collective-permute-done.12), channel_id=1, source_target_pairs={{0,4},{4,0},{1,5},{5,1},{2,6},{6,2},{3,7},{7,3},{8,12},{12,8},{9,1... | collective-permute-start | bytes 2162696 | tf_op jit(solution)/shard_map/ppermute | solution.py:340
  577.1 76.5 %collective-permute-start.18 = (bf16[256,1408]{1,0:T(8,128)(2,1)S(1)}, bf16[256,1408]{1,0:T(8,128)(2,1)S(1)}, u32[]{:S(2)}, u32[]{:S(2)}) collective-permute-start(bf16[256,1408]{1,0:T(8,128)(2,1)S(1)} %collective-permute-done.17), channel_id=1, source_target_pairs={{0,4},{4,0},{1,5},{5,1},{2,6},{6,2},{3,7},{7,3},{8,12},{12,8},{9,1... | collective-permute-start | bytes 2162696 | tf_op jit(solution)/shard_map/ppermute | solution.py:340
  763.0 322.2 %all-gather.12.cloned.1.call-start = ((), (), s32[]{:S(2)}) async-start(), calls=%async_computation.10 | async-start | bytes 8912896 | tf_op jit(solution)/shard_map/all_gather | solution.py:529
  890.4 498.5 %reduce-scatter.7.cloned.1.call-start = ((), (), s32[]{:S(2)}) async-start(), calls=%async_computation.8 | async-start | bytes 8912896 | tf_op jit(solution)/shard_map/reduce_scatter | solution.py:500
  909.2 522.8 %reduce-scatter.11.cloned.1.call-start = ((), (), s32[]{:S(2)}) async-start(), calls=%async_computation.11 | async-start | bytes 9469952 | tf_op jit(solution)/shard_map/reduce_scatter | solution.py:556
  989.0 77.2 %collective-permute-start.52 = (bf16[1,1,256,1408]{3,2,1,0:T(8,128)(2,1)S(1)}, bf16[1,1,256,1408]{3,2,1,0:T(8,128)(2,1)S(1)}, u32[]{:S(2)}, u32[]{:S(2)}) collective-permute-start(bf16[1,1,256,1408]{3,2,1,0:T(8,128)(2,1)S(1)} %get-tuple-element.88), channel_id=1, source_target_pairs={{0,4},{4,0},{1,5},{5,1},{2,6},{6,2},{3,7},{7,3},{8,12},{12,8},{9,1... | collective-permute-start | bytes 2162696 | tf_op jit(solution)/shard_map/ppermute | solution.py:340
  1004.4 77.2 %collective-permute-start.50 = (bf16[1,1,256,1408]{3,2,1,0:T(8,128)(2,1)S(1)}, bf16[1,1,256,1408]{3,2,1,0:T(8,128)(2,1)S(1)}, u32[]{:S(2)}, u32[]{:S(2)}) collective-permute-start(bf16[1,1,256,1408]{3,2,1,0:T(8,128)(2,1)S(1)} %get-tuple-element.89), channel_id=1, source_target_pairs={{0,4},{4,0},{1,5},{5,1},{2,6},{6,2},{3,7},{7,3},{8,12},{12,8},{9,1... | collective-permute-start | bytes 2162696 | tf_op jit(solution)/shard_map/ppermute | solution.py:340
  1019.9 94.7 %collective-permute-start.35 = (bf16[1,1,256,1408]{3,2,1,0:T(8,128)(2,1)}, bf16[1,1,256,1408]{3,2,1,0:T(8,128)(2,1)}, u32[]{:S(2)}, u32[]{:S(2)}) collective-permute-start(bf16[1,1,256,1408]{3,2,1,0:T(8,128)(2,1)} %get-tuple-element.104), channel_id=1, source_target_pairs={{0,4},{4,0},{1,5},{5,1},{2,6},{6,2},{3,7},{7,3},{8,12},{12,8},{9,1... | collective-permute-start | bytes 2162696 | tf_op jit(solution)/shard_map/ppermute | solution.py:340
  1035.3 118.1 %collective-permute-start.42 = (bf16[1,1,256,1408]{3,2,1,0:T(8,128)(2,1)}, bf16[1,1,256,1408]{3,2,1,0:T(8,128)(2,1)}, u32[]{:S(2)}, u32[]{:S(2)}) collective-permute-start(bf16[1,1,256,1408]{3,2,1,0:T(8,128)(2,1)} %get-tuple-element.97), channel_id=1, source_target_pairs={{0,4},{4,0},{1,5},{5,1},{2,6},{6,2},{3,7},{7,3},{8,12},{12,8},{9,1... | collective-permute-start | bytes 2162696 | tf_op jit(solution)/shard_map/ppermute | solution.py:340
  1050.8 198.4 %collective-permute-start.49 = (bf16[1,1,256,1408]{3,2,1,0:T(8,128)(2,1)}, bf16[1,1,256,1408]{3,2,1,0:T(8,128)(2,1)}, u32[]{:S(2)}, u32[]{:S(2)}) collective-permute-start(bf16[1,1,256,1408]{3,2,1,0:T(8,128)(2,1)} %get-tuple-element.90), channel_id=1, source_target_pairs={{0,4},{4,0},{1,5},{5,1},{2,6},{6,2},{3,7},{7,3},{8,12},{12,8},{9,1... | collective-permute-start | bytes 2162696 | tf_op jit(solution)/shard_map/ppermute | solution.py:340
  1114.6 465.2 %all-reduce.9.cloned.1.call-start = ((), (), s32[]{:S(2)}) async-start(), calls=%async_computation.12 | async-start | bytes 262144
  1121.5 126.7 %collective-permute-start.46 = (bf16[256,1408]{1,0:T(8,128)(2,1)S(1)}, bf16[256,1408]{1,0:T(8,128)(2,1)S(1)}, u32[]{:S(2)}, u32[]{:S(2)}) collective-permute-start(bf16[256,1408]{1,0:T(8,128)(2,1)S(1)} %get-tuple-element.92), channel_id=1, source_target_pairs={{0,16},{8,24},{16,0},{24,8},{1,17},{9,25},{17,1},{25,9},{2,18},{10... | collective-permute-start | bytes 2162696 | tf_op jit(solution)/shard_map/ppermute | solution.py:340
  1152.0 97.1 %collective-permute-start.48 = (bf16[256,1408]{1,0:T(8,128)(2,1)S(1)}, bf16[256,1408]{1,0:T(8,128)(2,1)S(1)}, u32[]{:S(2)}, u32[]{:S(2)}) collective-permute-start(bf16[256,1408]{1,0:T(8,128)(2,1)S(1)} %get-tuple-element.91), channel_id=1, source_target_pairs={{0,24},{8,0},{16,8},{24,16},{1,25},{9,1},{17,9},{25,17},{2,26},{10... | collective-permute-start | bytes 2162696 | tf_op jit(solution)/shard_map/ppermute | solution.py:340
  1153.4 97.6 %collective-permute-start.51 = (bf16[256,1408]{1,0:T(8,128)(2,1)S(1)}, bf16[256,1408]{1,0:T(8,128)(2,1)S(1)}, u32[]{:S(2)}, u32[]{:S(2)}) collective-permute-start(bf16[256,1408]{1,0:T(8,128)(2,1)S(1)} %copy-done.8), channel_id=1, source_target_pairs={{0,8},{8,16},{16,24},{24,0},{1,9},{9,17},{17,25},{25,1},{2,10},{10... | collective-permute-start | bytes 2162696 | tf_op jit(solution)/shard_map/ppermute | solution.py:340
  1182.8 114.4 %collective-permute-start.53 = (bf16[256,1408]{1,0:T(8,128)(2,1)S(1)}, bf16[256,1408]{1,0:T(8,128)(2,1)}, u32[]{:S(2)}, u32[]{:S(2)}) collective-permute-start(bf16[256,1408]{1,0:T(8,128)(2,1)S(1)} %get-tuple-element.85), channel_id=1, source_target_pairs={{0,16},{8,24},{16,0},{24,8},{1,17},{9,25},{17,1},{25,9},{2,18},{10... | collective-permute-start | bytes 2162696 | tf_op jit(solution)/shard_map/ppermute | solution.py:340
  (54 other events, 2276.4 us)
Sparse Core Ops, SparseCore 0:
  13.2 127.0 all-gather.5
  238.9 107.3 reduce-scatter.4
  348.4 141.5 all-gather.9
  492.2 131.3 all-gather.7
  763.2 122.8 reduce-scatter.8
  890.5 74.6 all-gather.11
  969.8 104.6 reduce-scatter.6
  1114.7 186.0 reduce-scatter.10
  1437.9 141.8 all-reduce.8

commit v2 on v1

--- a/solution.py
+++ b/solution.py
@@ -234,7 +234,8 @@
     back_ref[:, dim:] = put({0: parts[0], 1: parts[1]}, rows).astype(bf16)
 
 
-def mid_kernel(rs_ref, packed_ref, gain_ref, router_ref, out_ref, middle_ref, gate_ref):
+def mid_kernel(rs_ref, packed_ref, gain_ref, router_ref, *refs):
+    out_ref, middle_ref, gate_ref = refs[-3:]
     rows, dim = rs_ref.shape
     side = packed_ref[:, dim:].astype(f32)
     middle = packed_ref[:, :dim].astype(f32) + rs_ref[...].astype(f32)
@@ -249,9 +250,10 @@
 
 
 def norm_back_kernel(
-    route_at, where_ref, rsb_ref, rows_ref, base_ref, gain_ref, router_ref, gate_ref, side_ref,
-    *out_refs
+    route_at, outs, where_ref, rsb_ref, rows_ref, base_ref, gain_ref, router_ref, gate_ref, side_ref,
+    *refs
 ):
+    out_refs = refs[-outs:]
     count, dim = rows_ref.shape
     grad = rsb_ref[:, :dim].astype(f32)
     gp = rsb_ref[:, dim:].astype(f32)
@@ -282,40 +284,105 @@
         ref[...] = total.astype(ref.dtype)
 
 
-def ffn_kernel(
-    where_ref, x_ref, c_ref, wg_ref, wu_ref, wd_ref, back_ref, a_ref, gg_ref, ug_ref
-):
-    rows, dim = c_ref.shape
+def ffn_coef(side, mine):
+    in0, in1 = side[:, 2:3] == mine, side[:, 3:4] == mine
+    return in0, in1, jnp.where(in0, side[:, 0:1], 0.0) + jnp.where(in1, side[:, 1:2], 0.0)
+
+
+def ffn_fwd_kernel(where_ref, x_ref, wg_ref, wu_ref, gate_ref, up_ref, a_ref):
+    dim = wg_ref.shape[0]
     side = x_ref[:, dim:].astype(f32)
-    mine = where_ref[0].astype(f32)
-    in0, in1 = side[:, 2:3] == mine, side[:, 3:4] == mine
-    coef = jnp.where(in0, side[:, 0:1], 0.0) + jnp.where(in1, side[:, 1:2], 0.0)
+    coef = ffn_coef(side, where_ref[0].astype(f32))[2]
     x = x_ref[:, :dim]
     gate = dot(x, wg_ref[...])
     up = dot(x, wu_ref[...])
+    gate_ref[...] = gate.astype(bf16)
+    up_ref[...] = up.astype(bf16)
+    a_ref[...] = (gate * jax.nn.sigmoid(gate) * up * coef).astype(bf16)
+
+
+def ffn_act_kernel(
+    where_ref, side_ref, gate_ref, up_ref, c_ref, wd_ref, wait_ref, gg_ref, ug_ref, part_ref
+):
+    rows = c_ref.shape[0]
+    in0, in1, coef = ffn_coef(side_ref[...].astype(f32), where_ref[0].astype(f32))
+    gate = gate_ref[...].astype(f32)
+    up = up_ref[...].astype(f32)
     act_grad = dot(c_ref[...], wd_ref[...])
     sig = jax.nn.sigmoid(gate)
     silu = gate * sig
-    act = (silu * up).astype(bf16).astype(f32)
-    part = jnp.sum(act * act_grad, axis=-1, keepdims=True)
-    a_ref[...] = (act * coef).astype(bf16)
+    part = jnp.sum(silu * up * act_grad, axis=-1, keepdims=True)
     act_grad = act_grad * coef
-    gg = (act_grad * up * sig * (1.0 + gate * (1.0 - sig))).astype(bf16)
-    ug = (act_grad * silu).astype(bf16)
-    gg_ref[...] = gg
-    ug_ref[...] = ug
-    back_ref[:, :dim] = (dot_nt(gg, wg_ref[...]) + dot_nt(ug, wu_ref[...])).astype(bf16)
-    back_ref[:, dim:] = put(
+    gg_ref[...] = (act_grad * up * sig * (1.0 + gate * (1.0 - sig))).astype(bf16)
+    ug_ref[...] = (act_grad * silu).astype(bf16)
+    part_ref[...] = put(
         {0: jnp.where(in0, part, 0.0), 1: jnp.where(in1, part, 0.0)}, rows
     ).astype(bf16)
 
 
+def ffn_back_kernel(gg_ref, ug_ref, part_ref, wg_ref, wu_ref, wait_ref, back_ref):
+    dim = wg_ref.shape[0]
+    back_ref[:, :dim] = (
+        dot_nt(gg_ref[...], wg_ref[...]) + dot_nt(ug_ref[...], wu_ref[...])
+    ).astype(bf16)
+    back_ref[:, dim:] = part_ref[...]
+
+
+def split_kernel(query_ref, kv_ref, out_ref, wait_ref, piece_ref):
+    for head in range(piece_ref.shape[0]):
+        place = 0
+        for ref in (query_ref, kv_ref, out_ref):
+            for m in range(ref.shape[0]):
+                rows = ref[m, :, head * HS : (head + 1) * HS]
+                piece_ref[head, :, place : place + HS] = rows.astype(bf16)
+                place += HS
+
+
+def cast_kernel(*refs):
+    kinds = (len(refs) - 1) // 3
+    for kind in range(kinds):
+        first, second = refs[kinds + 1 + 2 * kind : kinds + 3 + 2 * kind]
+        cut = first.shape[1]
+        first[...] = refs[kind][:, :cut].astype(bf16)
+        second[...] = refs[kind][:, cut:].astype(bf16)
+
+
+def join_kernel(piece_ref, *outs):
+    for head in range(piece_ref.shape[0]):
+        place = 0
+        for ref in outs:
+            for m in range(ref.shape[0]):
+                rows = piece_ref[head, :, place : place + HS]
+                ref[m, :, head * HS : (head + 1) * HS] = rows.astype(f32)
+                place += HS
+
+
+def after(value, *waited):
+    def body(*refs):
+        pass
+
+    anywhere = pl.BlockSpec(memory_space=pl.ANY)
+    return pl.pallas_call(
+        body,
+        in_specs=[anywhere] * (1 + len(waited)),
+        out_specs=anywhere,
+        out_shape=shape(value.shape, value.dtype),
+        input_output_aliases={0: 0},
+        cost_estimate=cost(1e6, 1e3),
+        name="after",
+    )(value, *waited)
+
+
 def params():
     return pltpu.CompilerParams(vmem_limit_bytes=VMEM)
 
 
 def cost(flops, nbytes):
     return pl.CostEstimate(flops=int(flops), bytes_accessed=int(nbytes), transcendentals=0)
+
+
+def wall():
+    return cost(2e11, 1e6)
 
 
 def shape(dims, dtype):
@@ -352,45 +419,67 @@
     total = rows * zs * ts
     wide_cols = dim + SIDE
 
-    def bring_rows(pieces):
-        got = [pieces(0)] + [None] * (zs - 1)
-        for k in (1, 3, 2):
-            got[k] = shift(pieces(k), "zz", k, zs)
-        part, width = got[0].shape
+    def exchange(value):
+        return lax.all_to_all(value, "zz", 0, 0, tiled=True)
+
+    def swap(half):
+        return shift(half, "xx", 1, 2) if xs == 2 else half
+
+    def assemble(halves, others, *ready):
+        chunks = len(halves)
+        part, width = halves[0].shape[1:]
         if xs == 2:
-            full = jnp.zeros((zs, xs, part, width), bf16)
-            for k in (0, 1, 3, 2):
-                source = (zz - k) % zs
-                full = lax.dynamic_update_slice(full, got[k][None, None], (source, xx, 0, 0))
-                other = shift(got[k], "xx", 1, 2)
-                full = lax.dynamic_update_slice(full, other[None, None], (source, 1 - xx, 0, 0))
+            full = jnp.zeros((zs, xs, chunks, part, width), bf16)
+            full = after(full, *ready) if ready else full
+            for n in range(chunks):
+                for piece, column in ((halves[n], xx), (others[n], 1 - xx)):
+                    full = lax.dynamic_update_slice(
+                        full, piece[:, None, None], (0, column, n, 0, 0)
+                    )
         else:
-            half = jnp.zeros((zs, part, width), bf16)
-            for k in range(zs):
-                half = lax.dynamic_update_slice(half, got[k][None], ((zz - k) % zs, 0, 0))
-            full = lax.all_gather(half, "xx", axis=1)
-        return full.reshape(zs * xs * part, width)
-
-    def return_rows(grad):
-        width = grad.shape[1]
-        grad = grad.reshape(zs, xs, -1, width)
-        part = grad.shape[2]
+            full = jnp.stack([lax.all_gather(h, "xx", axis=1) for h in halves], axis=2)
+        return full.reshape(zs * xs * chunks * part, width)
+
+    core, line = tt % 2, tt // 2
+    across_core = [(i, i ^ 1) for i in range(ts)]
+    across_line = [(i, i ^ 2) for i in range(ts)]
+
+    def gather_line(mine):
+        spread_rows = jnp.broadcast_to(mine[None], (zs,) + mine.shape)
+        by_zz = exchange(spread_rows)
+        return by_zz, lax.ppermute(by_zz, "tensor", across_line)
+
+    def gather_core(by_zz, other_line):
+        pair = jnp.zeros((zs, 2) + by_zz.shape[1:], by_zz.dtype)
+        for piece, place in ((by_zz, line), (other_line, 1 - line)):
+            pair = lax.dynamic_update_slice(pair, piece[:, None], (0, place, 0, 0))
+        other_core = lax.ppermute(pair, "tensor", across_core)
+        full = jnp.zeros((zs, 2, 2) + by_zz.shape[1:], by_zz.dtype)
+        for piece, place in ((pair, core), (other_core, 1 - core)):
+            full = lax.dynamic_update_slice(full, piece[:, :, None], (0, 0, place, 0, 0))
+        return full.reshape(-1, by_zz.shape[-1])
+
+    def fold(value, axis, place, pairs):
+        sent = lax.dynamic_index_in_dim(value, 1 - place, axis, keepdims=False)
+        kept = lax.dynamic_index_in_dim(value, place, axis, keepdims=False)
+        came = lax.ppermute(sent, "tensor", pairs)
+        return (kept.astype(f32) + came.astype(f32)).astype(bf16)
+
+    def return_x(grad, parts=1):
+        grad = grad.reshape(zs, xs, -1, grad.shape[1])
+        halves = [grad[i * zs // parts : (i + 1) * zs // parts] for i in range(parts)]
         if xs != 2:
-            summed = lax.psum_scatter(
-                grad.transpose(1, 0, 2, 3), "xx", scatter_dimension=0, tiled=False
-            )
-        out = [None] * zs
-        for k in (2, 1, 3, 0):
-            target = (zz + k) % zs
-            if xs == 2:
-                sent = lax.dynamic_slice(grad, (target, 1 - xx, 0, 0), (1, 1, part, width))
-                kept = lax.dynamic_slice(grad, (target, xx, 0, 0), (1, 1, part, width))
-                piece = kept.astype(f32) + shift(sent, "xx", 1, 2).astype(f32)
-                piece = piece.astype(bf16)[0, 0]
-            else:
-                piece = lax.dynamic_index_in_dim(summed, target, 0, keepdims=False)
-            out[k] = shift(piece, "zz", k, zs) if k else piece
-        return out
+            came = [
+                lax.psum_scatter(h.transpose(1, 0, 2, 3), "xx", scatter_dimension=0, tiled=False)
+                for h in halves
+            ]
+            return came, jnp.concatenate(came, axis=0)
+        came = [
+            shift(lax.dynamic_index_in_dim(h, 1 - xx, 1, keepdims=False), "xx", 1, 2)
+            for h in halves
+        ]
+        kept = lax.dynamic_index_in_dim(grad, xx, 1, keepdims=False)
+        return came, (kept.astype(f32) + jnp.concatenate(came, 0).astype(f32)).astype(bf16)
 
     packed = pl.pallas_call(
         pack_kernel,
@@ -408,13 +497,16 @@
         compiler_params=params(),
         name="pack",
     )(here, parents, tokens, att_route, ffn_route)
+
     group_tokens = lax.all_gather(packed, GROUP, axis=0, tiled=True)
-
     small = jnp.concatenate(
         [norm_gain1[None], norm_gain2[None], att_router.T, ffn_router.T], axis=0
     )
-    small = lax.all_gather(small.reshape(1, -1), ALL, axis=0, tiled=True)
-    small = small.reshape(-1, 2 + 2 * EXPERTS, norm_gain1.shape[0])
+    devices = zs * xs * ts
+    small = jnp.broadcast_to(small.reshape(1, -1), (devices, small.size))
+    small = after(small, packed)
+    small = lax.all_to_all(small, ALL, 0, 0, tiled=True)
+    small = small.reshape(devices, 2 + 2 * EXPERTS, norm_gain1.shape[0])
     small = small.transpose(1, 0, 2).reshape(2 + 2 * EXPERTS, dim)
     gain1, gain2 = small[0:1], small[1:2]
     router1 = jnp.pad(small[2 : 2 + EXPERTS], ((0, 8 - EXPERTS), (0, 0)))
@@ -422,23 +514,54 @@
     parts1 = router_parts(small[2 : 2 + EXPERTS].T)
     parts2 = router_parts(small[2 + EXPERTS :].T)
 
-    maps = jnp.concatenate([query_maps, kv_maps, out_maps], axis=0).astype(bf16)
-    count = maps.shape[0]
-    part = maps.shape[1]
-    by_head = maps.reshape(count, part, zs, HS).transpose(2, 1, 0, 3).reshape(zs, part, count * HS)
-    w_att = bring_rows(
-        lambda k: lax.dynamic_index_in_dim(by_head, (zz + k) % zs, 0, keepdims=False)
-    )
-
-    def expert_rows(kind):
-        def piece(k):
-            index = kind * EXPERTS + (zz + k) % zs
-            return lax.dynamic_index_in_dim(ffn_maps, index, 0, keepdims=False).astype(bf16)
-
-        return bring_rows(piece)
-
-    w_gate, w_up, w_down = expert_rows(0), expert_rows(1), expert_rows(2)
-    group_cot = lax.all_gather(cotangent, GROUP, axis=0, tiled=True)
+    count = query_maps.shape[0] + kv_maps.shape[0] + out_maps.shape[0]
+    part = query_maps.shape[1]
+    zz_one = jnp.stack([zz]).astype(jnp.int32)
+    vmem = pl.BlockSpec(memory_space=pltpu.VMEM)
+    anywhere = pl.BlockSpec(memory_space=pl.ANY)
+    by_head = pl.pallas_call(
+        split_kernel,
+        in_specs=[vmem, vmem, vmem, anywhere],
+        out_specs=vmem,
+        out_shape=shape((zs, part, count * HS), bf16),
+        compiler_params=params(),
+        name="split",
+    )(query_maps, kv_maps, out_maps, small)
+    att_half = exchange(by_head)
+    att_other = swap(att_half)
+    w_att = assemble([att_half], [att_other])
+
+    cut, width = part // 2, ffn_maps.shape[2]
+    cast = pl.pallas_call(
+        cast_kernel,
+        grid=(EXPERTS,),
+        in_specs=[
+            pl.BlockSpec((1, part, width), lambda i, kind=kind: (kind * EXPERTS + i, 0, 0))
+            for kind in range(3)
+        ]
+        + [anywhere],
+        out_specs=[pl.BlockSpec((1, cut, width), lambda i: (i, 0, 0))] * 6,
+        out_shape=[shape((EXPERTS, cut, width), bf16)] * 6,
+        compiler_params=params(),
+        cost_estimate=wall(),
+        name="cast",
+    )(ffn_maps, ffn_maps, ffn_maps, by_head)
+    chunks = []
+
+    def chunk(n, *ready):
+        value = exchange(after(cast[n], *ready))
+        chunks.append(value)
+        others.append(swap(value))
+
+    others = []
+    chunk(0, att_half)
+    chunk(1, chunks[0])
+    chunk(2, chunks[1], others[0])
+    cot_zz, cot_line = gather_line(after(cotangent, chunks[2]))
+    chunk(3, cot_zz, others[1])
+    chunk(4, chunks[3], others[2])
+    chunk(5, chunks[4], others[3])
+    w_gate, w_up = [assemble(chunks[n : n + 2], others[n : n + 2]) for n in (0, 2)]
 
     half = HS // 2
     frequency = rope_base ** (-2.0 * jnp.arange(half, dtype=f32) / HS)
@@ -461,51 +584,91 @@
             shape((total, SIDE), f32),
         ],
         compiler_params=params(),
-        cost_estimate=cost(2 * total * dim * 11 * HS, 6 * total * dim),
+        cost_estimate=wall(),
         name="att_fwd",
     )(group_tokens, w_att, parts1, gain1, cos, sin)
+    part_att = after(part_att, others[0], chunks[1])
     sum_att = lax.psum_scatter(part_att, GROUP, scatter_dimension=0, tiled=True)
 
+    waited = [cot_zz, others[1]]
     packed2, middle, gate2 = pl.pallas_call(
         mid_kernel,
+        in_specs=[vmem] * 4 + [pl.BlockSpec(memory_space=pl.ANY)] * len(waited),
         out_shape=[shape((rows, wide_cols), bf16), shape((rows, dim), f32), shape((rows, SIDE), f32)],
         compiler_params=params(),
+        cost_estimate=wall(),
         name="mid",
-    )(sum_att, packed, gain2, parts2)
+    )(sum_att, packed, gain2, parts2, *waited)
     x2 = lax.all_gather(packed2, GROUP, axis=0, tiled=True)
 
-    width = w_gate.shape[1]
-    step = 256
-    rows_of = lambda w: pl.BlockSpec((step, w), lambda i, s: (i, 0))
-    fixed = lambda: pl.BlockSpec(
-        (dim, width), lambda i, s: (0, 0), pipeline_mode=pl.Buffered(buffer_count=1)
-    )
-    back2, act, gate_grad, up_grad = pl.pallas_call(
-        ffn_kernel,
+    step = 512
+    steps = (total // step,)
+    rows_of = lambda w: pl.BlockSpec((step, w), lambda i, *s: (i, 0))
+    side_of = pl.BlockSpec((step, SIDE), lambda i, *s: (i, dim // SIDE))
+    fixed = pl.BlockSpec(
+        (dim, width), lambda i, *s: (0, 0), pipeline_mode=pl.Buffered(buffer_count=1)
+    )
+    gate_h, up_h, act = pl.pallas_call(
+        ffn_fwd_kernel,
         grid_spec=pltpu.PrefetchScalarGridSpec(
             num_scalar_prefetch=1,
-            grid=(total // step,),
-            in_specs=[rows_of(wide_cols), rows_of(dim), fixed(), fixed(), fixed()],
-            out_specs=[rows_of(wide_cols), rows_of(width), rows_of(width), rows_of(width)],
+            grid=steps,
+            in_specs=[rows_of(wide_cols), fixed, fixed],
+            out_specs=[rows_of(width)] * 3,
         ),
-        out_shape=[shape((total, wide_cols), bf16)] + [shape((total, width), bf16)] * 3,
-        compiler_params=params(),
-        cost_estimate=cost(2 * total * dim * 5 * width, 6 * dim * width + 12 * total * dim),
-        name="ffn",
-    )(jnp.stack([zz]).astype(jnp.int32), x2, group_cot, w_gate, w_up, w_down)
+        out_shape=[shape((total, width), bf16)] * 3,
+        compiler_params=params(),
+        cost_estimate=wall(),
+        name="ffn_fwd",
+    )(zz_one, x2, w_gate, w_up)
+    group_cot = gather_core(cot_zz, cot_line)
+    down_grad = dot_tn(group_cot, act).astype(bf16)
+    down_came, down_sum = return_x(down_grad, 2)
+    w_down = assemble(chunks[4:], others[4:], act)
+    gate_grad, up_grad, part2 = pl.pallas_call(
+        ffn_act_kernel,
+        grid_spec=pltpu.PrefetchScalarGridSpec(
+            num_scalar_prefetch=1,
+            grid=steps,
+            in_specs=[
+                side_of, rows_of(width), rows_of(width), rows_of(dim), fixed, anywhere
+            ],
+            out_specs=[rows_of(width)] * 2 + [rows_of(SIDE)],
+        ),
+        out_shape=[shape((total, width), bf16)] * 2 + [shape((total, SIDE), bf16)],
+        compiler_params=params(),
+        cost_estimate=wall(),
+        name="ffn_act",
+    )(zz_one, x2, gate_h, up_h, group_cot, w_down, down_grad)
+    back2 = pl.pallas_call(
+        ffn_back_kernel,
+        grid=steps,
+        in_specs=[rows_of(width), rows_of(width), rows_of(SIDE), fixed, fixed, anywhere],
+        out_specs=rows_of(wide_cols),
+        out_shape=shape((total, wide_cols), bf16),
+        compiler_params=params(),
+        cost_estimate=wall(),
+        name="ffn_back",
+    )(gate_grad, up_grad, part2, w_gate, w_up, down_came[0])
     sum_back2 = lax.psum_scatter(back2, GROUP, scatter_dimension=0, tiled=True)
 
-    part_ffn = dot_nt(act, w_down).astype(bf16)
-    mixed = (
-        middle + lax.psum_scatter(part_ffn, GROUP, scatter_dimension=0, tiled=True).astype(f32)
-    ).astype(bf16)
-
-    def norm_back(route_at, rsb, wide_rows, base, gain, router, gate, gate_at, outs, name):
+    x2_low = x2[:, :dim]
+    gate_dw = dot_tn(x2_low, after(gate_grad, down_sum, back2)).astype(bf16)
+    up_dw = dot_tn(x2_low, after(up_grad, gate_dw)).astype(bf16)
+    gate_came, gate_sum = return_x(gate_dw)
+    up_came, up_sum = return_x(up_dw)
+    down_back = exchange(down_sum)
+    gate_back = exchange(after(gate_sum, down_back))
+    up_back = exchange(after(up_sum, gate_back))
+    part_ffn = dot_nt(after(act, up_dw), w_down).astype(bf16)
+    by_core = fold(part_ffn.reshape(zs, 2, 2, rows, dim), 2, core, across_core)
+
+    def norm_back(route_at, rsb, wide_rows, base, gain, router, gate, gate_at, outs, name, *waited):
         def pick(a):
             return pl.BlockSpec(a.shape, lambda i, w: (0,) * a.ndim)
 
         return pl.pallas_call(
-            functools.partial(norm_back_kernel, route_at),
+            functools.partial(norm_back_kernel, route_at, 1 + len(outs)),
             grid_spec=pltpu.PrefetchScalarGridSpec(
                 num_scalar_prefetch=1,
                 grid=(1,),
@@ -513,30 +676,25 @@
                     pick(rsb), pl.BlockSpec((rows, dim), lambda i, w: (0, 0)), pick(base), pick(gain), pick(router),
                     pl.BlockSpec((rows, SIDE), lambda i, w: (w[0], 0)),
                     pl.BlockSpec((rows, SIDE), lambda i, w: (0, dim // SIDE)),
-                ],
+                ]
+                + [anywhere] * len(waited),
                 out_specs=[pl.BlockSpec((8, dim), lambda i, w: (0, 0))]
                 + [pl.BlockSpec((rows, dim), lambda i, w: (0, 0)) for _ in outs],
             ),
             out_shape=[shape((8, dim), f32)] + [shape((rows, dim), d) for d in outs],
             compiler_params=params(),
+            cost_estimate=wall(),
             name=name,
-        )(gate_at, rsb, wide_rows, base, gain, router, gate, packed)
+        )(gate_at, rsb, wide_rows, base, gain, router, gate, packed, *waited)
 
     zero = jnp.zeros((1,), jnp.int32)
     parts_ffn, middle_grad, att_cot = norm_back(
-        7, sum_back2, middle, cotangent, gain2, router2, gate2, zero, [f32, bf16], "mid_back"
+        7, sum_back2, middle, cotangent, gain2, router2, gate2, zero, [f32, bf16], "mid_back",
+        down_back, gate_sum, part_ffn,
     )
     group_att_cot = lax.all_gather(att_cot, GROUP, axis=0, tiled=True)
 
-    x2_low = x2[:, :dim]
-    ffn_out = jnp.zeros(ffn_maps.shape, f32)
-    for kind, grad in (
-        (2, dot_tn(group_cot, act)), (0, dot_tn(x2_low, gate_grad)), (1, dot_tn(x2_low, up_grad))
-    ):
-        for k, piece in enumerate(return_rows(grad.astype(bf16))):
-            index = kind * EXPERTS + (zz - k) % zs
-            ffn_out = lax.dynamic_update_slice(ffn_out, piece.astype(f32)[None], (index, 0, 0))
-
+    group_att_cot = after(group_att_cot, gate_back, up_sum, by_core)
     back1, grad_qkv, z = pl.pallas_call(
         att_bwd_kernel,
         grid=(trees,),
@@ -550,7 +708,7 @@
             shape((total, EXPERTS * HS), bf16),
         ],
         compiler_params=params(),
-        cost_estimate=cost(2 * total * dim * 11 * HS, 6 * total * dim),
+        cost_estimate=wall(),
         name="att_bwd",
     )(group_att_cot, w_att, kept, gate1, group_tokens, cos, sin)
     sum_back1 = lax.psum_scatter(back1, GROUP, scatter_dimension=0, tiled=True)
@@ -558,39 +716,42 @@
     grad_att = jnp.concatenate(
         [dot_tn(x1, grad_qkv).astype(bf16), dot_tn(group_att_cot, z).astype(bf16)], axis=1
     )
-    gathered = jnp.zeros((zs, part, count * HS), bf16)
-    for k, piece in enumerate(return_rows(grad_att)):
-        gathered = lax.dynamic_update_slice(gathered, piece[None], ((zz - k) % zs, 0, 0))
-    maps_grad = (
-        gathered.reshape(zs, part, count, HS).transpose(2, 1, 0, 3).reshape(maps.shape).astype(f32)
-    )
+    by_line = fold(after(by_core, grad_att), 1, line, across_line)
+    att_sum = return_x(grad_att)[1]
+    att_back = exchange(after(att_sum, up_back))
+    mixed_zz = exchange(after(by_line, up_back, att_sum))
+    query_grad, kv_grad, out_grad = pl.pallas_call(
+        join_kernel,
+        in_specs=[vmem],
+        out_specs=[vmem] * 3,
+        out_shape=[shape(a.shape, f32) for a in (query_maps, kv_maps, out_maps)],
+        compiler_params=params(),
+        name="join",
+    )(att_back)
+    ffn_out = jnp.concatenate([v.astype(f32) for v in (gate_back, up_back, down_back)], axis=0)
+
+    mixed = (middle + jnp.sum(mixed_zz.astype(f32), axis=0)).astype(bf16)
 
     parts_att, input_grad = norm_back(
         0, sum_back1, tokens, middle_grad, gain1, router1, gate1,
         (zz * ts + tt)[None].astype(jnp.int32), [bf16], "input_back",
     )
 
-    def small_sum(parts):
-        parts = parts.reshape(8, zs * xs * ts, -1).transpose(1, 0, 2)
-        devices = parts.shape[0]
-        summed = lax.psum_scatter(
-            parts.reshape(devices, -1), ALL, scatter_dimension=0, tiled=True
-        ).reshape(8, -1)
-        return summed[EXPERTS], summed[:EXPERTS].T
-
-    gain2_grad, ffn_router_grad = small_sum(parts_ffn)
-    gain1_grad, att_router_grad = small_sum(parts_att)
-    queries = query_maps.shape[0]
-    keys = kv_maps.shape[0]
+    used = EXPERTS + 1
+    parts = jnp.concatenate([parts_ffn[:used], parts_att[:used]], axis=0)
+    parts = parts.reshape(2 * used, devices, -1).transpose(1, 0, 2).reshape(devices, -1)
+    parts = jnp.sum(lax.all_to_all(parts, ALL, 0, 0, tiled=True), axis=0).reshape(2, used, -1)
+    ffn_router_grad, gain2_grad = parts[0, :EXPERTS].T, parts[0, EXPERTS]
+    att_router_grad, gain1_grad = parts[1, :EXPERTS].T, parts[1, EXPERTS]
     return (
         mixed,
         input_grad,
         gain1_grad,
         gain2_grad,
         att_router_grad,
-        maps_grad[:queries],
-        maps_grad[queries : queries + keys],
-        maps_grad[queries + keys :],
+        query_grad,
+        kv_grad,
+        out_grad,
         ffn_router_grad,
         ffn_out,
     )

time: 1600 us -> 1250 us (0.78)
  waiting for transfers between devices: 866 us -> 687 us
  starting transfers between devices: 211 us -> 79.9 us
  blocking collectives: 101 us -> 14.7 us
  Pallas kernels: 150 us -> 193 us
    all_to_all x0 -> x14, waiting for transfers between devices: none -> 412 us  [the longest x13 410 us: exchange(): return lax.all_to_all(value, 'zz', 0, 0, tiled=True)]
    ppermute x56 -> x12, waiting for transfers between devices: 508 us -> 159 us  [shift(): lax.ppermute(value, axis, [(i, (i + step) % size) for i in range(size)])]
    ppermute x56 -> x12, starting transfers between devices: 210 us -> 14.7 us  [shift(): lax.ppermute(value, axis, [(i, (i + step) % size) for i in range(size)])]
    unnamed x10 -> x6, waiting for transfers between devices: 131 us -> 0.76 us
    reduce_scatter x1, waiting for transfers between devices: 122 us -> 0.01 us  [local(): sum_back2 = lax.psum_scatter(back2, GROUP, scatter_dimension=0, tiled=True)]
    all_gather x1 -> x0, blocking collectives: 101 us -> none  [local(): small = lax.all_gather(small.reshape(1, -1), ALL, axis=0, tiled=True)]
    ppermute x0 -> x4, waiting for transfers between devices: none -> 91.9 us  [the longest x2 54.2 us: fold(): came = lax.ppermute(sent, 'tensor', pairs)]
    reduce_scatter x1, waiting for transfers between devices: 105 us -> 20 us  [local(): sum_att = lax.psum_scatter(part_att, GROUP, scatter_dimension=0, tiled=True)]
  transfers between devices with their start and end apart: 65 -> 36, of which waited for: 31 -> 23; matrix products, arithmetic and copies ran while one was open for 15% -> 19% of each run, Pallas kernels for 2% -> 8%
where the time goes in v2:
time: 1250 us; the launch traced here: 1240 us
  waiting for transfers between devices  687 us (55%)
  Pallas kernels  193 us (15%)
  local copies, waits for them, and re-layouts  117 us (9%)
  matrix products  91.7 us (7%)
  starting transfers between devices  79.9 us (6%)
  other arithmetic  46.1 us (4%)
  between operations  14.8 us (1%)
  blocking collectives  14.7 us (1%)
    all_to_all x13, waiting for transfers between devices, exchange(): return lax.all_to_all(value, 'zz', 0, 0, tiled=True)  410 us
    ppermute x12, waiting for transfers between devices, shift(): lax.ppermute(value, axis, [(i, (i + step) % size) for i in range(size)])  159 us
    dot_general x5, matrix products, dot_tn(): lax.dot_general(a, b, (((0,), (0,)), ((), ())), preferred_element_type=f32)  72.8 us
    all_to_all x13, starting transfers between devices, exchange(): return lax.all_to_all(value, 'zz', 0, 0, tiled=True)  58 us
    ppermute x2, waiting for transfers between devices, fold(): came = lax.ppermute(sent, 'tensor', pairs)  54.2 us
    pallas_call x1, Pallas kernels, local(): pl.pallas_call(ffn_back_kernel, grid=steps, in_specs=[rows_of(width), row...  44.6 us
    ppermute x1, waiting for transfers between devices, gather_line(): return (by_zz, lax.ppermute(by_zz, 'tensor', across_line))  37.7 us
    dynamic_update_slice x14, local copies, waits for them, and re-layouts, assemble(): lax.dynamic_update_slice(full, piece[:, None, None], (0, column, n, 0, 0))  34 us
  transfers between devices with their start and end apart: 36, of which 23 were waited for; matrix products, arithmetic and copies ran while one was open for 19% of the time, Pallas kernels for 8%

profile of v2, /device:TPU:0, one launch (start us, length us, event | category | flops | bytes accessed | tf_op | source)
XLA Modules:
  0.0 1244.1 jit_solution(8688067052061071914)
XLA Ops:
  15.3 14.7 %all_to_all.84 = f32[32,1,640]{2,1,0:T(1,128)S(1)} all-to-all(f32[32,1,640]{2,1,0:T(1,128)S(1)} %copy.102), channel_id=1, replica_groups=mesh['zz'=4,'xx'=2,'tensor'=4] {'zz','xx','tensor'}, dimensions={0} | all-to-all | bytes 163840 | tf_op jit(solution)/shard_map/all_to_all | solution.py:508
  41.2 77.3 %all-to-all-done.1.refs_1_ = bf16[4,256,1280]{2,1,0:T(8,128)(2,1)} async-done(((bf16[4,256,1280]{2,1,0:T(8,128)(2,1)}), bf16[4,256,1280]{2,1,0:T(8,128)(2,1)}, u32[]{:S(2)}, u32[]{:S(2)}) %all-to-all-start.1) | async-done | bytes 2621472 | tf_op jit(solution)/shard_map/all_to_all | solution.py:423
  118.9 9.3 cast.1
  144.6 40.7 %all-to-all-done.2.refs_1_ = bf16[4,128,1408]{2,1,0:T(8,128)(2,1)S(1)} async-done(((bf16[4,128,1408]{2,1,0:T(8,128)(2,1)}), bf16[4,128,1408]{2,1,0:T(8,128)(2,1)S(1)}, u32[]{:S(2)}, u32[]{:S(2)}) %all-to-all-start.2) | async-done | bytes 1441824 | tf_op jit(solution)/shard_map/all_to_all | solution.py:423
  195.7 29.1 %att_fwd.1 = (bf16[2048,2048]{1,0:T(8,128)(2,1)}, bf16[2048,2048]{1,0:T(8,128)(2,1)}, bf16[2048,768]{1,0:T(8,128)(2,1)}, f32[2048,128]{1,0:T(8,128)}) custom-call(bf16[2048,2176]{1,0:T(8,128)(2,1)} %all-gather.4.cloned.1.call-done.tok_ref.side_ref, bf16[2048,1280]{1,0:T(8,128)(2,1)} %bitcast.11.w_ref, bf16[2048,128]{1,0:T(8,128)(2,1)} %pad.16.clone.router_ref, ...), custom_call_target="tpu_custom_call" | custom-call | flops 199999995904 | bytes 1000000 | tf_op jit(solution)/shard_map/att_fwd/pallas_call | solution.py:575
  230.7 44.2 %all-to-all-done.4.refs_1_ = bf16[4,128,1408]{2,1,0:T(8,128)(2,1)S(1)} async-done(((bf16[4,128,1408]{2,1,0:T(8,128)(2,1)}), bf16[4,128,1408]{2,1,0:T(8,128)(2,1)S(1)}, u32[]{:S(2)}, u32[]{:S(2)}) %all-to-all-start.4) | async-done | bytes 1441824 | tf_op jit(solution)/shard_map/all_to_all | solution.py:423
  293.4 17.0 %collective-permute-done.2.refs_1_.refs_2_ = bf16[4,128,1408]{2,1,0:T(8,128)(2,1)S(1)} collective-permute-done((bf16[4,128,1408]{2,1,0:T(8,128)(2,1)}, bf16[4,128,1408]{2,1,0:T(8,128)(2,1)S(1)}, u32[]{:S(2)}, u32[]{:S(2)}) %collective-permute-start.2) | collective-permute-done | bytes 1441824 | tf_op jit(solution)/shard_map/ppermute | solution.py:407
  310.4 31.8 %all-to-all-done.5.refs_0_.refs_1_ = bf16[4,128,2048]{2,1,0:T(8,128)(2,1)S(1)} async-done(((bf16[4,128,2048]{2,1,0:T(8,128)(2,1)}), bf16[4,128,2048]{2,1,0:T(8,128)(2,1)S(1)}, u32[]{:S(2)}, u32[]{:S(2)}) %all-to-all-start.5) | async-done | bytes 2097184 | tf_op jit(solution)/shard_map/all_to_all | solution.py:423
  342.2 20.0 %reduce-scatter.4.cloned.1.call-done.rs_ref = bf16[128,2048]{1,0:T(8,128)(2,1)} async-done(((bf16[2048,2048]{1,0:T(8,128)(2,1)}), bf16[128,2048]{1,0:T(8,128)(2,1)}) %reduce-scatter.4.cloned.1.call-update) | async-done | bytes 524304 | tf_op jit(solution)/shard_map/reduce_scatter | solution.py:591
  381.3 37.7 %collective-permute-done.5 = bf16[4,128,2048]{2,1,0:T(8,128)(2,1)} collective-permute-done((bf16[4,128,2048]{2,1,0:T(8,128)(2,1)}, bf16[4,128,2048]{2,1,0:T(8,128)(2,1)}, u32[]{:S(2)}, u32[]{:S(2)}) %collective-permute-start.5) | collective-permute-done | bytes 2097184 | tf_op jit(solution)/shard_map/ppermute | solution.py:450
  441.8 24.6 %collective-permute-done.4.refs_2_ = bf16[4,128,1408]{2,1,0:T(8,128)(2,1)} collective-permute-done((bf16[4,128,1408]{2,1,0:T(8,128)(2,1)}, bf16[4,128,1408]{2,1,0:T(8,128)(2,1)}, u32[]{:S(2)}, u32[]{:S(2)}) %collective-permute-start.4) | collective-permute-done | bytes 1441824 | tf_op jit(solution)/shard_map/ppermute | solution.py:407
  466.4 28.1 %all-to-all-done.7.refs_1_ = bf16[4,128,1408]{2,1,0:T(8,128)(2,1)} async-done(((bf16[4,128,1408]{2,1,0:T(8,128)(2,1)}), bf16[4,128,1408]{2,1,0:T(8,128)(2,1)}, u32[]{:S(2)}, u32[]{:S(2)}) %all-to-all-start.7) | async-done | bytes 1441824 | tf_op jit(solution)/shard_map/all_to_all | solution.py:423
  519.5 13.9 %all-to-all-done.8 = bf16[4,128,1408]{2,1,0:T(8,128)(2,1)} async-done(((bf16[4,128,1408]{2,1,0:T(8,128)(2,1)}), bf16[4,128,1408]{2,1,0:T(8,128)(2,1)}, u32[]{:S(2)}, u32[]{:S(2)}) %all-to-all-start.8) | async-done | bytes 1441824 | tf_op jit(solution)/shard_map/all_to_all | solution.py:423
  534.8 33.4 %ffn_fwd.1 = (bf16[2048,1408]{1,0:T(8,128)(2,1)}, bf16[2048,1408]{1,0:T(8,128)(2,1)}, bf16[2048,1408]{1,0:T(8,128)(2,1)}) custom-call(s32[1]{0:T(128)} %bitcast.14.where_ref, bf16[2048,2176]{1,0:T(8,128)(2,1)} %all-gather.6.cloned.1.call-done.x_ref.side_ref, bf16[2048,1408]{1,0:T(8,128)(2,1)} %bitcast.21.wg_ref, bf16[2048,1408]{1,0:T(8,128)(2,1)} %bitcast.30.wu_ref), custom_call_target="tpu_custom_call" | custom-call | flops 199999995904 | bytes 1000000 | tf_op jit(solution)/shard_map/ffn_fwd/pallas_call | solution.py:611
  568.3 17.2 %convolution_convert_fusion.3.wait_ref = bf16[2048,1408]{1,0:T(8,128)(2,1)S(1)} fusion(bf16[2048,2048]{1,0:T(8,128)(2,1)} %bitcast.38.c_ref, bf16[2048,1408]{1,0:T(8,128)(2,1)} %get-tuple-element.47.refs_1_.refs_0_), kind=kOutput, calls=%fused_computation.6 | convolution fusion | flops 11814043648 | bytes 19922944 | tf_op jit(solution)/shard_map/dot_general | solution.py:32
  604.0 24.3 %ffn_act.1 = (bf16[2048,1408]{1,0:T(8,128)(2,1)}, bf16[2048,1408]{1,0:T(8,128)(2,1)}, bf16[2048,128]{1,0:T(8,128)(2,1)}) custom-call(s32[1]{0:T(128)} %bitcast.14.where_ref, bf16[2048,2176]{1,0:T(8,128)(2,1)} %all-gather.6.cloned.1.call-done.x_ref.side_ref, bf16[2048,1408]{1,0:T(8,128)(2,1)} %get-tuple-element.48.gate_ref, ...), custom_call_target="tpu_custom_call" | custom-call | flops 199999995904 | bytes 1000000 | tf_op jit(solution)/shard_map/ffn_act/pallas_call | solution.py:628
  628.3 44.6 %ffn_back.1.refs_2_ = bf16[2048,2176]{1,0:T(8,128)(2,1)} custom-call(bf16[2048,1408]{1,0:T(8,128)(2,1)} %get-tuple-element.53.gg_ref.refs_0_, bf16[2048,1408]{1,0:T(8,128)(2,1)} %get-tuple-element.52.ug_ref.refs_0_, bf16[2048,128]{1,0:T(8,128)(2,1)} %get-tuple-element.54.part_ref, bf16[2048,1408]{1,0:T(8,128)(2,1)} %bitcast.21.wg_ref, ...), custom_call_target="tpu_custom_call" | custom-call | flops 199999995904 | bytes 1000000 | tf_op jit(solution)/shard_map/ffn_back/pallas_call | solution.py:643
  677.0 30.0 %collective-permute-done.10 = bf16[2,256,1408]{2,1,0:T(8,128)(2,1)S(1)} collective-permute-done((bf16[2,256,1408]{2,1,0:T(8,128)(2,1)S(1)}, bf16[2,256,1408]{2,1,0:T(8,128)(2,1)S(1)}, u32[]{:S(2)}, u32[]{:S(2)}) %collective-permute-start.10) | collective-permute-done | bytes 1441824 | tf_op jit(solution)/shard_map/ppermute | solution.py:407
  715.1 17.2 %convolution_convert_fusion.2.refs_1_ = bf16[2048,1408]{1,0:T(8,128)(2,1)S(1)} fusion(bf16[2048,1408]{1,0:T(8,128)(2,1)} %after.29, bf16[2048,2176]{1,0:T(8,128)(2,1)} %all-gather.6.cloned.1.call-done.x_ref.side_ref), kind=kOutput, calls=%fused_computation.5 | convolution fusion | flops 11814043648 | bytes 19922944 | tf_op jit(solution)/shard_map/dot_general | solution.py:32
  738.2 19.0 %convolution_convert_fusion.1.refs_1_ = bf16[2048,1408]{1,0:T(8,128)(2,1)} fusion(bf16[2048,1408]{1,0:T(8,128)(2,1)} %after.30, bf16[2048,2176]{1,0:T(8,128)(2,1)} %all-gather.6.cloned.1.call-done.x_ref.side_ref), kind=kOutput, calls=%fused_computation.4 | convolution fusion | flops 11814043648 | bytes 19922944 | tf_op jit(solution)/shard_map/dot_general | solution.py:32
  757.2 18.9 %convolution_convert_fusion.refs_2_ = bf16[2048,2048]{1,0:T(8,128)(2,1)} fusion(bf16[2048,1408]{1,0:T(8,128)(2,1)} %after.31, bf16[2048,1408]{1,0:T(8,128)(2,1)} %bitcast.185), kind=kOutput, calls=%fused_computation.3 | convolution fusion | flops 11815354368 | bytes 19922944 | tf_op jit(solution)/shard_map/dot_general | solution.py:28
  776.1 23.1 %collective-permute-done.12 = bf16[4,256,1408]{2,1,0:T(8,128)(2,1)} collective-permute-done((bf16[4,256,1408]{2,1,0:T(8,128)(2,1)}, bf16[4,256,1408]{2,1,0:T(8,128)(2,1)}, u32[]{:S(2)}, u32[]{:S(2)}) %collective-permute-start.12) | collective-permute-done | bytes 2883616 | tf_op jit(solution)/shard_map/ppermute | solution.py:407
  804.2 18.4 %all-to-all-done.9.refs_0_.refs_1_ = bf16[4,256,1408]{2,1,0:T(8,128)(2,1)S(1)} async-done(((bf16[4,256,1408]{2,1,0:T(8,128)(2,1)}), bf16[4,256,1408]{2,1,0:T(8,128)(2,1)S(1)}, u32[]{:S(2)}, u32[]{:S(2)}) %all-to-all-start.9) | async-done | bytes 2883616 | tf_op jit(solution)/shard_map/all_to_all | solution.py:423
  840.8 63.4 %collective-permute-done.13 = bf16[4,256,1408]{2,1,0:T(8,128)(2,1)S(1)} collective-permute-done((bf16[4,256,1408]{2,1,0:T(8,128)(2,1)S(1)}, bf16[4,256,1408]{2,1,0:T(8,128)(2,1)S(1)}, u32[]{:S(2)}, u32[]{:S(2)}) %collective-permute-start.13) | collective-permute-done | bytes 2883616 | tf_op jit(solution)/shard_map/ppermute | solution.py:407
  916.1 35.4 %all-to-all-done.10.refs_1_ = bf16[4,256,1408]{2,1,0:T(8,128)(2,1)S(1)} async-done(((bf16[4,256,1408]{2,1,0:T(8,128)(2,1)}), bf16[4,256,1408]{2,1,0:T(8,128)(2,1)S(1)}, u32[]{:S(2)}, u32[]{:S(2)}) %all-to-all-start.10) | async-done | bytes 2883616 | tf_op jit(solution)/shard_map/all_to_all | solution.py:423
  954.4 29.4 %att_bwd.1 = (bf16[2048,2176]{1,0:T(8,128)(2,1)}, bf16[2048,768]{1,0:T(8,128)(2,1)}, bf16[2048,512]{1,0:T(8,128)(2,1)}) custom-call(bf16[2048,2048]{1,0:T(8,128)(2,1)} %after.33.c_ref, bf16[2048,1280]{1,0:T(8,128)(2,1)} %bitcast.11.w_ref, bf16[2048,768]{1,0:T(8,128)(2,1)} %get-tuple-element.58.keep_ref, f32[2048,128]{1,0:T(8,128)} %get-tuple-element.59.gate_ref, ...), custom_call_target="tpu_custom_call" | custom-call | flops 199999995904 | bytes 1000000 | tf_op jit(solution)/shard_map/att_bwd/pallas_call | solution.py:698
  988.8 9.5 convolution_convert_fusion.5
  998.3 9.9 convolution_convert_fusion.4
  1018.5 54.2 %collective-permute-done.14 = bf16[4,128,2048]{2,1,0:T(8,128)(2,1)S(1)} collective-permute-done((bf16[4,128,2048]{2,1,0:T(8,128)(2,1)S(1)}, bf16[4,128,2048]{2,1,0:T(8,128)(2,1)S(1)}, u32[]{:S(2)}, u32[]{:S(2)}) %collective-permute-start.14) | collective-permute-done | bytes 2097184 | tf_op jit(solution)/shard_map/ppermute | solution.py:465
  1077.9 12.5 %all-to-all-done.11.refs_1_ = bf16[4,256,1408]{2,1,0:T(8,128)(2,1)} async-done(((bf16[4,256,1408]{2,1,0:T(8,128)(2,1)}), bf16[4,256,1408]{2,1,0:T(8,128)(2,1)}, u32[]{:S(2)}, u32[]{:S(2)}) %all-to-all-start.11) | async-done | bytes 2883616 | tf_op jit(solution)/shard_map/all_to_all | solution.py:423
  1104.1 56.9 %all-to-all-done.12 = bf16[4,128,2048]{2,1,0:T(8,128)(2,1)} async-done(((bf16[4,128,2048]{2,1,0:T(8,128)(2,1)}), bf16[4,128,2048]{2,1,0:T(8,128)(2,1)}, u32[]{:S(2)}, u32[]{:S(2)}) %all-to-all-start.12) | async-done | bytes 2097184 | tf_op jit(solution)/shard_map/all_to_all | solution.py:423
  1174.6 50.0 %all-to-all-done.14.piece_ref = bf16[4,256,1280]{2,1,0:T(8,128)(2,1)} async-done(((bf16[4,256,1280]{2,1,0:T(8,128)(2,1)}), bf16[4,256,1280]{2,1,0:T(8,128)(2,1)}, u32[]{:S(2)}, u32[]{:S(2)}) %all-to-all-start.14) | async-done | bytes 2621472 | tf_op jit(solution)/shard_map/all_to_all | solution.py:423
  (226 shorter events, 273.7 us)
Async XLA Ops:
  35.8 82.6 %all-to-all-start.1 = ((bf16[4,256,1280]{2,1,0:T(8,128)(2,1)}), bf16[4,256,1280]{2,1,0:T(8,128)(2,1)}, u32[]{:S(2)}, u32[]{:S(2)}) async-start(bf16[4,256,1280]{2,1,0:T(8,128)(2,1)} %split.1.refs_3_), calls=%async_computation.1 | async-start | bytes 5242880 | tf_op jit(solution)/shard_map/all_to_all | solution.py:423
  40.4 155.2 %all-gather.4.cloned.1.call-start = ((), (), s32[]{:S(2)}) async-start(), calls=%async_computation.18 | async-start | bytes 9469952 | tf_op jit(solution)/shard_map/all_gather | solution.py:501
  118.5 73.8 %collective-permute-start = (bf16[4,256,1280]{2,1,0:T(8,128)(2,1)}, bf16[4,256,1280]{2,1,0:T(8,128)(2,1)}, u32[]{:S(2)}, u32[]{:S(2)}) collective-permute-start(bf16[4,256,1280]{2,1,0:T(8,128)(2,1)} %all-to-all-done.1.refs_1_), channel_id=1, source_target_pairs={{0,4},{4,0},{1,5},{5,1},{2,6},{6,2},{3,7},{7,3},{8,12},{12,8},{9,1... | collective-permute-start | bytes 7864328 | tf_op jit(solution)/shard_map/ppermute | solution.py:407
  128.2 57.0 %all-to-all-start.2 = ((bf16[4,128,1408]{2,1,0:T(8,128)(2,1)}), bf16[4,128,1408]{2,1,0:T(8,128)(2,1)S(1)}, u32[]{:S(2)}, u32[]{:S(2)}) async-start(bf16[4,128,1408]{2,1,0:T(8,128)(2,1)} %after.20), calls=%async_computation.2 | async-start | bytes 2883584 | tf_op jit(solution)/shard_map/all_to_all | solution.py:423
  186.3 38.9 %all-to-all-start.3 = ((bf16[4,128,1408]{2,1,0:T(8,128)(2,1)}), bf16[4,128,1408]{2,1,0:T(8,128)(2,1)}, u32[]{:S(2)}, u32[]{:S(2)}) async-start(bf16[4,128,1408]{2,1,0:T(8,128)(2,1)} %after.21), calls=%async_computation.3 | async-start | bytes 2883584 | tf_op jit(solution)/shard_map/all_to_all | solution.py:423
  190.7 171.5 %reduce-scatter.4.cloned.1.call-start = ((), (), s32[]{:S(2)}) async-start(), calls=%async_computation.19 | async-start | bytes 8912896 | tf_op jit(solution)/shard_map/reduce_scatter | solution.py:591
  225.3 49.7 %all-to-all-start.4 = ((bf16[4,128,1408]{2,1,0:T(8,128)(2,1)}), bf16[4,128,1408]{2,1,0:T(8,128)(2,1)S(1)}, u32[]{:S(2)}, u32[]{:S(2)}) async-start(bf16[4,128,1408]{2,1,0:T(8,128)(2,1)} %after.23), calls=%async_computation.5 | async-start | bytes 2883584 | tf_op jit(solution)/shard_map/all_to_all | solution.py:423
  278.7 63.6 %all-to-all-start.5 = ((bf16[4,128,2048]{2,1,0:T(8,128)(2,1)}), bf16[4,128,2048]{2,1,0:T(8,128)(2,1)S(1)}, u32[]{:S(2)}, u32[]{:S(2)}) async-start(bf16[4,128,2048]{2,1,0:T(8,128)(2,1)} %broadcast_in_dim.94), calls=%async_computation.6 | async-start | bytes 4194304 | tf_op jit(solution)/shard_map/all_to_all | solution.py:423
  284.1 250.7 %all-gather.6.cloned.1.call-start = ((), (), s32[]{:S(2)}) async-start(), calls=%async_computation.20 | async-start | bytes 9469952 | tf_op jit(solution)/shard_map/all_gather | solution.py:602
  365.3 53.8 %collective-permute-start.5 = (bf16[4,128,2048]{2,1,0:T(8,128)(2,1)}, bf16[4,128,2048]{2,1,0:T(8,128)(2,1)}, u32[]{:S(2)}, u32[]{:S(2)}) collective-permute-start(bf16[4,128,2048]{2,1,0:T(8,128)(2,1)} %copy-done.5), channel_id=1, source_target_pairs={{0,2},{1,3},{2,0},{3,1},{4,6},{5,7},{6,4},{7,5},{8,10},{9,11},{10,... | collective-permute-start | bytes 6291464 | tf_op jit(solution)/shard_map/ppermute | solution.py:450
  366.8 57.9 %all-to-all-start.6 = ((bf16[4,128,1408]{2,1,0:T(8,128)(2,1)}), bf16[4,128,1408]{2,1,0:T(8,128)(2,1)}, u32[]{:S(2)}, u32[]{:S(2)}) async-start(bf16[4,128,1408]{2,1,0:T(8,128)(2,1)} %after.25), calls=%async_computation.7 | async-start | bytes 2883584 | tf_op jit(solution)/shard_map/all_to_all | solution.py:423
  375.7 49.1 %collective-permute-start.3 = (bf16[4,128,1408]{2,1,0:T(8,128)(2,1)S(1)}, bf16[4,128,1408]{2,1,0:T(8,128)(2,1)}, u32[]{:S(2)}, u32[]{:S(2)}) collective-permute-start(bf16[4,128,1408]{2,1,0:T(8,128)(2,1)S(1)} %copy-done.11), channel_id=1, source_target_pairs={{0,4},{4,0},{1,5},{5,1},{2,6},{6,2},{3,7},{7,3},{8,12},{12,8},{9,1... | collective-permute-start | bytes 4325384 | tf_op jit(solution)/shard_map/ppermute | solution.py:407
  422.2 92.5 %collective-permute-start.6 = (bf16[4,2,128,2048]{3,2,1,0:T(8,128)(2,1)}, bf16[4,2,128,2048]{3,2,1,0:T(8,128)(2,1)}, u32[]{:S(2)}, u32[]{:S(2)}) collective-permute-start(bf16[4,2,128,2048]{3,2,1,0:T(8,128)(2,1)} %bitcast_dynamic-update-slice_fusion.4), channel_id=1, source_target_pairs={{0,1},{1,0},{2,3},{3,2},{4,5},{5,4},{6,7},{7,6},{8,9},{9,8},{10,11... | collective-permute-start | bytes 12582920 | tf_op jit(solution)/shard_map/ppermute | solution.py:456
  424.8 69.6 %all-to-all-start.7 = ((bf16[4,128,1408]{2,1,0:T(8,128)(2,1)}), bf16[4,128,1408]{2,1,0:T(8,128)(2,1)}, u32[]{:S(2)}, u32[]{:S(2)}) async-start(bf16[4,128,1408]{2,1,0:T(8,128)(2,1)} %after.27), calls=%async_computation.8 | async-start | bytes 2883584 | tf_op jit(solution)/shard_map/all_to_all | solution.py:423
  432.1 34.3 %collective-permute-start.4 = (bf16[4,128,1408]{2,1,0:T(8,128)(2,1)}, bf16[4,128,1408]{2,1,0:T(8,128)(2,1)}, u32[]{:S(2)}, u32[]{:S(2)}) collective-permute-start(bf16[4,128,1408]{2,1,0:T(8,128)(2,1)} %all-to-all-done.6.refs_1_), channel_id=1, source_target_pairs={{0,4},{4,0},{1,5},{5,1},{2,6},{6,2},{3,7},{7,3},{8,12},{12,8},{9,1... | collective-permute-start | bytes 4325384 | tf_op jit(solution)/shard_map/ppermute | solution.py:407
  494.4 38.9 %all-to-all-start.8 = ((bf16[4,128,1408]{2,1,0:T(8,128)(2,1)}), bf16[4,128,1408]{2,1,0:T(8,128)(2,1)}, u32[]{:S(2)}, u32[]{:S(2)}) async-start(bf16[4,128,1408]{2,1,0:T(8,128)(2,1)} %after.28), calls=%async_computation.9 | async-start | bytes 2883584 | tf_op jit(solution)/shard_map/all_to_all | solution.py:423
  498.7 323.9 %reduce-scatter.6.cloned.1.call-start = ((), (), s32[]{:S(2)}) async-start(), calls=%async_computation.21 | async-start | bytes 9469952 | tf_op jit(solution)/shard_map/reduce_scatter | solution.py:653
  513.2 83.0 %collective-permute-start.7 = (bf16[4,128,1408]{2,1,0:T(8,128)(2,1)}, bf16[4,128,1408]{2,1,0:T(8,128)(2,1)}, u32[]{:S(2)}, u32[]{:S(2)}) collective-permute-start(bf16[4,128,1408]{2,1,0:T(8,128)(2,1)} %all-to-all-done.7.refs_1_), channel_id=1, source_target_pairs={{0,4},{4,0},{1,5},{5,1},{2,6},{6,2},{3,7},{7,3},{8,12},{12,8},{9,1... | collective-permute-start | bytes 4325384 | tf_op jit(solution)/shard_map/ppermute | solution.py:407
  533.4 68.1 %collective-permute-start.8 = (bf16[4,128,1408]{2,1,0:T(8,128)(2,1)}, bf16[4,128,1408]{2,1,0:T(8,128)(2,1)}, u32[]{:S(2)}, u32[]{:S(2)}) collective-permute-start(bf16[4,128,1408]{2,1,0:T(8,128)(2,1)} %all-to-all-done.8), channel_id=1, source_target_pairs={{0,4},{4,0},{1,5},{5,1},{2,6},{6,2},{3,7},{7,3},{8,12},{12,8},{9,1... | collective-permute-start | bytes 4325384 | tf_op jit(solution)/shard_map/ppermute | solution.py:407
  590.0 38.3 %collective-permute-start.9 = (bf16[2,256,1408]{2,1,0:T(8,128)(2,1)}, bf16[2,256,1408]{2,1,0:T(8,128)(2,1)}, u32[]{:S(2)}, u32[]{:S(2)}) collective-permute-start(bf16[2,256,1408]{2,1,0:T(8,128)(2,1)} %dynamic-slice_bitcast_fusion.6), channel_id=1, source_target_pairs={{0,4},{4,0},{1,5},{5,1},{2,6},{6,2},{3,7},{7,3},{8,12},{12,8},{9,1... | collective-permute-start | bytes 4325384 | tf_op jit(solution)/shard_map/ppermute | solution.py:407
  711.4 111.3 %all-to-all-start.9 = ((bf16[4,256,1408]{2,1,0:T(8,128)(2,1)}), bf16[4,256,1408]{2,1,0:T(8,128)(2,1)S(1)}, u32[]{:S(2)}, u32[]{:S(2)}) async-start(bf16[4,256,1408]{2,1,0:T(8,128)(2,1)} %fusion.5.refs_1_), calls=%async_computation.11 | async-start | bytes 5767168 | tf_op jit(solution)/shard_map/all_to_all | solution.py:423
  715.1 239.3 %all-gather.8.cloned.1.call-start = ((), (), s32[]{:S(2)}) async-start(), calls=%async_computation.22 | async-start | bytes 8912896 | tf_op jit(solution)/shard_map/all_gather | solution.py:695
  736.7 62.5 %collective-permute-start.12 = (bf16[4,256,1408]{2,1,0:T(8,128)(2,1)}, bf16[4,256,1408]{2,1,0:T(8,128)(2,1)}, u32[]{:S(2)}, u32[]{:S(2)}) collective-permute-start(bf16[4,256,1408]{2,1,0:T(8,128)(2,1)} %dynamic-slice_bitcast_fusion.2), channel_id=1, source_target_pairs={{0,4},{4,0},{1,5},{5,1},{2,6},{6,2},{3,7},{7,3},{8,12},{12,8},{9,1... | collective-permute-start | bytes 8650760 | tf_op jit(solution)/shard_map/ppermute | solution.py:407
  833.4 74.8 %collective-permute-start.11 = (bf16[4,2,128,2048]{3,2,1,0:T(8,128)(2,1)}, bf16[4,2,128,2048]{3,2,1,0:T(8,128)(2,1)}, u32[]{:S(2)}, u32[]{:S(2)}) collective-permute-start(bf16[4,2,128,2048]{3,2,1,0:T(8,128)(2,1)} %dynamic-slice_bitcast_fusion), channel_id=1, source_target_pairs={{0,1},{1,0},{2,3},{3,2},{4,5},{5,4},{6,7},{7,6},{8,9},{9,8},{10,11... | collective-permute-start | bytes 12582920 | tf_op jit(solution)/shard_map/ppermute | solution.py:465
  833.4 118.1 %all-to-all-start.10 = ((bf16[4,256,1408]{2,1,0:T(8,128)(2,1)}), bf16[4,256,1408]{2,1,0:T(8,128)(2,1)S(1)}, u32[]{:S(2)}, u32[]{:S(2)}) async-start(bf16[4,256,1408]{2,1,0:T(8,128)(2,1)} %after.32), calls=%async_computation.12 | async-start | bytes 5767168 | tf_op jit(solution)/shard_map/all_to_all | solution.py:423
  837.1 331.5 %reduce-scatter.8.cloned.1.call-start = ((), (), s32[]{:S(2)}) async-start(), calls=%async_computation.23 | async-start | bytes 9469952 | tf_op jit(solution)/shard_map/reduce_scatter | solution.py:714
  839.2 64.9 %collective-permute-start.13 = (bf16[4,256,1408]{2,1,0:T(8,128)(2,1)S(1)}, bf16[4,256,1408]{2,1,0:T(8,128)(2,1)S(1)}, u32[]{:S(2)}, u32[]{:S(2)}) collective-permute-start(bf16[4,256,1408]{2,1,0:T(8,128)(2,1)S(1)} %dynamic-slice_bitcast_fusion.1), channel_id=1, source_target_pairs={{0,4},{4,0},{1,5},{5,1},{2,6},{6,2},{3,7},{7,3},{8,12},{12,8},{9,1... | collective-permute-start | bytes 8650760 | tf_op jit(solution)/shard_map/ppermute | solution.py:407
  983.8 106.7 %all-to-all-start.11 = ((bf16[4,256,1408]{2,1,0:T(8,128)(2,1)}), bf16[4,256,1408]{2,1,0:T(8,128)(2,1)}, u32[]{:S(2)}, u32[]{:S(2)}) async-start(bf16[4,256,1408]{2,1,0:T(8,128)(2,1)} %after.35), calls=%async_computation.13 | async-start | bytes 5767168 | tf_op jit(solution)/shard_map/all_to_all | solution.py:423
  1012.9 59.8 %collective-permute-start.14 = (bf16[4,128,2048]{2,1,0:T(8,128)(2,1)S(1)}, bf16[4,128,2048]{2,1,0:T(8,128)(2,1)S(1)}, u32[]{:S(2)}, u32[]{:S(2)}) collective-permute-start(bf16[4,128,2048]{2,1,0:T(8,128)(2,1)S(1)} %dynamic-slice_bitcast_fusion.4), channel_id=1, source_target_pairs={{0,2},{1,3},{2,0},{3,1},{4,6},{5,7},{6,4},{7,5},{8,10},{9,11},{10,... | collective-permute-start | bytes 6291464 | tf_op jit(solution)/shard_map/ppermute | solution.py:465
  1016.7 59.0 %collective-permute-start.15 = (bf16[4,256,1280]{2,1,0:T(8,128)(2,1)S(1)}, bf16[4,256,1280]{2,1,0:T(8,128)(2,1)S(1)}, u32[]{:S(2)}, u32[]{:S(2)}) collective-permute-start(bf16[4,256,1280]{2,1,0:T(8,128)(2,1)S(1)} %dynamic-slice_bitcast_fusion.3), channel_id=1, source_target_pairs={{0,4},{4,0},{1,5},{5,1},{2,6},{6,2},{3,7},{7,3},{8,12},{12,8},{9,1... | collective-permute-start | bytes 7864328 | tf_op jit(solution)/shard_map/ppermute | solution.py:407
  1090.5 70.5 %all-to-all-start.12 = ((bf16[4,128,2048]{2,1,0:T(8,128)(2,1)}), bf16[4,128,2048]{2,1,0:T(8,128)(2,1)}, u32[]{:S(2)}, u32[]{:S(2)}) async-start(bf16[4,128,2048]{2,1,0:T(8,128)(2,1)} %after.36), calls=%async_computation.14 | async-start | bytes 4194304 | tf_op jit(solution)/shard_map/all_to_all | solution.py:423
  1161.0 63.6 %all-to-all-start.14 = ((bf16[4,256,1280]{2,1,0:T(8,128)(2,1)}), bf16[4,256,1280]{2,1,0:T(8,128)(2,1)}, u32[]{:S(2)}, u32[]{:S(2)}) async-start(bf16[4,256,1280]{2,1,0:T(8,128)(2,1)} %after.37), calls=%async_computation.17 | async-start | bytes 5242880 | tf_op jit(solution)/shard_map/all_to_all | solution.py:423
  (33 other events, 664.5 us)
Sparse Core Ops, SparseCore 0:
  43.5 137.7 all-gather.3
  225.4 136.8 reduce-scatter.3
  365.4 130.4 all-gather.5
  673.0 145.4 reduce-scatter.5
  828.7 125.6 all-gather.7
  983.9 172.0 reduce-scatter.7

commit v3 on v2

--- a/solution.py
+++ b/solution.py
@@ -105,6 +105,22 @@
     top = jnp.max(scores, axis=-1, keepdims=True)
     exponent = jnp.exp(scores - top)
     return exponent / jnp.sum(exponent, axis=-1, keepdims=True)
+
+
+def by_core(ref, core):
+    half = ref.shape[0] // 4
+    parts = []
+    for other in range(2):
+        for line in range(2):
+            first = (2 * line + lax.rem(core + other, 2)) * half
+            parts.append(ref[pl.ds(pl.multiple_of(first, half), half), :])
+    return jnp.concatenate(parts, axis=0)
+
+
+def split_rows(value, kept_ref, sent_ref, columns):
+    half = value.shape[0] // 4
+    for i, ref in enumerate((kept_ref, kept_ref, sent_ref, sent_ref)):
+        ref[i % 2, 0, :, columns] = value[i * half : (i + 1) * half]
 
 
 def pack_kernel(where_ref, parents_ref, tok_ref, att_ref, ffn_ref, out_ref):
@@ -129,7 +145,8 @@
 
 
 def att_fwd_kernel(
-    tok_ref, w_ref, router_ref, gain_ref, cos_ref, sin_ref, part_ref, x_ref, keep_ref, gate_ref
+    core_ref, tok_ref, w_ref, router_ref, gain_ref, cos_ref, sin_ref, kept_ref, sent_ref, x_ref,
+    keep_ref, gate_ref, z_ref
 ):
     dim = x_ref.shape[1]
     rows = x_ref.shape[0]
@@ -171,12 +188,14 @@
     for i, piece in enumerate([q[0], q[1], k, v, heads[0], heads[1]]):
         keep_ref[:, i * HS : (i + 1) * HS] = piece
     gated = [gates[:, s : s + 1] * heads[s].astype(f32) for s in range(2)]
-    z = jnp.concatenate([b.astype(bf16) for b in spread(gated, routes)], axis=1)
-    part_ref[...] = dot_nt(z, w_ref[:, qkv_width:]).astype(bf16)
+    z_ref[...] = jnp.concatenate([b.astype(bf16) for b in spread(gated, routes)], axis=1)
+    part = dot_nt(by_core(z_ref, core_ref[0]), w_ref[:, qkv_width:]).astype(bf16)
+    split_rows(part, kept_ref, sent_ref, slice(None))
 
 
 def att_bwd_kernel(
-    c_ref, w_ref, keep_ref, gate_ref, side_ref, cos_ref, sin_ref, back_ref, grad_ref, z_ref
+    core_ref, c_ref, w_ref, keep_ref, gate_ref, side_ref, cos_ref, sin_ref, kept_ref, sent_ref,
+    grad_ref, z_ref, part_ref
 ):
     dim = c_ref.shape[1]
     rows = c_ref.shape[0]
@@ -230,8 +249,17 @@
     blocks = spread(dq, routes) + [unturn(jnp.concatenate(dk, axis=0)), jnp.concatenate(dv, axis=0)]
     grad = jnp.concatenate([b.astype(bf16) for b in blocks], axis=1)
     grad_ref[...] = grad
-    back_ref[:, :dim] = dot_nt(grad, w_ref[:, :qkv_width]).astype(bf16)
-    back_ref[:, dim:] = put({0: parts[0], 1: parts[1]}, rows).astype(bf16)
+    part_ref[...] = put({0: parts[0], 1: parts[1]}, rows).astype(bf16)
+    core = core_ref[0]
+    back = dot_nt(by_core(grad_ref, core), w_ref[:, :qkv_width]).astype(bf16)
+    split_rows(back, kept_ref, sent_ref, slice(0, dim))
+    split_rows(by_core(part_ref, core), kept_ref, sent_ref, slice(dim, dim + SIDE))
+
+
+def att_grad_kernel(x_ref, c_ref, grad_ref, z_ref, wait_ref, out_ref):
+    width = grad_ref.shape[1]
+    out_ref[:, :width] = dot_tn(x_ref[...], grad_ref[...]).astype(bf16)
+    out_ref[:, width:] = dot_tn(c_ref[...], z_ref[...]).astype(bf16)
 
 
 def mid_kernel(rs_ref, packed_ref, gain_ref, router_ref, *refs):
@@ -320,22 +348,26 @@
     ).astype(bf16)
 
 
-def ffn_back_kernel(gg_ref, ug_ref, part_ref, wg_ref, wu_ref, wait_ref, back_ref):
+def ffn_back_kernel(
+    core_ref, gg_ref, ug_ref, part_ref, wg_ref, wu_ref, wait_ref, kept_ref, sent_ref
+):
     dim = wg_ref.shape[0]
-    back_ref[:, :dim] = (
-        dot_nt(gg_ref[...], wg_ref[...]) + dot_nt(ug_ref[...], wu_ref[...])
-    ).astype(bf16)
-    back_ref[:, dim:] = part_ref[...]
-
-
-def split_kernel(query_ref, kv_ref, out_ref, wait_ref, piece_ref):
-    for head in range(piece_ref.shape[0]):
-        place = 0
-        for ref in (query_ref, kv_ref, out_ref):
-            for m in range(ref.shape[0]):
-                rows = ref[m, :, head * HS : (head + 1) * HS]
-                piece_ref[head, :, place : place + HS] = rows.astype(bf16)
-                place += HS
+    core = core_ref[0]
+    back = dot_nt(by_core(gg_ref, core), wg_ref[...]) + dot_nt(by_core(ug_ref, core), wu_ref[...])
+    split_rows(back.astype(bf16), kept_ref, sent_ref, slice(0, dim))
+    split_rows(by_core(part_ref, core), kept_ref, sent_ref, slice(dim, dim + SIDE))
+
+
+def split_kernel(query_ref, kv_ref, out_ref, wait_ref, *piece_refs):
+    cut = piece_refs[0].shape[1]
+    for n, piece_ref in enumerate(piece_refs):
+        for head in range(piece_ref.shape[0]):
+            place = 0
+            for ref in (query_ref, kv_ref, out_ref):
+                for m in range(ref.shape[0]):
+                    rows = ref[m, n * cut : (n + 1) * cut, head * HS : (head + 1) * HS]
+                    piece_ref[head, :, place : place + HS] = rows.astype(bf16)
+                    place += HS
 
 
 def cast_kernel(*refs):
@@ -430,8 +462,9 @@
         part, width = halves[0].shape[1:]
         if xs == 2:
             full = jnp.zeros((zs, xs, chunks, part, width), bf16)
-            full = after(full, *ready) if ready else full
             for n in range(chunks):
+                if ready and n == chunks - 1:
+                    full = after(full, *ready)
                 for piece, column in ((halves[n], xx), (others[n], 1 - xx)):
                     full = lax.dynamic_update_slice(
                         full, piece[:, None, None], (0, column, n, 0, 0)
@@ -445,8 +478,7 @@
     across_line = [(i, i ^ 2) for i in range(ts)]
 
     def gather_line(mine):
-        spread_rows = jnp.broadcast_to(mine[None], (zs,) + mine.shape)
-        by_zz = exchange(spread_rows)
+        by_zz = lax.all_gather(mine, "zz", axis=0)
         return by_zz, lax.ppermute(by_zz, "tensor", across_line)
 
     def gather_core(by_zz, other_line):
@@ -465,6 +497,27 @@
         came = lax.ppermute(sent, "tensor", pairs)
         return (kept.astype(f32) + came.astype(f32)).astype(bf16)
 
+    core_one = jnp.stack([core]).astype(jnp.int32)
+    smem = pl.BlockSpec(memory_space=pltpu.SMEM)
+    segment = group_len // 4
+
+    def halves_of(w):
+        return [pl.BlockSpec((2, 1, segment, w), lambda i, *s: (0, i, 0, 0))] * 2
+
+    def halves_shape(w):
+        return [shape((2, zs, segment, w), bf16)] * 2
+
+    def add(one, two):
+        return (one.astype(f32) + two.astype(f32)).astype(bf16)
+
+    def sum_core(kept, sent):
+        came = lax.ppermute(sent, "tensor", across_core)
+        pick = lambda v, place: lax.dynamic_index_in_dim(v, place, 0, keepdims=False)
+        return [add(pick(kept, place), pick(came, place)) for place in (1 - line, line)]
+
+    def sum_line(sent, kept):
+        return add(kept, lax.ppermute(sent, "tensor", across_line))
+
     def return_x(grad, parts=1):
         grad = grad.reshape(zs, xs, -1, grad.shape[1])
         halves = [grad[i * zs // parts : (i + 1) * zs // parts] for i in range(parts)]
@@ -473,13 +526,11 @@
                 lax.psum_scatter(h.transpose(1, 0, 2, 3), "xx", scatter_dimension=0, tiled=False)
                 for h in halves
             ]
-            return came, jnp.concatenate(came, axis=0)
-        came = [
-            shift(lax.dynamic_index_in_dim(h, 1 - xx, 1, keepdims=False), "xx", 1, 2)
-            for h in halves
-        ]
+            return halves, came, jnp.concatenate(came, axis=0)
+        sent = [lax.dynamic_index_in_dim(h, 1 - xx, 1, keepdims=False) for h in halves]
+        came = [shift(h, "xx", 1, 2) for h in sent]
         kept = lax.dynamic_index_in_dim(grad, xx, 1, keepdims=False)
-        return came, (kept.astype(f32) + jnp.concatenate(came, 0).astype(f32)).astype(bf16)
+        return sent, came, (kept.astype(f32) + jnp.concatenate(came, 0).astype(f32)).astype(bf16)
 
     packed = pl.pallas_call(
         pack_kernel,
@@ -519,19 +570,19 @@
     zz_one = jnp.stack([zz]).astype(jnp.int32)
     vmem = pl.BlockSpec(memory_space=pltpu.VMEM)
     anywhere = pl.BlockSpec(memory_space=pl.ANY)
+    cut, width = part // 2, ffn_maps.shape[2]
     by_head = pl.pallas_call(
         split_kernel,
         in_specs=[vmem, vmem, vmem, anywhere],
-        out_specs=vmem,
-        out_shape=shape((zs, part, count * HS), bf16),
+        out_specs=[vmem] * 2,
+        out_shape=[shape((zs, cut, count * HS), bf16)] * 2,
         compiler_params=params(),
         name="split",
     )(query_maps, kv_maps, out_maps, small)
-    att_half = exchange(by_head)
-    att_other = swap(att_half)
-    w_att = assemble([att_half], [att_other])
-
-    cut, width = part // 2, ffn_maps.shape[2]
+    att_first = exchange(by_head[0])
+    att_half = exchange(after(by_head[1], att_first))
+    w_att = assemble([att_first, att_half], [swap(att_first), swap(att_half)])
+
     cast = pl.pallas_call(
         cast_kernel,
         grid=(EXPERTS,),
@@ -543,9 +594,9 @@
         out_specs=[pl.BlockSpec((1, cut, width), lambda i: (i, 0, 0))] * 6,
         out_shape=[shape((EXPERTS, cut, width), bf16)] * 6,
         compiler_params=params(),
-        cost_estimate=wall(),
+        cost_estimate=cost(1e6, 6 * ffn_maps.size),
         name="cast",
-    )(ffn_maps, ffn_maps, ffn_maps, by_head)
+    )(ffn_maps, ffn_maps, ffn_maps, by_head[0])
     chunks = []
 
     def chunk(n, *ready):
@@ -556,11 +607,9 @@
     others = []
     chunk(0, att_half)
     chunk(1, chunks[0])
-    chunk(2, chunks[1], others[0])
-    cot_zz, cot_line = gather_line(after(cotangent, chunks[2]))
-    chunk(3, cot_zz, others[1])
-    chunk(4, chunks[3], others[2])
-    chunk(5, chunks[4], others[3])
+    cot_zz, cot_line = gather_line(after(cotangent, chunks[0]))
+    for n in range(2, 6):
+        chunk(n, chunks[-1])
     w_gate, w_up = [assemble(chunks[n : n + 2], others[n : n + 2]) for n in (0, 2)]
 
     half = HS // 2
@@ -572,25 +621,28 @@
 
     trees = total // group_len
     block = lambda width: pl.BlockSpec((group_len, width), lambda i: (i, 0))
-    part_att, x1, kept, gate1 = pl.pallas_call(
+    kept_att, sent_att, x1, kept, gate1 = pl.pallas_call(
         att_fwd_kernel,
         grid=(trees,),
         in_specs=[
-            block(wide_cols), whole(w_att), whole(parts1), whole(gain1), whole(cos), whole(sin)
+            smem, block(wide_cols), whole(w_att), whole(parts1), whole(gain1), whole(cos), whole(sin)
         ],
-        out_specs=[block(dim), block(dim), block(6 * HS), block(SIDE)],
+        out_specs=[*halves_of(dim), block(dim), block(6 * HS), block(SIDE)],
         out_shape=[
-            shape((total, dim), bf16), shape((total, dim), bf16), shape((total, 6 * HS), bf16),
+            *halves_shape(dim), shape((total, dim), bf16), shape((total, 6 * HS), bf16),
             shape((total, SIDE), f32),
         ],
+        scratch_shapes=[pltpu.VMEM((group_len, EXPERTS * HS), bf16)],
         compiler_params=params(),
         cost_estimate=wall(),
         name="att_fwd",
-    )(group_tokens, w_att, parts1, gain1, cos, sin)
-    part_att = after(part_att, others[0], chunks[1])
-    sum_att = lax.psum_scatter(part_att, GROUP, scatter_dimension=0, tiled=True)
-
-    waited = [cot_zz, others[1]]
+    )(core_one, group_tokens, w_att, parts1, gain1, cos, sin)
+    sent_att = after(sent_att, others[0], chunks[1])
+    core_att = sum_core(kept_att, sent_att)
+    line_att = after(sum_line(*core_att), cot_zz, others[1])
+    sum_att = lax.psum_scatter(line_att, "zz", scatter_dimension=0, tiled=False)
+
+    waited = [chunks[3], others[2], cot_line]
     packed2, middle, gate2 = pl.pallas_call(
         mid_kernel,
         in_specs=[vmem] * 4 + [pl.BlockSpec(memory_space=pl.ANY)] * len(waited),
@@ -601,7 +653,7 @@
     )(sum_att, packed, gain2, parts2, *waited)
     x2 = lax.all_gather(packed2, GROUP, axis=0, tiled=True)
 
-    step = 512
+    step = group_len
     steps = (total // step,)
     rows_of = lambda w: pl.BlockSpec((step, w), lambda i, *s: (i, 0))
     side_of = pl.BlockSpec((step, SIDE), lambda i, *s: (i, dim // SIDE))
@@ -623,7 +675,7 @@
     )(zz_one, x2, w_gate, w_up)
     group_cot = gather_core(cot_zz, cot_line)
     down_grad = dot_tn(group_cot, act).astype(bf16)
-    down_came, down_sum = return_x(down_grad, 2)
+    down_sent, down_came, down_sum = return_x(down_grad, 2)
     w_down = assemble(chunks[4:], others[4:], act)
     gate_grad, up_grad, part2 = pl.pallas_call(
         ffn_act_kernel,
@@ -640,28 +692,32 @@
         cost_estimate=wall(),
         name="ffn_act",
     )(zz_one, x2, gate_h, up_h, group_cot, w_down, down_grad)
-    back2 = pl.pallas_call(
+    kept2, sent2 = pl.pallas_call(
         ffn_back_kernel,
         grid=steps,
-        in_specs=[rows_of(width), rows_of(width), rows_of(SIDE), fixed, fixed, anywhere],
-        out_specs=rows_of(wide_cols),
-        out_shape=shape((total, wide_cols), bf16),
+        in_specs=[smem, rows_of(width), rows_of(width), rows_of(SIDE), fixed, fixed, anywhere],
+        out_specs=halves_of(wide_cols),
+        out_shape=halves_shape(wide_cols),
         compiler_params=params(),
         cost_estimate=wall(),
         name="ffn_back",
-    )(gate_grad, up_grad, part2, w_gate, w_up, down_came[0])
-    sum_back2 = lax.psum_scatter(back2, GROUP, scatter_dimension=0, tiled=True)
+    )(core_one, gate_grad, up_grad, part2, w_gate, w_up, down_came[0])
+    core2 = sum_core(kept2, after(sent2, down_came[1]))
+    line2 = sum_line(*core2)
+    sum_back2 = lax.psum_scatter(line2, "zz", scatter_dimension=0, tiled=False)
 
     x2_low = x2[:, :dim]
-    gate_dw = dot_tn(x2_low, after(gate_grad, down_sum, back2)).astype(bf16)
+    gate_dw = dot_tn(x2_low, after(gate_grad, core2[0])).astype(bf16)
     up_dw = dot_tn(x2_low, after(up_grad, gate_dw)).astype(bf16)
-    gate_came, gate_sum = return_x(gate_dw)
-    up_came, up_sum = return_x(up_dw)
-    down_back = exchange(down_sum)
+    gate_sent, gate_came, gate_sum = return_x(gate_dw)
+    up_sent, up_came, up_sum = return_x(up_dw)
+    down_back = exchange(after(down_sum, core2[0]))
     gate_back = exchange(after(gate_sum, down_back))
-    up_back = exchange(after(up_sum, gate_back))
-    part_ffn = dot_nt(after(act, up_dw), w_down).astype(bf16)
-    by_core = fold(part_ffn.reshape(zs, 2, 2, rows, dim), 2, core, across_core)
+    up_back = [exchange(after(up_sum[:, :cut], gate_back))]
+    up_back.append(exchange(after(up_sum[:, cut:], up_back[0])))
+    part_ffn = dot_nt(after(act, up_dw, line2), w_down).astype(bf16)
+    core_ffn = fold(part_ffn.reshape(zs, 2, 2, rows, dim), 2, core, across_core)
+    by_line = fold(after(core_ffn, gate_sum), 1, line, across_line)
 
     def norm_back(route_at, rsb, wide_rows, base, gain, router, gate, gate_at, outs, name, *waited):
         def pick(a):
@@ -694,32 +750,46 @@
     )
     group_att_cot = lax.all_gather(att_cot, GROUP, axis=0, tiled=True)
 
-    group_att_cot = after(group_att_cot, gate_back, up_sum, by_core)
-    back1, grad_qkv, z = pl.pallas_call(
+    group_att_cot = after(group_att_cot, gate_back, up_sum, by_line)
+    mixed_rows = lax.psum_scatter(
+        after(by_line, group_att_cot), "zz", scatter_dimension=0, tiled=False
+    )
+    kept1, sent1, grad_qkv, z = pl.pallas_call(
         att_bwd_kernel,
         grid=(trees,),
         in_specs=[
-            block(dim), whole(w_att), block(6 * HS), block(SIDE),
+            smem, block(dim), whole(w_att), block(6 * HS), block(SIDE),
             pl.BlockSpec((group_len, SIDE), lambda i: (i, dim // SIDE)), whole(cos), whole(sin),
         ],
-        out_specs=[block(wide_cols), block(6 * HS), block(EXPERTS * HS)],
+        out_specs=[*halves_of(wide_cols), block(6 * HS), block(EXPERTS * HS)],
         out_shape=[
-            shape((total, wide_cols), bf16), shape((total, 6 * HS), bf16),
+            *halves_shape(wide_cols), shape((total, 6 * HS), bf16),
             shape((total, EXPERTS * HS), bf16),
         ],
+        scratch_shapes=[pltpu.VMEM((group_len, SIDE), bf16)],
         compiler_params=params(),
         cost_estimate=wall(),
         name="att_bwd",
-    )(group_att_cot, w_att, kept, gate1, group_tokens, cos, sin)
-    sum_back1 = lax.psum_scatter(back1, GROUP, scatter_dimension=0, tiled=True)
-
-    grad_att = jnp.concatenate(
-        [dot_tn(x1, grad_qkv).astype(bf16), dot_tn(group_att_cot, z).astype(bf16)], axis=1
-    )
-    by_line = fold(after(by_core, grad_att), 1, line, across_line)
-    att_sum = return_x(grad_att)[1]
-    att_back = exchange(after(att_sum, up_back))
-    mixed_zz = exchange(after(by_line, up_back, att_sum))
+    )(core_one, group_att_cot, w_att, kept, gate1, group_tokens, cos, sin)
+    core1 = sum_core(kept1, after(sent1, up_back[0]))
+    grad_att = pl.pallas_call(
+        att_grad_kernel,
+        grid=(zs,),
+        in_specs=[
+            pl.BlockSpec((total, dim // zs), lambda i: (0, i)),
+            pl.BlockSpec((total, dim // zs), lambda i: (0, i)),
+            whole(grad_qkv), whole(z), anywhere,
+        ],
+        out_specs=pl.BlockSpec((dim // zs, count * HS), lambda i: (i, 0)),
+        out_shape=shape((dim, count * HS), bf16),
+        compiler_params=params(),
+        cost_estimate=cost(2 * total * dim * count * HS, 6 * total * dim),
+        name="att_grad",
+    )(x1, group_att_cot, grad_qkv, z, core1[0])
+    att_sent, att_came, att_sum = return_x(grad_att)
+    line1 = sum_line(core1[0], after(core1[1], *att_sent, mixed_rows, up_back[1]))
+    sum_back1 = lax.psum_scatter(line1, "zz", scatter_dimension=0, tiled=False)
+    att_back = exchange(after(att_sum, up_back[1]))
     query_grad, kv_grad, out_grad = pl.pallas_call(
         join_kernel,
         in_specs=[vmem],
@@ -728,9 +798,9 @@
         compiler_params=params(),
         name="join",
     )(att_back)
-    ffn_out = jnp.concatenate([v.astype(f32) for v in (gate_back, up_back, down_back)], axis=0)
-
-    mixed = (middle + jnp.sum(mixed_zz.astype(f32), axis=0)).astype(bf16)
+    ffn_out = jnp.concatenate([v.astype(f32) for v in (gate_back, jnp.concatenate(up_back, axis=1), down_back)], axis=0)
+
+    mixed = (middle + mixed_rows.astype(f32)).astype(bf16)
 
     parts_att, input_grad = norm_back(
         0, sum_back1, tokens, middle_grad, gain1, router1, gate1,

time: 1250 us -> 1150 us (0.920)
  waiting for transfers between devices: 687 us -> 506 us
  blocking collectives: 14.7 us -> 77.8 us
  other arithmetic: 46.1 us -> 70 us
  matrix products: 91.7 us -> 72.4 us
    all_to_all x13 -> x12, waiting for transfers between devices: 410 us -> 212 us  [exchange(): return lax.all_to_all(value, 'zz', 0, 0, tiled=True)]
    ppermute x0 -> x6, waiting for transfers between devices: none -> 79.3 us  [the longest x3 64.6 us: sum_line(): return add(kept, lax.ppermute(sent, 'tensor', across_line))]
    all_to_all x0 -> x1, blocking collectives: none -> 63 us  [exchange(): return lax.all_to_all(value, 'zz', 0, 0, tiled=True)]
    ppermute x2, waiting for transfers between devices: 54.2 us -> 11.1 us  [fold(): came = lax.ppermute(sent, 'tensor', pairs)]
    convert_element_type x1 -> x7, other arithmetic: 0.91 us -> 29.4 us  [the longest x6 28.5 us: add(): return (one.astype(f32) + two.astype(f32)).astype(bf16)]
    dot_general x5 -> x3, matrix products: 72.8 us -> 53.6 us  [dot_tn(): lax.dot_general(a, b, (((0,), (0,)), ((), ())), preferred_element_type=f32)]
    ppermute x12 -> x13, waiting for transfers between devices: 159 us -> 140 us  [shift(): lax.ppermute(value, axis, [(i, (i + step) % size) for i in range(size)])]
    all_to_all x13 -> x12, starting transfers between devices: 58 us -> 47.9 us  [exchange(): return lax.all_to_all(value, 'zz', 0, 0, tiled=True)]
  transfers between devices with their start and end apart: 36 -> 44, of which waited for: 23 -> 27; matrix products, arithmetic and copies ran while one was open for 19% -> 20% of each run, Pallas kernels for 8% -> 17%
where the time goes in v3:
time: 1150 us; the launch traced here: 1140 us
  waiting for transfers between devices  506 us (44%)
  Pallas kernels  202 us (18%)
  local copies, waits for them, and re-layouts  116 us (10%)
  blocking collectives  77.8 us (7%)
  starting transfers between devices  75 us (7%)
  matrix products  72.4 us (6%)
  other arithmetic  70 us (6%)
  between operations  16.5 us (1%)
    all_to_all x12, waiting for transfers between devices, exchange(): return lax.all_to_all(value, 'zz', 0, 0, tiled=True)  212 us
    ppermute x13, waiting for transfers between devices, shift(): lax.ppermute(value, axis, [(i, (i + step) % size) for i in range(size)])  140 us
    ppermute x3, waiting for transfers between devices, sum_line(): return add(kept, lax.ppermute(sent, 'tensor', across_line))  64.6 us
    all_to_all x1, blocking collectives, exchange(): return lax.all_to_all(value, 'zz', 0, 0, tiled=True)  63 us
    dot_general x3, matrix products, dot_tn(): lax.dot_general(a, b, (((0,), (0,)), ((), ())), preferred_element_type=f32)  53.6 us
    all_to_all x12, starting transfers between devices, exchange(): return lax.all_to_all(value, 'zz', 0, 0, tiled=True)  47.9 us
    ppermute x1, waiting for transfers between devices, gather_line(): return (by_zz, lax.ppermute(by_zz, 'tensor', across_line))  42.1 us
    pallas_call x1, Pallas kernels, local(): pl.pallas_call(ffn_back_kernel, grid=steps, in_specs=[smem, rows_of(width...  34.3 us
  transfers between devices with their start and end apart: 44, of which 27 were waited for; matrix products, arithmetic and copies ran while one was open for 20% of the time, Pallas kernels for 17%

profile of v3, /device:TPU:0, one launch (start us, length us, event | category | flops | bytes accessed | tf_op | source)
XLA Modules:
  0.0 1136.2 jit_solution(15744458169157359539)
XLA Ops:
  16.3 14.8 %all_to_all.84 = f32[32,1,640]{2,1,0:T(1,128)S(1)} all-to-all(f32[32,1,640]{2,1,0:T(1,128)S(1)} %copy.106), channel_id=1, replica_groups=mesh['zz'=4,'xx'=2,'tensor'=4] {'zz','xx','tensor'}, dimensions={0} | all-to-all | bytes 163840 | tf_op jit(solution)/shard_map/all_to_all | solution.py:559
  36.6 63.0 %all_to_all.85.refs_1_ = bf16[4,128,1280]{2,1,0:T(8,128)(2,1)} all-to-all(bf16[4,128,1280]{2,1,0:T(8,128)(2,1)} %get-tuple-element.46.refs_3_), channel_id=1, replica_groups=mesh['zz'=4,'xx'=2,'tensor'=4] {'zz'}, dimensions={0} | all-to-all | bytes 2621440 | tf_op jit(solution)/shard_map/all_to_all | solution.py:455
  110.1 9.2 cast.1
  119.3 19.9 %all-to-all-done.2.refs_1_ = bf16[4,128,1280]{2,1,0:T(8,128)(2,1)S(1)} async-done(((bf16[4,128,1280]{2,1,0:T(8,128)(2,1)}), bf16[4,128,1280]{2,1,0:T(8,128)(2,1)S(1)}, u32[]{:S(2)}, u32[]{:S(2)}) %all-to-all-start.2) | async-done | bytes 1310752 | tf_op jit(solution)/shard_map/all_to_all | solution.py:455
  154.4 20.2 %collective-permute-done.1 = bf16[4,128,1280]{2,1,0:T(8,128)(2,1)S(1)} collective-permute-done((bf16[4,128,1280]{2,1,0:T(8,128)(2,1)}, bf16[4,128,1280]{2,1,0:T(8,128)(2,1)S(1)}, u32[]{:S(2)}, u32[]{:S(2)}) %collective-permute-start.1) | collective-permute-done | bytes 1310752 | tf_op jit(solution)/shard_map/ppermute | solution.py:439
  185.2 30.4 %att_fwd.1 = (bf16[2,4,128,2048]{3,2,1,0:T(8,128)(2,1)}, bf16[2,4,128,2048]{3,2,1,0:T(8,128)(2,1)}, bf16[2048,2048]{1,0:T(8,128)(2,1)}, bf16[2048,768]{1,0:T(8,128)(2,1)}, f32[2048,128]{1,0:T(8,128)}) custom-call(s32[1]{0:T(128)} %bitcast.core_ref, bf16[2048,2176]{1,0:T(8,128)(2,1)} %all-gather.6.cloned.1.call-done.tok_ref.side_ref, ...), custom_call_target="tpu_custom_call" | custom-call | flops 199999995904 | bytes 1000000 | tf_op jit(solution)/shard_map/att_fwd/pallas_call | solution.py:624
  236.4 41.1 %collective-permute-done.4 = bf16[4,128,2048]{2,1,0:T(8,128)(2,1)} collective-permute-done((bf16[4,128,2048]{2,1,0:T(8,128)(2,1)}, bf16[4,128,2048]{2,1,0:T(8,128)(2,1)}, u32[]{:S(2)}, u32[]{:S(2)}) %collective-permute-start.4) | collective-permute-done | bytes 2097184 | tf_op jit(solution)/shard_map/ppermute | solution.py:519
  283.2 10.4 all-gather.12.cloned.1.call-done
  306.1 42.1 %collective-permute-done.7.refs_2_ = bf16[4,128,2048]{2,1,0:T(8,128)(2,1)} collective-permute-done((bf16[4,128,2048]{2,1,0:T(8,128)(2,1)}, bf16[4,128,2048]{2,1,0:T(8,128)(2,1)}, u32[]{:S(2)}, u32[]{:S(2)}) %collective-permute-start.7) | collective-permute-done | bytes 2097184 | tf_op jit(solution)/shard_map/ppermute | solution.py:482
  348.2 18.9 %all-to-all-done.6.refs_0_.refs_1_ = bf16[4,128,1408]{2,1,0:T(8,128)(2,1)S(1)} async-done(((bf16[4,128,1408]{2,1,0:T(8,128)(2,1)}), bf16[4,128,1408]{2,1,0:T(8,128)(2,1)S(1)}, u32[]{:S(2)}, u32[]{:S(2)}) %all-to-all-start.6) | async-done | bytes 1441824 | tf_op jit(solution)/shard_map/all_to_all | solution.py:455
  412.8 40.1 %all-to-all-done.7.refs_1_ = bf16[4,128,1408]{2,1,0:T(8,128)(2,1)} async-done(((bf16[4,128,1408]{2,1,0:T(8,128)(2,1)}), bf16[4,128,1408]{2,1,0:T(8,128)(2,1)}, u32[]{:S(2)}, u32[]{:S(2)}) %all-to-all-start.7) | async-done | bytes 1441824 | tf_op jit(solution)/shard_map/all_to_all | solution.py:455
  470.8 20.2 %collective-permute-done.10 = bf16[4,128,1408]{2,1,0:T(8,128)(2,1)S(1)} collective-permute-done((bf16[4,128,1408]{2,1,0:T(8,128)(2,1)}, bf16[4,128,1408]{2,1,0:T(8,128)(2,1)S(1)}, u32[]{:S(2)}, u32[]{:S(2)}) %collective-permute-start.10) | collective-permute-done | bytes 1441824 | tf_op jit(solution)/shard_map/ppermute | solution.py:439
  500.5 33.5 %ffn_fwd.1 = (bf16[2048,1408]{1,0:T(8,128)(2,1)}, bf16[2048,1408]{1,0:T(8,128)(2,1)}, bf16[2048,1408]{1,0:T(8,128)(2,1)}) custom-call(s32[1]{0:T(128)} %bitcast.23.where_ref, bf16[2048,2176]{1,0:T(8,128)(2,1)} %all-gather.8.cloned.1.call-done.x_ref.side_ref, bf16[2048,1408]{1,0:T(8,128)(2,1)} %bitcast.30.wg_ref, bf16[2048,1408]{1,0:T(8,128)(2,1)} %bitcast.37.wu_ref), custom_call_target="tpu_custom_call" | custom-call | flops 199999995904 | bytes 1000000 | tf_op jit(solution)/shard_map/ffn_fwd/pallas_call | solution.py:663
  534.0 17.2 %convolution_convert_fusion.3.wait_ref = bf16[2048,1408]{1,0:T(8,128)(2,1)S(1)} fusion(bf16[2048,2048]{1,0:T(8,128)(2,1)} %bitcast.45.c_ref, bf16[2048,1408]{1,0:T(8,128)(2,1)} %get-tuple-element.56.refs_1_.refs_0_), kind=kOutput, calls=%fused_computation.6 | convolution fusion | flops 11814043648 | bytes 19922944 | tf_op jit(solution)/shard_map/dot_general | solution.py:32
  563.3 24.7 %ffn_act.1 = (bf16[2048,1408]{1,0:T(8,128)(2,1)}, bf16[2048,1408]{1,0:T(8,128)(2,1)}, bf16[2048,128]{1,0:T(8,128)(2,1)}) custom-call(s32[1]{0:T(128)} %bitcast.23.where_ref, bf16[2048,2176]{1,0:T(8,128)(2,1)} %all-gather.8.cloned.1.call-done.x_ref.side_ref, bf16[2048,1408]{1,0:T(8,128)(2,1)} %get-tuple-element.57.gate_ref, ...), custom_call_target="tpu_custom_call" | custom-call | flops 199999995904 | bytes 1000000 | tf_op jit(solution)/shard_map/ffn_act/pallas_call | solution.py:680
  589.7 34.3 %ffn_back.1 = (bf16[2,4,128,2176]{3,2,1,0:T(8,128)(2,1)}, bf16[2,4,128,2176]{3,2,1,0:T(8,128)(2,1)}) custom-call(s32[1]{0:T(128)} %bitcast.core_ref, bf16[2048,1408]{1,0:T(8,128)(2,1)} %get-tuple-element.62.gg_ref.refs_0_, bf16[2048,1408]{1,0:T(8,128)(2,1)} %get-tuple-element.61.ug_ref.refs_0_, bf16[2048,128]{1,0:T(8,128)(2,1)} %get-tuple-element.63.part_ref, ...), custom_call_target="tpu_custom_call" | custom-call | flops 199999995904 | bytes 1000000 | tf_op jit(solution)/shard_map/ffn_back/pallas_call | solution.py:695
  641.1 17.4 %convolution_convert_fusion.2.refs_1_ = bf16[2048,1408]{1,0:T(8,128)(2,1)S(1)} fusion(bf16[2048,1408]{1,0:T(8,128)(2,1)} %after.39, bf16[2048,2176]{1,0:T(8,128)(2,1)} %all-gather.8.cloned.1.call-done.x_ref.side_ref), kind=kOutput, calls=%fused_computation.5 | convolution fusion | flops 11814043648 | bytes 19922944 | tf_op jit(solution)/shard_map/dot_general | solution.py:32
  663.3 23.4 %collective-permute-done.15 = bf16[4,128,2176]{2,1,0:T(8,128)(2,1)} collective-permute-done((bf16[4,128,2176]{2,1,0:T(8,128)(2,1)}, bf16[4,128,2176]{2,1,0:T(8,128)(2,1)}, u32[]{:S(2)}, u32[]{:S(2)}) %collective-permute-start.15) | collective-permute-done | bytes 2228256 | tf_op jit(solution)/shard_map/ppermute | solution.py:519
  691.9 19.1 %convolution_convert_fusion.1.refs_1_ = bf16[2048,1408]{1,0:T(8,128)(2,1)} fusion(bf16[2048,1408]{1,0:T(8,128)(2,1)} %after.40, bf16[2048,2176]{1,0:T(8,128)(2,1)} %all-gather.8.cloned.1.call-done.x_ref.side_ref), kind=kOutput, calls=%fused_computation.4 | convolution fusion | flops 11814043648 | bytes 19922944 | tf_op jit(solution)/shard_map/dot_general | solution.py:32
  711.0 18.8 %convolution_convert_fusion.refs_2_ = bf16[2048,2048]{1,0:T(8,128)(2,1)} fusion(bf16[2048,1408]{1,0:T(8,128)(2,1)} %after.41, bf16[2048,1408]{1,0:T(8,128)(2,1)} %bitcast.54.wd_ref), kind=kOutput, calls=%fused_computation.3 | convolution fusion | flops 11815354368 | bytes 19922944 | tf_op jit(solution)/shard_map/dot_general | solution.py:28
  734.7 8.5 reduce-scatter.7.cloned.1.call-done
  760.7 7.8 fusion.refs_0_
  770.8 48.6 %collective-permute-done.19 = bf16[4,256,1408]{2,1,0:T(8,128)(2,1)} collective-permute-done((bf16[4,256,1408]{2,1,0:T(8,128)(2,1)}, bf16[4,256,1408]{2,1,0:T(8,128)(2,1)}, u32[]{:S(2)}, u32[]{:S(2)}) %collective-permute-start.19) | collective-permute-done | bytes 2883616 | tf_op jit(solution)/shard_map/ppermute | solution.py:439
  824.7 11.1 collective-permute-done.18
  837.8 31.8 %all-to-all-done.10.refs_1_ = bf16[4,256,1408]{2,1,0:T(8,128)(2,1)S(1)} async-done(((bf16[4,256,1408]{2,1,0:T(8,128)(2,1)}), bf16[4,256,1408]{2,1,0:T(8,128)(2,1)S(1)}, u32[]{:S(2)}, u32[]{:S(2)}) %all-to-all-start.10) | async-done | bytes 2883616 | tf_op jit(solution)/shard_map/all_to_all | solution.py:455
  875.6 30.2 %att_bwd.1 = (bf16[2,4,128,2176]{3,2,1,0:T(8,128)(2,1)}, bf16[2,4,128,2176]{3,2,1,0:T(8,128)(2,1)}, bf16[2048,768]{1,0:T(8,128)(2,1)}, bf16[2048,512]{1,0:T(8,128)(2,1)}) custom-call(s32[1]{0:T(128)} %bitcast.core_ref, bf16[2048,2048]{1,0:T(8,128)(2,1)} %after.45.refs_1_.c_ref, bf16[2048,1280]{1,0:T(8,128)(2,1)} %bitcast.16.w_ref, ...), custom_call_target="tpu_custom_call" | custom-call | flops 199999995904 | bytes 1000000 | tf_op jit(solution)/shard_map/att_bwd/pallas_call | solution.py:757
  910.1 7.8 collective-permute-done.20
  929.9 16.7 %att_grad.1 = bf16[2048,1280]{1,0:T(8,128)(2,1)} custom-call(bf16[2048,2048]{1,0:T(8,128)(2,1)} %get-tuple-element.72.x_ref, bf16[2048,2048]{1,0:T(8,128)(2,1)} %after.45.refs_1_.c_ref, bf16[2048,768]{1,0:T(8,128)(2,1)} %get-tuple-element.73.grad_ref, bf16[2048,512]{1,0:T(8,128)(2,1)} %get-tuple-element.74.z_ref, ...), custom_call_target="tpu_custom_call" | custom-call | flops 10737418240 | bytes 25165824 | tf_op jit(solution)/shard_map/att_grad/pallas_call | solution.py:775
  950.0 32.8 %all-to-all-done.12.refs_3_.refs_1_ = bf16[4,128,1408]{2,1,0:T(8,128)(2,1)S(1)} async-done(((bf16[4,128,1408]{2,1,0:T(8,128)(2,1)}), bf16[4,128,1408]{2,1,0:T(8,128)(2,1)S(1)}, u32[]{:S(2)}, u32[]{:S(2)}) %all-to-all-start.12) | async-done | bytes 1441824 | tf_op jit(solution)/shard_map/all_to_all | solution.py:455
  990.4 8.7 maximum_convert_fusion
  999.1 48.4 %collective-permute-done.22 = bf16[4,256,1280]{2,1,0:T(8,128)(2,1)} collective-permute-done((bf16[4,256,1280]{2,1,0:T(8,128)(2,1)}, bf16[4,256,1280]{2,1,0:T(8,128)(2,1)}, u32[]{:S(2)}, u32[]{:S(2)}) %collective-permute-start.22) | collective-permute-done | bytes 2621472 | tf_op jit(solution)/shard_map/ppermute | solution.py:439
  1063.1 53.2 %all-to-all-done.14.piece_ref = bf16[4,256,1280]{2,1,0:T(8,128)(2,1)} async-done(((bf16[4,256,1280]{2,1,0:T(8,128)(2,1)}), bf16[4,256,1280]{2,1,0:T(8,128)(2,1)}, u32[]{:S(2)}, u32[]{:S(2)}) %all-to-all-start.14) | async-done | bytes 2621472 | tf_op jit(solution)/shard_map/all_to_all | solution.py:455
  (265 shorter events, 295.6 us)
Async XLA Ops:
  8.0 177.2 %all-gather.6.cloned.1.call-start = ((), (), s32[]{:S(2)}) async-start(), calls=%async_computation.19 | async-start | bytes 9469952 | tf_op jit(solution)/shard_map/all_gather | solution.py:552
  99.6 39.6 %all-to-all-start.2 = ((bf16[4,128,1280]{2,1,0:T(8,128)(2,1)}), bf16[4,128,1280]{2,1,0:T(8,128)(2,1)S(1)}, u32[]{:S(2)}, u32[]{:S(2)}) async-start(bf16[4,128,1280]{2,1,0:T(8,128)(2,1)} %after.27), calls=%async_computation.2 | async-start | bytes 2621440 | tf_op jit(solution)/shard_map/all_to_all | solution.py:455
  106.0 44.7 %collective-permute-start = (bf16[4,128,1280]{2,1,0:T(8,128)(2,1)}, bf16[4,128,1280]{2,1,0:T(8,128)(2,1)}, u32[]{:S(2)}, u32[]{:S(2)}) collective-permute-start(bf16[4,128,1280]{2,1,0:T(8,128)(2,1)} %all_to_all.85.refs_1_), channel_id=1, source_target_pairs={{0,4},{4,0},{1,5},{5,1},{2,6},{6,2},{3,7},{7,3},{8,12},{12,8},{9,1... | collective-permute-start | bytes 3932168 | tf_op jit(solution)/shard_map/ppermute | solution.py:439
  183.7 109.9 %all-gather.12.cloned.1.call-start = ((), (), s32[]{:S(2)}) async-start(), calls=%async_computation.26 | async-start | bytes 2621440 | tf_op jit(solution)/shard_map/all_gather | solution.py:481
  229.7 47.9 %collective-permute-start.4 = (bf16[4,128,2048]{2,1,0:T(8,128)(2,1)}, bf16[4,128,2048]{2,1,0:T(8,128)(2,1)}, u32[]{:S(2)}, u32[]{:S(2)}) collective-permute-start(bf16[4,128,2048]{2,1,0:T(8,128)(2,1)} %fusion.15), channel_id=1, source_target_pairs={{0,2},{1,3},{2,0},{3,1},{4,6},{5,7},{6,4},{7,5},{8,10},{9,11},{10,... | collective-permute-start | bytes 6291464 | tf_op jit(solution)/shard_map/ppermute | solution.py:519
  231.0 62.6 %collective-permute-start.5 = (bf16[4,128,1408]{2,1,0:T(8,128)(2,1)}, bf16[4,128,1408]{2,1,0:T(8,128)(2,1)S(1)}, u32[]{:S(2)}, u32[]{:S(2)}) collective-permute-start(bf16[4,128,1408]{2,1,0:T(8,128)(2,1)} %all-to-all-done.4.refs_2_.refs_1_), channel_id=1, source_target_pairs={{0,4},{4,0},{1,5},{5,1},{2,6},{6,2},{3,7},{7,3},{8,12},{12,8},{9,1... | collective-permute-start | bytes 4325384 | tf_op jit(solution)/shard_map/ppermute | solution.py:439
  232.5 63.3 %all-to-all-start.5 = ((bf16[4,128,1408]{2,1,0:T(8,128)(2,1)}), bf16[4,128,1408]{2,1,0:T(8,128)(2,1)S(1)}, u32[]{:S(2)}, u32[]{:S(2)}) async-start(bf16[4,128,1408]{2,1,0:T(8,128)(2,1)} %after.33), calls=%async_computation.6 | async-start | bytes 2883584 | tf_op jit(solution)/shard_map/all_to_all | solution.py:455
  236.3 130.9 %reduce-scatter.5.cloned.1.call-start = ((), (), s32[]{:S(2)}) async-start(), calls=%async_computation.20 | async-start | bytes 2621440 | tf_op jit(solution)/shard_map/reduce_scatter | solution.py:643
  296.9 70.2 %all-to-all-start.6 = ((bf16[4,128,1408]{2,1,0:T(8,128)(2,1)}), bf16[4,128,1408]{2,1,0:T(8,128)(2,1)S(1)}, u32[]{:S(2)}, u32[]{:S(2)}) async-start(bf16[4,128,1408]{2,1,0:T(8,128)(2,1)} %after.34), calls=%async_computation.7 | async-start | bytes 2883584 | tf_op jit(solution)/shard_map/all_to_all | solution.py:455
  300.4 200.1 %all-gather.8.cloned.1.call-start = ((), (), s32[]{:S(2)}) async-start(), calls=%async_computation.21 | async-start | bytes 9469952 | tf_op jit(solution)/shard_map/all_gather | solution.py:654
  300.5 47.7 %collective-permute-start.7 = (bf16[4,128,2048]{2,1,0:T(8,128)(2,1)}, bf16[4,128,2048]{2,1,0:T(8,128)(2,1)}, u32[]{:S(2)}, u32[]{:S(2)}) collective-permute-start(bf16[4,128,2048]{2,1,0:T(8,128)(2,1)} %bitcast.208), channel_id=1, source_target_pairs={{0,2},{1,3},{2,0},{3,1},{4,6},{5,7},{6,4},{7,5},{8,10},{9,11},{10,... | collective-permute-start | bytes 6291464 | tf_op jit(solution)/shard_map/ppermute | solution.py:482
  302.0 46.2 %collective-permute-start.6 = (bf16[4,128,1408]{2,1,0:T(8,128)(2,1)}, bf16[4,128,1408]{2,1,0:T(8,128)(2,1)}, u32[]{:S(2)}, u32[]{:S(2)}) collective-permute-start(bf16[4,128,1408]{2,1,0:T(8,128)(2,1)} %copy-done.12), channel_id=1, source_target_pairs={{0,4},{4,0},{1,5},{5,1},{2,6},{6,2},{3,7},{7,3},{8,12},{12,8},{9,1... | collective-permute-start | bytes 4325384 | tf_op jit(solution)/shard_map/ppermute | solution.py:439
  385.6 80.3 %collective-permute-start.9 = (bf16[4,2,128,2048]{3,2,1,0:T(8,128)(2,1)}, bf16[4,2,128,2048]{3,2,1,0:T(8,128)(2,1)}, u32[]{:S(2)}, u32[]{:S(2)}) collective-permute-start(bf16[4,2,128,2048]{3,2,1,0:T(8,128)(2,1)} %bitcast_dynamic-update-slice_fusion.2), channel_id=1, source_target_pairs={{0,1},{1,0},{2,3},{3,2},{4,5},{5,4},{6,7},{7,6},{8,9},{9,8},{10,11... | collective-permute-start | bytes 12582920 | tf_op jit(solution)/shard_map/ppermute | solution.py:488
  389.5 63.5 %all-to-all-start.7 = ((bf16[4,128,1408]{2,1,0:T(8,128)(2,1)}), bf16[4,128,1408]{2,1,0:T(8,128)(2,1)}, u32[]{:S(2)}, u32[]{:S(2)}) async-start(bf16[4,128,1408]{2,1,0:T(8,128)(2,1)} %after.35), calls=%async_computation.8 | async-start | bytes 2883584 | tf_op jit(solution)/shard_map/all_to_all | solution.py:455
  398.3 60.8 %collective-permute-start.8 = (bf16[4,128,1408]{2,1,0:T(8,128)(2,1)S(1)}, bf16[4,128,1408]{2,1,0:T(8,128)(2,1)S(1)}, u32[]{:S(2)}, u32[]{:S(2)}) collective-permute-start(bf16[4,128,1408]{2,1,0:T(8,128)(2,1)S(1)} %copy-done.15), channel_id=1, source_target_pairs={{0,4},{4,0},{1,5},{5,1},{2,6},{6,2},{3,7},{7,3},{8,12},{12,8},{9,1... | collective-permute-start | bytes 4325384 | tf_op jit(solution)/shard_map/ppermute | solution.py:439
  453.0 46.1 %all-to-all-start.8 = ((bf16[4,128,1408]{2,1,0:T(8,128)(2,1)}), bf16[4,128,1408]{2,1,0:T(8,128)(2,1)}, u32[]{:S(2)}, u32[]{:S(2)}) async-start(bf16[4,128,1408]{2,1,0:T(8,128)(2,1)} %after.37), calls=%async_computation.9 | async-start | bytes 2883584 | tf_op jit(solution)/shard_map/all_to_all | solution.py:455
  499.1 61.6 %collective-permute-start.11 = (bf16[4,128,1408]{2,1,0:T(8,128)(2,1)}, bf16[4,128,1408]{2,1,0:T(8,128)(2,1)}, u32[]{:S(2)}, u32[]{:S(2)}) collective-permute-start(bf16[4,128,1408]{2,1,0:T(8,128)(2,1)} %all-to-all-done.8), channel_id=1, source_target_pairs={{0,4},{4,0},{1,5},{5,1},{2,6},{6,2},{3,7},{7,3},{8,12},{12,8},{9,1... | collective-permute-start | bytes 4325384 | tf_op jit(solution)/shard_map/ppermute | solution.py:439
  556.6 67.4 %collective-permute-start.13 = (bf16[2,256,1408]{2,1,0:T(8,128)(2,1)}, bf16[2,256,1408]{2,1,0:T(8,128)(2,1)}, u32[]{:S(2)}, u32[]{:S(2)}) collective-permute-start(bf16[2,256,1408]{2,1,0:T(8,128)(2,1)} %dynamic-slice_bitcast_fusion.5), channel_id=1, source_target_pairs={{0,4},{4,0},{1,5},{5,1},{2,6},{6,2},{3,7},{7,3},{8,12},{12,8},{9,1... | collective-permute-start | bytes 4325384 | tf_op jit(solution)/shard_map/ppermute | solution.py:439
  635.9 50.8 %collective-permute-start.15 = (bf16[4,128,2176]{2,1,0:T(8,128)(2,1)}, bf16[4,128,2176]{2,1,0:T(8,128)(2,1)}, u32[]{:S(2)}, u32[]{:S(2)}) collective-permute-start(bf16[4,128,2176]{2,1,0:T(8,128)(2,1)} %fusion.10.refs_1_), channel_id=1, source_target_pairs={{0,2},{1,3},{2,0},{3,1},{4,6},{5,7},{6,4},{7,5},{8,10},{9,11},{10,... | collective-permute-start | bytes 6684680 | tf_op jit(solution)/shard_map/ppermute | solution.py:519
  637.4 97.4 %all-to-all-start.9 = ((bf16[4,256,1408]{2,1,0:T(8,128)(2,1)}), bf16[4,256,1408]{2,1,0:T(8,128)(2,1)S(1)}, u32[]{:S(2)}, u32[]{:S(2)}) async-start(bf16[4,256,1408]{2,1,0:T(8,128)(2,1)} %after.43), calls=%async_computation.11 | async-start | bytes 5767168 | tf_op jit(solution)/shard_map/all_to_all | solution.py:455
  641.0 102.1 %reduce-scatter.7.cloned.1.call-start = ((), (), s32[]{:S(2)}) async-start(), calls=%async_computation.22 | async-start | bytes 2785280 | tf_op jit(solution)/shard_map/reduce_scatter | solution.py:707
  662.7 67.1 %collective-permute-start.17 = (bf16[4,256,1408]{2,1,0:T(8,128)(2,1)}, bf16[4,256,1408]{2,1,0:T(8,128)(2,1)}, u32[]{:S(2)}, u32[]{:S(2)}) collective-permute-start(bf16[4,256,1408]{2,1,0:T(8,128)(2,1)} %dynamic-slice_bitcast_fusion.2), channel_id=1, source_target_pairs={{0,4},{4,0},{1,5},{5,1},{2,6},{6,2},{3,7},{7,3},{8,12},{12,8},{9,1... | collective-permute-start | bytes 8650760 | tf_op jit(solution)/shard_map/ppermute | solution.py:439
  691.9 183.7 %all-gather.10.cloned.1.call-start = ((), (), s32[]{:S(2)}) async-start(), calls=%async_computation.23 | async-start | bytes 8912896 | tf_op jit(solution)/shard_map/all_gather | solution.py:751
  754.3 65.1 %collective-permute-start.19 = (bf16[4,256,1408]{2,1,0:T(8,128)(2,1)}, bf16[4,256,1408]{2,1,0:T(8,128)(2,1)}, u32[]{:S(2)}, u32[]{:S(2)}) collective-permute-start(bf16[4,256,1408]{2,1,0:T(8,128)(2,1)} %dynamic-slice_bitcast_fusion.1), channel_id=1, source_target_pairs={{0,4},{4,0},{1,5},{5,1},{2,6},{6,2},{3,7},{7,3},{8,12},{12,8},{9,1... | collective-permute-start | bytes 8650760 | tf_op jit(solution)/shard_map/ppermute | solution.py:439
  757.0 112.6 %all-to-all-start.10 = ((bf16[4,256,1408]{2,1,0:T(8,128)(2,1)}), bf16[4,256,1408]{2,1,0:T(8,128)(2,1)S(1)}, u32[]{:S(2)}, u32[]{:S(2)}) async-start(bf16[4,256,1408]{2,1,0:T(8,128)(2,1)} %after.44), calls=%async_computation.12 | async-start | bytes 5767168 | tf_op jit(solution)/shard_map/all_to_all | solution.py:455
  770.2 65.6 %collective-permute-start.18 = (bf16[4,128,2048]{2,1,0:T(8,128)(2,1)S(1)}, bf16[4,128,2048]{2,1,0:T(8,128)(2,1)S(1)}, u32[]{:S(2)}, u32[]{:S(2)}) collective-permute-start(bf16[4,128,2048]{2,1,0:T(8,128)(2,1)S(1)} %dynamic-slice_bitcast_fusion.4), channel_id=1, source_target_pairs={{0,2},{1,3},{2,0},{3,1},{4,6},{5,7},{6,4},{7,5},{8,10},{9,11},{10,... | collective-permute-start | bytes 6291464 | tf_op jit(solution)/shard_map/ppermute | solution.py:497
  875.5 107.4 %reduce-scatter.9.cloned.1.call-start = ((), (), s32[]{:S(2)}) async-start(), calls=%async_computation.24 | async-start | bytes 2621440 | tf_op jit(solution)/shard_map/reduce_scatter | solution.py:754
  924.8 59.1 %collective-permute-start.21 = (bf16[4,128,2176]{2,1,0:T(8,128)(2,1)}, bf16[4,128,2176]{2,1,0:T(8,128)(2,1)}, u32[]{:S(2)}, u32[]{:S(2)}) collective-permute-start(bf16[4,128,2176]{2,1,0:T(8,128)(2,1)} %get-tuple-element.85.wait_ref), channel_id=1, source_target_pairs={{0,2},{1,3},{2,0},{3,1},{4,6},{5,7},{6,4},{7,5},{8,10},{9,11},{10,... | collective-permute-start | bytes 6684680 | tf_op jit(solution)/shard_map/ppermute | solution.py:519
  926.3 56.5 %all-to-all-start.12 = ((bf16[4,128,1408]{2,1,0:T(8,128)(2,1)}), bf16[4,128,1408]{2,1,0:T(8,128)(2,1)S(1)}, u32[]{:S(2)}, u32[]{:S(2)}) async-start(bf16[4,128,1408]{2,1,0:T(8,128)(2,1)} %after.49), calls=%async_computation.15 | async-start | bytes 2883584 | tf_op jit(solution)/shard_map/all_to_all | solution.py:455
  929.9 127.3 %reduce-scatter.11.cloned.1.call-start = ((), (), s32[]{:S(2)}) async-start(), calls=%async_computation.25 | async-start | bytes 2785280 | tf_op jit(solution)/shard_map/reduce_scatter | solution.py:791
  988.3 59.3 %collective-permute-start.22 = (bf16[4,256,1280]{2,1,0:T(8,128)(2,1)}, bf16[4,256,1280]{2,1,0:T(8,128)(2,1)}, u32[]{:S(2)}, u32[]{:S(2)}) collective-permute-start(bf16[4,256,1280]{2,1,0:T(8,128)(2,1)} %dynamic-slice_bitcast_fusion.3.refs_1_), channel_id=1, source_target_pairs={{0,4},{4,0},{1,5},{5,1},{2,6},{6,2},{3,7},{7,3},{8,12},{12,8},{9,1... | collective-permute-start | bytes 7864328 | tf_op jit(solution)/shard_map/ppermute | solution.py:439
  1052.2 64.1 %all-to-all-start.14 = ((bf16[4,256,1280]{2,1,0:T(8,128)(2,1)}), bf16[4,256,1280]{2,1,0:T(8,128)(2,1)}, u32[]{:S(2)}, u32[]{:S(2)}) async-start(bf16[4,256,1280]{2,1,0:T(8,128)(2,1)} %after.51), calls=%async_computation.18 | async-start | bytes 5242880 | tf_op jit(solution)/shard_map/all_to_all | solution.py:455
  (45 other events, 555.0 us)
Sparse Core Ops, SparseCore 0:
  14.0 117.2 all-gather.5
  371.4 119.5 all-gather.7
  747.6 122.1 all-gather.9
Sparse Core Ops, SparseCore 1:
  219.4 74.1 all-gather.11
  296.3 68.0 reduce-scatter.4
  692.0 51.2 reduce-scatter.6
  910.2 59.6 reduce-scatter.8
  988.3 44.5 reduce-scatter.10

commit v4 on v3

--- a/solution.py
+++ b/solution.py
@@ -317,16 +317,25 @@
     return in0, in1, jnp.where(in0, side[:, 0:1], 0.0) + jnp.where(in1, side[:, 1:2], 0.0)
 
 
+def column_chunks(width):
+    return [slice(n, min(n + 256, width)) for n in range(0, width, 256)]
+
+
+def sigmoid(v):
+    return 0.5 * jnp.tanh(0.5 * v) + 0.5
+
+
 def ffn_fwd_kernel(where_ref, x_ref, wg_ref, wu_ref, gate_ref, up_ref, a_ref):
-    dim = wg_ref.shape[0]
+    dim, width = wg_ref.shape
     side = x_ref[:, dim:].astype(f32)
     coef = ffn_coef(side, where_ref[0].astype(f32))[2]
     x = x_ref[:, :dim]
-    gate = dot(x, wg_ref[...])
-    up = dot(x, wu_ref[...])
-    gate_ref[...] = gate.astype(bf16)
-    up_ref[...] = up.astype(bf16)
-    a_ref[...] = (gate * jax.nn.sigmoid(gate) * up * coef).astype(bf16)
+    for at in column_chunks(width):
+        gate = dot(x, wg_ref[:, at])
+        up = dot(x, wu_ref[:, at])
+        gate_ref[:, at] = gate.astype(bf16)
+        up_ref[:, at] = up.astype(bf16)
+        a_ref[:, at] = (gate * sigmoid(gate) * up * coef).astype(bf16)
 
 
 def ffn_act_kernel(
@@ -334,15 +343,18 @@
 ):
     rows = c_ref.shape[0]
     in0, in1, coef = ffn_coef(side_ref[...].astype(f32), where_ref[0].astype(f32))
-    gate = gate_ref[...].astype(f32)
-    up = up_ref[...].astype(f32)
-    act_grad = dot(c_ref[...], wd_ref[...])
-    sig = jax.nn.sigmoid(gate)
-    silu = gate * sig
-    part = jnp.sum(silu * up * act_grad, axis=-1, keepdims=True)
-    act_grad = act_grad * coef
-    gg_ref[...] = (act_grad * up * sig * (1.0 + gate * (1.0 - sig))).astype(bf16)
-    ug_ref[...] = (act_grad * silu).astype(bf16)
+    c = c_ref[...]
+    part = jnp.zeros((rows, 1), f32)
+    for at in column_chunks(wd_ref.shape[1]):
+        gate = gate_ref[:, at].astype(f32)
+        up = up_ref[:, at].astype(f32)
+        act_grad = dot(c, wd_ref[:, at])
+        sig = sigmoid(gate)
+        silu = gate * sig
+        part = part + jnp.sum(silu * up * act_grad, axis=-1, keepdims=True)
+        act_grad = act_grad * coef
+        gg_ref[:, at] = (act_grad * up * (sig + silu * (1.0 - sig))).astype(bf16)
+        ug_ref[:, at] = (act_grad * silu).astype(bf16)
     part_ref[...] = put(
         {0: jnp.where(in0, part, 0.0), 1: jnp.where(in1, part, 0.0)}, rows
     ).astype(bf16)
@@ -786,8 +798,8 @@
         cost_estimate=cost(2 * total * dim * count * HS, 6 * total * dim),
         name="att_grad",
     )(x1, group_att_cot, grad_qkv, z, core1[0])
-    att_sent, att_came, att_sum = return_x(grad_att)
-    line1 = sum_line(core1[0], after(core1[1], *att_sent, mixed_rows, up_back[1]))
+    att_sent, att_came, att_sum = return_x(grad_att, 2)
+    line1 = sum_line(core1[0], after(core1[1], *att_sent, att_came[0], mixed_rows, up_back[1]))
     sum_back1 = lax.psum_scatter(line1, "zz", scatter_dimension=0, tiled=False)
     att_back = exchange(after(att_sum, up_back[1]))
     query_grad, kv_grad, out_grad = pl.pallas_call(

time: 1150 us -> 1120 us (0.974)
  waiting for transfers between devices: 506 us -> 473 us
    ppermute x13 -> x14, waiting for transfers between devices: 140 us -> 110 us  [shift(): lax.ppermute(value, axis, [(i, (i + step) % size) for i in range(size)])]
    unnamed x72 -> x76, local copies, waits for them, and re-layouts: 23.8 us -> 24.2 us
  transfers between devices with their start and end apart: 44 -> 45, of which waited for: 27 -> 28; matrix products, arithmetic and copies ran while one was open for 20% -> 21% of each run, Pallas kernels for 17% -> 17%
where the time goes in v4:
time: 1120 us; the launch traced here: 1110 us
  waiting for transfers between devices  473 us (42%)
  Pallas kernels  203 us (18%)
  local copies, waits for them, and re-layouts  119 us (11%)
  blocking collectives  77.8 us (7%)
  starting transfers between devices  77.3 us (7%)
  matrix products  72.4 us (6%)
  other arithmetic  70.1 us (6%)
  between operations  16.5 us (1%)
    all_to_all x12, waiting for transfers between devices, exchange(): return lax.all_to_all(value, 'zz', 0, 0, tiled=True)  206 us
    ppermute x14, waiting for transfers between devices, shift(): lax.ppermute(value, axis, [(i, (i + step) % size) for i in range(size)])  110 us
    ppermute x3, waiting for transfers between devices, sum_line(): return add(kept, lax.ppermute(sent, 'tensor', across_line))  64.5 us
    all_to_all x1, blocking collectives, exchange(): return lax.all_to_all(value, 'zz', 0, 0, tiled=True)  63 us
    dot_general x3, matrix products, dot_tn(): lax.dot_general(a, b, (((0,), (0,)), ((), ())), preferred_element_type=f32)  53.6 us
    all_to_all x12, starting transfers between devices, exchange(): return lax.all_to_all(value, 'zz', 0, 0, tiled=True)  47.9 us
    ppermute x1, waiting for transfers between devices, gather_line(): return (by_zz, lax.ppermute(by_zz, 'tensor', across_line))  42.1 us
    pallas_call x1, Pallas kernels, local(): pl.pallas_call(ffn_back_kernel, grid=steps, in_specs=[smem, rows_of(width...  34.3 us
  transfers between devices with their start and end apart: 45, of which 28 were waited for; matrix products, arithmetic and copies ran while one was open for 21% of the time, Pallas kernels for 17%

profile of v4, /device:TPU:0, one launch (start us, length us, event | category | flops | bytes accessed | tf_op | source)
XLA Modules:
  0.0 1109.2 jit_solution(12358080459990341608)
XLA Ops:
  16.3 14.8 %all_to_all.84 = f32[32,1,640]{2,1,0:T(1,128)S(1)} all-to-all(f32[32,1,640]{2,1,0:T(1,128)S(1)} %copy.110), channel_id=1, replica_groups=mesh['zz'=4,'xx'=2,'tensor'=4] {'zz','xx','tensor'}, dimensions={0} | all-to-all | bytes 163840 | tf_op jit(solution)/shard_map/all_to_all | solution.py:571
  36.6 63.0 %all_to_all.85.refs_1_ = bf16[4,128,1280]{2,1,0:T(8,128)(2,1)} all-to-all(bf16[4,128,1280]{2,1,0:T(8,128)(2,1)} %get-tuple-element.46.refs_3_), channel_id=1, replica_groups=mesh['zz'=4,'xx'=2,'tensor'=4] {'zz'}, dimensions={0} | all-to-all | bytes 2621440 | tf_op jit(solution)/shard_map/all_to_all | solution.py:467
  110.2 9.2 cast.1
  119.3 19.9 %all-to-all-done.2.refs_1_ = bf16[4,128,1280]{2,1,0:T(8,128)(2,1)S(1)} async-done(((bf16[4,128,1280]{2,1,0:T(8,128)(2,1)}), bf16[4,128,1280]{2,1,0:T(8,128)(2,1)S(1)}, u32[]{:S(2)}, u32[]{:S(2)}) %all-to-all-start.2) | async-done | bytes 1310752 | tf_op jit(solution)/shard_map/all_to_all | solution.py:467
  154.3 20.3 %collective-permute-done.1 = bf16[4,128,1280]{2,1,0:T(8,128)(2,1)S(1)} collective-permute-done((bf16[4,128,1280]{2,1,0:T(8,128)(2,1)}, bf16[4,128,1280]{2,1,0:T(8,128)(2,1)S(1)}, u32[]{:S(2)}, u32[]{:S(2)}) %collective-permute-start.1) | collective-permute-done | bytes 1310752 | tf_op jit(solution)/shard_map/ppermute | solution.py:451
  185.2 30.4 %att_fwd.1 = (bf16[2,4,128,2048]{3,2,1,0:T(8,128)(2,1)}, bf16[2,4,128,2048]{3,2,1,0:T(8,128)(2,1)}, bf16[2048,2048]{1,0:T(8,128)(2,1)}, bf16[2048,768]{1,0:T(8,128)(2,1)}, f32[2048,128]{1,0:T(8,128)}) custom-call(s32[1]{0:T(128)} %bitcast.core_ref, bf16[2048,2176]{1,0:T(8,128)(2,1)} %all-gather.6.cloned.1.call-done.tok_ref.side_ref, ...), custom_call_target="tpu_custom_call" | custom-call | flops 199999995904 | bytes 1000000 | tf_op jit(solution)/shard_map/att_fwd/pallas_call | solution.py:636
  236.4 41.1 %collective-permute-done.4 = bf16[4,128,2048]{2,1,0:T(8,128)(2,1)} collective-permute-done((bf16[4,128,2048]{2,1,0:T(8,128)(2,1)}, bf16[4,128,2048]{2,1,0:T(8,128)(2,1)}, u32[]{:S(2)}, u32[]{:S(2)}) %collective-permute-start.4) | collective-permute-done | bytes 2097184 | tf_op jit(solution)/shard_map/ppermute | solution.py:531
  283.2 10.4 all-gather.12.cloned.1.call-done
  306.1 42.1 %collective-permute-done.7.refs_2_ = bf16[4,128,2048]{2,1,0:T(8,128)(2,1)} collective-permute-done((bf16[4,128,2048]{2,1,0:T(8,128)(2,1)}, bf16[4,128,2048]{2,1,0:T(8,128)(2,1)}, u32[]{:S(2)}, u32[]{:S(2)}) %collective-permute-start.7) | collective-permute-done | bytes 2097184 | tf_op jit(solution)/shard_map/ppermute | solution.py:494
  348.2 18.9 %all-to-all-done.6.refs_0_.refs_1_ = bf16[4,128,1408]{2,1,0:T(8,128)(2,1)S(1)} async-done(((bf16[4,128,1408]{2,1,0:T(8,128)(2,1)}), bf16[4,128,1408]{2,1,0:T(8,128)(2,1)S(1)}, u32[]{:S(2)}, u32[]{:S(2)}) %all-to-all-start.6) | async-done | bytes 1441824 | tf_op jit(solution)/shard_map/all_to_all | solution.py:467
  413.2 39.9 %all-to-all-done.7.refs_1_ = bf16[4,128,1408]{2,1,0:T(8,128)(2,1)} async-done(((bf16[4,128,1408]{2,1,0:T(8,128)(2,1)}), bf16[4,128,1408]{2,1,0:T(8,128)(2,1)}, u32[]{:S(2)}, u32[]{:S(2)}) %all-to-all-start.7) | async-done | bytes 1441824 | tf_op jit(solution)/shard_map/all_to_all | solution.py:467
  470.9 20.1 %collective-permute-done.10 = bf16[4,128,1408]{2,1,0:T(8,128)(2,1)S(1)} collective-permute-done((bf16[4,128,1408]{2,1,0:T(8,128)(2,1)}, bf16[4,128,1408]{2,1,0:T(8,128)(2,1)S(1)}, u32[]{:S(2)}, u32[]{:S(2)}) %collective-permute-start.10) | collective-permute-done | bytes 1441824 | tf_op jit(solution)/shard_map/ppermute | solution.py:451
  500.5 33.7 %ffn_fwd.1 = (bf16[2048,1408]{1,0:T(8,128)(2,1)}, bf16[2048,1408]{1,0:T(8,128)(2,1)}, bf16[2048,1408]{1,0:T(8,128)(2,1)}) custom-call(s32[1]{0:T(128)} %bitcast.23.where_ref, bf16[2048,2176]{1,0:T(8,128)(2,1)} %all-gather.8.cloned.1.call-done.x_ref.side_ref, bf16[2048,1408]{1,0:T(8,128)(2,1)} %bitcast.30.wg_ref, bf16[2048,1408]{1,0:T(8,128)(2,1)} %bitcast.37.wu_ref), custom_call_target="tpu_custom_call" | custom-call | flops 199999995904 | bytes 1000000 | tf_op jit(solution)/shard_map/ffn_fwd/pallas_call | solution.py:675
  534.2 17.2 %convolution_convert_fusion.3.wait_ref = bf16[2048,1408]{1,0:T(8,128)(2,1)S(1)} fusion(bf16[2048,2048]{1,0:T(8,128)(2,1)} %bitcast.45.c_ref, bf16[2048,1408]{1,0:T(8,128)(2,1)} %get-tuple-element.56.refs_1_.refs_0_), kind=kOutput, calls=%fused_computation.6 | convolution fusion | flops 11814043648 | bytes 19922944 | tf_op jit(solution)/shard_map/dot_general | solution.py:32
  563.5 26.1 %ffn_act.1 = (bf16[2048,1408]{1,0:T(8,128)(2,1)}, bf16[2048,1408]{1,0:T(8,128)(2,1)}, bf16[2048,128]{1,0:T(8,128)(2,1)}) custom-call(s32[1]{0:T(128)} %bitcast.23.where_ref, bf16[2048,2176]{1,0:T(8,128)(2,1)} %all-gather.8.cloned.1.call-done.x_ref.side_ref, bf16[2048,1408]{1,0:T(8,128)(2,1)} %get-tuple-element.57.gate_ref, ...), custom_call_target="tpu_custom_call" | custom-call | flops 199999995904 | bytes 1000000 | tf_op jit(solution)/shard_map/ffn_act/pallas_call | solution.py:692
  589.9 34.3 %ffn_back.1 = (bf16[2,4,128,2176]{3,2,1,0:T(8,128)(2,1)}, bf16[2,4,128,2176]{3,2,1,0:T(8,128)(2,1)}) custom-call(s32[1]{0:T(128)} %bitcast.core_ref, bf16[2048,1408]{1,0:T(8,128)(2,1)} %get-tuple-element.62.gg_ref.refs_0_, bf16[2048,1408]{1,0:T(8,128)(2,1)} %get-tuple-element.61.ug_ref.refs_0_, bf16[2048,128]{1,0:T(8,128)(2,1)} %get-tuple-element.63.part_ref, ...), custom_call_target="tpu_custom_call" | custom-call | flops 199999995904 | bytes 1000000 | tf_op jit(solution)/shard_map/ffn_back/pallas_call | solution.py:707
  641.3 17.4 %convolution_convert_fusion.2.refs_1_ = bf16[2048,1408]{1,0:T(8,128)(2,1)S(1)} fusion(bf16[2048,1408]{1,0:T(8,128)(2,1)} %after.39, bf16[2048,2176]{1,0:T(8,128)(2,1)} %all-gather.8.cloned.1.call-done.x_ref.side_ref), kind=kOutput, calls=%fused_computation.5 | convolution fusion | flops 11814043648 | bytes 19922944 | tf_op jit(solution)/shard_map/dot_general | solution.py:32
  663.5 23.4 %collective-permute-done.15 = bf16[4,128,2176]{2,1,0:T(8,128)(2,1)} collective-permute-done((bf16[4,128,2176]{2,1,0:T(8,128)(2,1)}, bf16[4,128,2176]{2,1,0:T(8,128)(2,1)}, u32[]{:S(2)}, u32[]{:S(2)}) %collective-permute-start.15) | collective-permute-done | bytes 2228256 | tf_op jit(solution)/shard_map/ppermute | solution.py:531
  692.1 19.1 %convolution_convert_fusion.1.refs_1_ = bf16[2048,1408]{1,0:T(8,128)(2,1)} fusion(bf16[2048,1408]{1,0:T(8,128)(2,1)} %after.40, bf16[2048,2176]{1,0:T(8,128)(2,1)} %all-gather.8.cloned.1.call-done.x_ref.side_ref), kind=kOutput, calls=%fused_computation.4 | convolution fusion | flops 11814043648 | bytes 19922944 | tf_op jit(solution)/shard_map/dot_general | solution.py:32
  711.2 18.8 %convolution_convert_fusion.refs_2_ = bf16[2048,2048]{1,0:T(8,128)(2,1)} fusion(bf16[2048,1408]{1,0:T(8,128)(2,1)} %after.41, bf16[2048,1408]{1,0:T(8,128)(2,1)} %bitcast.54.wd_ref), kind=kOutput, calls=%fused_computation.3 | convolution fusion | flops 11815354368 | bytes 19922944 | tf_op jit(solution)/shard_map/dot_general | solution.py:28
  734.9 8.5 reduce-scatter.7.cloned.1.call-done
  760.9 7.8 fusion.refs_0_
  771.1 48.6 %collective-permute-done.19 = bf16[4,256,1408]{2,1,0:T(8,128)(2,1)} collective-permute-done((bf16[4,256,1408]{2,1,0:T(8,128)(2,1)}, bf16[4,256,1408]{2,1,0:T(8,128)(2,1)}, u32[]{:S(2)}, u32[]{:S(2)}) %collective-permute-start.19) | collective-permute-done | bytes 2883616 | tf_op jit(solution)/shard_map/ppermute | solution.py:451
  824.9 11.1 collective-permute-done.18
  838.0 31.8 %all-to-all-done.10.refs_1_ = bf16[4,256,1408]{2,1,0:T(8,128)(2,1)S(1)} async-done(((bf16[4,256,1408]{2,1,0:T(8,128)(2,1)}), bf16[4,256,1408]{2,1,0:T(8,128)(2,1)S(1)}, u32[]{:S(2)}, u32[]{:S(2)}) %all-to-all-start.10) | async-done | bytes 2883616 | tf_op jit(solution)/shard_map/all_to_all | solution.py:467
  875.8 30.2 %att_bwd.1 = (bf16[2,4,128,2176]{3,2,1,0:T(8,128)(2,1)}, bf16[2,4,128,2176]{3,2,1,0:T(8,128)(2,1)}, bf16[2048,768]{1,0:T(8,128)(2,1)}, bf16[2048,512]{1,0:T(8,128)(2,1)}) custom-call(s32[1]{0:T(128)} %bitcast.core_ref, bf16[2048,2048]{1,0:T(8,128)(2,1)} %after.45.refs_1_.c_ref, bf16[2048,1280]{1,0:T(8,128)(2,1)} %bitcast.16.w_ref, ...), custom_call_target="tpu_custom_call" | custom-call | flops 199999995904 | bytes 1000000 | tf_op jit(solution)/shard_map/att_bwd/pallas_call | solution.py:769
  918.2 6.9 fusion.12
  926.6 16.6 %att_grad.1 = bf16[2048,1280]{1,0:T(8,128)(2,1)} custom-call(bf16[2048,2048]{1,0:T(8,128)(2,1)} %get-tuple-element.72.x_ref, bf16[2048,2048]{1,0:T(8,128)(2,1)} %after.45.refs_1_.c_ref, bf16[2048,768]{1,0:T(8,128)(2,1)} %get-tuple-element.73.grad_ref, bf16[2048,512]{1,0:T(8,128)(2,1)} %get-tuple-element.74.z_ref, ...), custom_call_target="tpu_custom_call" | custom-call | flops 10737418240 | bytes 25165824 | tf_op jit(solution)/shard_map/att_grad/pallas_call | solution.py:787
  949.9 31.4 %all-to-all-done.12.refs_5_.refs_1_ = bf16[4,128,1408]{2,1,0:T(8,128)(2,1)S(1)} async-done(((bf16[4,128,1408]{2,1,0:T(8,128)(2,1)}), bf16[4,128,1408]{2,1,0:T(8,128)(2,1)S(1)}, u32[]{:S(2)}, u32[]{:S(2)}) %all-to-all-start.12) | async-done | bytes 1441824 | tf_op jit(solution)/shard_map/all_to_all | solution.py:467
  989.3 9.0 maximum_convert_fusion
  998.3 19.3 %collective-permute-done.23 = bf16[2,256,1280]{2,1,0:T(8,128)(2,1)} collective-permute-done((bf16[2,256,1280]{2,1,0:T(8,128)(2,1)}, bf16[2,256,1280]{2,1,0:T(8,128)(2,1)}, u32[]{:S(2)}, u32[]{:S(2)}) %collective-permute-start.23) | collective-permute-done | bytes 1310752 | tf_op jit(solution)/shard_map/ppermute | solution.py:451
  1039.5 48.8 %all-to-all-done.14.piece_ref = bf16[4,256,1280]{2,1,0:T(8,128)(2,1)} async-done(((bf16[4,256,1280]{2,1,0:T(8,128)(2,1)}), bf16[4,256,1280]{2,1,0:T(8,128)(2,1)}, u32[]{:S(2)}, u32[]{:S(2)}) %all-to-all-start.14) | async-done | bytes 2621472 | tf_op jit(solution)/shard_map/all_to_all | solution.py:467
  (273 shorter events, 302.7 us)
Async XLA Ops:
  8.0 177.2 %all-gather.6.cloned.1.call-start = ((), (), s32[]{:S(2)}) async-start(), calls=%async_computation.19 | async-start | bytes 9469952 | tf_op jit(solution)/shard_map/all_gather | solution.py:564
  99.6 39.6 %all-to-all-start.2 = ((bf16[4,128,1280]{2,1,0:T(8,128)(2,1)}), bf16[4,128,1280]{2,1,0:T(8,128)(2,1)S(1)}, u32[]{:S(2)}, u32[]{:S(2)}) async-start(bf16[4,128,1280]{2,1,0:T(8,128)(2,1)} %after.27), calls=%async_computation.2 | async-start | bytes 2621440 | tf_op jit(solution)/shard_map/all_to_all | solution.py:467
  106.0 44.6 %collective-permute-start = (bf16[4,128,1280]{2,1,0:T(8,128)(2,1)}, bf16[4,128,1280]{2,1,0:T(8,128)(2,1)}, u32[]{:S(2)}, u32[]{:S(2)}) collective-permute-start(bf16[4,128,1280]{2,1,0:T(8,128)(2,1)} %all_to_all.85.refs_1_), channel_id=1, source_target_pairs={{0,4},{4,0},{1,5},{5,1},{2,6},{6,2},{3,7},{7,3},{8,12},{12,8},{9,1... | collective-permute-start | bytes 3932168 | tf_op jit(solution)/shard_map/ppermute | solution.py:451
  183.7 109.9 %all-gather.12.cloned.1.call-start = ((), (), s32[]{:S(2)}) async-start(), calls=%async_computation.26 | async-start | bytes 2621440 | tf_op jit(solution)/shard_map/all_gather | solution.py:493
  229.6 47.9 %collective-permute-start.4 = (bf16[4,128,2048]{2,1,0:T(8,128)(2,1)}, bf16[4,128,2048]{2,1,0:T(8,128)(2,1)}, u32[]{:S(2)}, u32[]{:S(2)}) collective-permute-start(bf16[4,128,2048]{2,1,0:T(8,128)(2,1)} %fusion.15), channel_id=1, source_target_pairs={{0,2},{1,3},{2,0},{3,1},{4,6},{5,7},{6,4},{7,5},{8,10},{9,11},{10,... | collective-permute-start | bytes 6291464 | tf_op jit(solution)/shard_map/ppermute | solution.py:531
  230.9 62.6 %collective-permute-start.5 = (bf16[4,128,1408]{2,1,0:T(8,128)(2,1)}, bf16[4,128,1408]{2,1,0:T(8,128)(2,1)S(1)}, u32[]{:S(2)}, u32[]{:S(2)}) collective-permute-start(bf16[4,128,1408]{2,1,0:T(8,128)(2,1)} %all-to-all-done.4.refs_2_.refs_1_), channel_id=1, source_target_pairs={{0,4},{4,0},{1,5},{5,1},{2,6},{6,2},{3,7},{7,3},{8,12},{12,8},{9,1... | collective-permute-start | bytes 4325384 | tf_op jit(solution)/shard_map/ppermute | solution.py:451
  232.4 63.3 %all-to-all-start.5 = ((bf16[4,128,1408]{2,1,0:T(8,128)(2,1)}), bf16[4,128,1408]{2,1,0:T(8,128)(2,1)S(1)}, u32[]{:S(2)}, u32[]{:S(2)}) async-start(bf16[4,128,1408]{2,1,0:T(8,128)(2,1)} %after.33), calls=%async_computation.6 | async-start | bytes 2883584 | tf_op jit(solution)/shard_map/all_to_all | solution.py:467
  236.2 130.8 %reduce-scatter.5.cloned.1.call-start = ((), (), s32[]{:S(2)}) async-start(), calls=%async_computation.20 | async-start | bytes 2621440 | tf_op jit(solution)/shard_map/reduce_scatter | solution.py:655
  296.8 70.2 %all-to-all-start.6 = ((bf16[4,128,1408]{2,1,0:T(8,128)(2,1)}), bf16[4,128,1408]{2,1,0:T(8,128)(2,1)S(1)}, u32[]{:S(2)}, u32[]{:S(2)}) async-start(bf16[4,128,1408]{2,1,0:T(8,128)(2,1)} %after.34), calls=%async_computation.7 | async-start | bytes 2883584 | tf_op jit(solution)/shard_map/all_to_all | solution.py:467
  300.4 200.1 %all-gather.8.cloned.1.call-start = ((), (), s32[]{:S(2)}) async-start(), calls=%async_computation.21 | async-start | bytes 9469952 | tf_op jit(solution)/shard_map/all_gather | solution.py:666
  300.5 47.7 %collective-permute-start.7 = (bf16[4,128,2048]{2,1,0:T(8,128)(2,1)}, bf16[4,128,2048]{2,1,0:T(8,128)(2,1)}, u32[]{:S(2)}, u32[]{:S(2)}) collective-permute-start(bf16[4,128,2048]{2,1,0:T(8,128)(2,1)} %bitcast.217), channel_id=1, source_target_pairs={{0,2},{1,3},{2,0},{3,1},{4,6},{5,7},{6,4},{7,5},{8,10},{9,11},{10,... | collective-permute-start | bytes 6291464 | tf_op jit(solution)/shard_map/ppermute | solution.py:494
  302.0 46.2 %collective-permute-start.6 = (bf16[4,128,1408]{2,1,0:T(8,128)(2,1)}, bf16[4,128,1408]{2,1,0:T(8,128)(2,1)}, u32[]{:S(2)}, u32[]{:S(2)}) collective-permute-start(bf16[4,128,1408]{2,1,0:T(8,128)(2,1)} %copy-done.12), channel_id=1, source_target_pairs={{0,4},{4,0},{1,5},{5,1},{2,6},{6,2},{3,7},{7,3},{8,12},{12,8},{9,1... | collective-permute-start | bytes 4325384 | tf_op jit(solution)/shard_map/ppermute | solution.py:451
  385.8 80.4 %collective-permute-start.9 = (bf16[4,2,128,2048]{3,2,1,0:T(8,128)(2,1)}, bf16[4,2,128,2048]{3,2,1,0:T(8,128)(2,1)}, u32[]{:S(2)}, u32[]{:S(2)}) collective-permute-start(bf16[4,2,128,2048]{3,2,1,0:T(8,128)(2,1)} %bitcast_dynamic-update-slice_fusion.2), channel_id=1, source_target_pairs={{0,1},{1,0},{2,3},{3,2},{4,5},{5,4},{6,7},{7,6},{8,9},{9,8},{10,11... | collective-permute-start | bytes 12582920 | tf_op jit(solution)/shard_map/ppermute | solution.py:500
  389.6 63.5 %all-to-all-start.7 = ((bf16[4,128,1408]{2,1,0:T(8,128)(2,1)}), bf16[4,128,1408]{2,1,0:T(8,128)(2,1)}, u32[]{:S(2)}, u32[]{:S(2)}) async-start(bf16[4,128,1408]{2,1,0:T(8,128)(2,1)} %after.35), calls=%async_computation.8 | async-start | bytes 2883584 | tf_op jit(solution)/shard_map/all_to_all | solution.py:467
  398.5 60.7 %collective-permute-start.8 = (bf16[4,128,1408]{2,1,0:T(8,128)(2,1)S(1)}, bf16[4,128,1408]{2,1,0:T(8,128)(2,1)S(1)}, u32[]{:S(2)}, u32[]{:S(2)}) collective-permute-start(bf16[4,128,1408]{2,1,0:T(8,128)(2,1)S(1)} %copy-done.15), channel_id=1, source_target_pairs={{0,4},{4,0},{1,5},{5,1},{2,6},{6,2},{3,7},{7,3},{8,12},{12,8},{9,1... | collective-permute-start | bytes 4325384 | tf_op jit(solution)/shard_map/ppermute | solution.py:451
  453.1 45.9 %all-to-all-start.8 = ((bf16[4,128,1408]{2,1,0:T(8,128)(2,1)}), bf16[4,128,1408]{2,1,0:T(8,128)(2,1)}, u32[]{:S(2)}, u32[]{:S(2)}) async-start(bf16[4,128,1408]{2,1,0:T(8,128)(2,1)} %after.37), calls=%async_computation.9 | async-start | bytes 2883584 | tf_op jit(solution)/shard_map/all_to_all | solution.py:467
  499.0 61.9 %collective-permute-start.11 = (bf16[4,128,1408]{2,1,0:T(8,128)(2,1)}, bf16[4,128,1408]{2,1,0:T(8,128)(2,1)}, u32[]{:S(2)}, u32[]{:S(2)}) collective-permute-start(bf16[4,128,1408]{2,1,0:T(8,128)(2,1)} %all-to-all-done.8), channel_id=1, source_target_pairs={{0,4},{4,0},{1,5},{5,1},{2,6},{6,2},{3,7},{7,3},{8,12},{12,8},{9,1... | collective-permute-start | bytes 4325384 | tf_op jit(solution)/shard_map/ppermute | solution.py:451
  556.9 67.4 %collective-permute-start.13 = (bf16[2,256,1408]{2,1,0:T(8,128)(2,1)}, bf16[2,256,1408]{2,1,0:T(8,128)(2,1)}, u32[]{:S(2)}, u32[]{:S(2)}) collective-permute-start(bf16[2,256,1408]{2,1,0:T(8,128)(2,1)} %dynamic-slice_bitcast_fusion.4), channel_id=1, source_target_pairs={{0,4},{4,0},{1,5},{5,1},{2,6},{6,2},{3,7},{7,3},{8,12},{12,8},{9,1... | collective-permute-start | bytes 4325384 | tf_op jit(solution)/shard_map/ppermute | solution.py:451
  636.1 50.8 %collective-permute-start.15 = (bf16[4,128,2176]{2,1,0:T(8,128)(2,1)}, bf16[4,128,2176]{2,1,0:T(8,128)(2,1)}, u32[]{:S(2)}, u32[]{:S(2)}) collective-permute-start(bf16[4,128,2176]{2,1,0:T(8,128)(2,1)} %fusion.10.refs_1_), channel_id=1, source_target_pairs={{0,2},{1,3},{2,0},{3,1},{4,6},{5,7},{6,4},{7,5},{8,10},{9,11},{10,... | collective-permute-start | bytes 6684680 | tf_op jit(solution)/shard_map/ppermute | solution.py:531
  637.6 97.3 %all-to-all-start.9 = ((bf16[4,256,1408]{2,1,0:T(8,128)(2,1)}), bf16[4,256,1408]{2,1,0:T(8,128)(2,1)S(1)}, u32[]{:S(2)}, u32[]{:S(2)}) async-start(bf16[4,256,1408]{2,1,0:T(8,128)(2,1)} %after.43), calls=%async_computation.11 | async-start | bytes 5767168 | tf_op jit(solution)/shard_map/all_to_all | solution.py:467
  641.3 102.2 %reduce-scatter.7.cloned.1.call-start = ((), (), s32[]{:S(2)}) async-start(), calls=%async_computation.22 | async-start | bytes 2785280 | tf_op jit(solution)/shard_map/reduce_scatter | solution.py:719
  662.9 67.0 %collective-permute-start.17 = (bf16[4,256,1408]{2,1,0:T(8,128)(2,1)}, bf16[4,256,1408]{2,1,0:T(8,128)(2,1)}, u32[]{:S(2)}, u32[]{:S(2)}) collective-permute-start(bf16[4,256,1408]{2,1,0:T(8,128)(2,1)} %dynamic-slice_bitcast_fusion.2), channel_id=1, source_target_pairs={{0,4},{4,0},{1,5},{5,1},{2,6},{6,2},{3,7},{7,3},{8,12},{12,8},{9,1... | collective-permute-start | bytes 8650760 | tf_op jit(solution)/shard_map/ppermute | solution.py:451
  692.1 183.7 %all-gather.10.cloned.1.call-start = ((), (), s32[]{:S(2)}) async-start(), calls=%async_computation.23 | async-start | bytes 8912896 | tf_op jit(solution)/shard_map/all_gather | solution.py:763
  754.6 65.1 %collective-permute-start.19 = (bf16[4,256,1408]{2,1,0:T(8,128)(2,1)}, bf16[4,256,1408]{2,1,0:T(8,128)(2,1)}, u32[]{:S(2)}, u32[]{:S(2)}) collective-permute-start(bf16[4,256,1408]{2,1,0:T(8,128)(2,1)} %dynamic-slice_bitcast_fusion.1), channel_id=1, source_target_pairs={{0,4},{4,0},{1,5},{5,1},{2,6},{6,2},{3,7},{7,3},{8,12},{12,8},{9,1... | collective-permute-start | bytes 8650760 | tf_op jit(solution)/shard_map/ppermute | solution.py:451
  757.2 112.6 %all-to-all-start.10 = ((bf16[4,256,1408]{2,1,0:T(8,128)(2,1)}), bf16[4,256,1408]{2,1,0:T(8,128)(2,1)S(1)}, u32[]{:S(2)}, u32[]{:S(2)}) async-start(bf16[4,256,1408]{2,1,0:T(8,128)(2,1)} %after.44), calls=%async_computation.12 | async-start | bytes 5767168 | tf_op jit(solution)/shard_map/all_to_all | solution.py:467
  770.4 65.5 %collective-permute-start.18 = (bf16[4,128,2048]{2,1,0:T(8,128)(2,1)S(1)}, bf16[4,128,2048]{2,1,0:T(8,128)(2,1)S(1)}, u32[]{:S(2)}, u32[]{:S(2)}) collective-permute-start(bf16[4,128,2048]{2,1,0:T(8,128)(2,1)S(1)} %dynamic-slice_bitcast_fusion.3), channel_id=1, source_target_pairs={{0,2},{1,3},{2,0},{3,1},{4,6},{5,7},{6,4},{7,5},{8,10},{9,11},{10,... | collective-permute-start | bytes 6291464 | tf_op jit(solution)/shard_map/ppermute | solution.py:509
  871.4 38.9 %all-to-all-start.11 = ((bf16[4,128,1408]{2,1,0:T(8,128)(2,1)}), bf16[4,128,1408]{2,1,0:T(8,128)(2,1)}, u32[]{:S(2)}, u32[]{:S(2)}) async-start(bf16[4,128,1408]{2,1,0:T(8,128)(2,1)} %after.47), calls=%async_computation.14 | async-start | bytes 2883584 | tf_op jit(solution)/shard_map/all_to_all | solution.py:467
  875.7 105.6 %reduce-scatter.9.cloned.1.call-start = ((), (), s32[]{:S(2)}) async-start(), calls=%async_computation.24 | async-start | bytes 2621440 | tf_op jit(solution)/shard_map/reduce_scatter | solution.py:766
  910.4 70.9 %all-to-all-start.12 = ((bf16[4,128,1408]{2,1,0:T(8,128)(2,1)}), bf16[4,128,1408]{2,1,0:T(8,128)(2,1)S(1)}, u32[]{:S(2)}, u32[]{:S(2)}) async-start(bf16[4,128,1408]{2,1,0:T(8,128)(2,1)} %after.49), calls=%async_computation.15 | async-start | bytes 2883584 | tf_op jit(solution)/shard_map/all_to_all | solution.py:467
  913.9 119.6 %reduce-scatter.11.cloned.1.call-start = ((), (), s32[]{:S(2)}) async-start(), calls=%async_computation.25 | async-start | bytes 2785280 | tf_op jit(solution)/shard_map/reduce_scatter | solution.py:803
  925.2 57.7 %collective-permute-start.22 = (bf16[4,128,2176]{2,1,0:T(8,128)(2,1)}, bf16[4,128,2176]{2,1,0:T(8,128)(2,1)}, u32[]{:S(2)}, u32[]{:S(2)}) collective-permute-start(bf16[4,128,2176]{2,1,0:T(8,128)(2,1)} %get-tuple-element.85.wait_ref), channel_id=1, source_target_pairs={{0,2},{1,3},{2,0},{3,1},{4,6},{5,7},{6,4},{7,5},{8,10},{9,11},{10,... | collective-permute-start | bytes 6684680 | tf_op jit(solution)/shard_map/ppermute | solution.py:531
  1022.0 66.4 %all-to-all-start.14 = ((bf16[4,256,1280]{2,1,0:T(8,128)(2,1)}), bf16[4,256,1280]{2,1,0:T(8,128)(2,1)}, u32[]{:S(2)}, u32[]{:S(2)}) async-start(bf16[4,256,1280]{2,1,0:T(8,128)(2,1)} %after.51), calls=%async_computation.18 | async-start | bytes 5242880 | tf_op jit(solution)/shard_map/all_to_all | solution.py:467
  (48 other events, 604.1 us)
Sparse Core Ops, SparseCore 0:
  14.0 117.2 all-gather.5
  371.4 119.5 all-gather.7
  747.9 122.1 all-gather.9
Sparse Core Ops, SparseCore 1:
  219.4 74.1 all-gather.11
  296.3 67.9 reduce-scatter.4
  692.2 51.2 reduce-scatter.6
  910.5 66.8 reduce-scatter.8
  987.3 46.3 reduce-scatter.10

commit v5 on v4

--- a/solution.py
+++ b/solution.py
@@ -391,7 +391,7 @@
         second[...] = refs[kind][:, cut:].astype(bf16)
 
 
-def join_kernel(piece_ref, *outs):
+def join_kernel(piece_ref, wait_ref, *outs):
     for head in range(piece_ref.shape[0]):
         place = 0
         for ref in outs:
@@ -503,8 +503,9 @@
             full = lax.dynamic_update_slice(full, piece[:, :, None], (0, 0, place, 0, 0))
         return full.reshape(-1, by_zz.shape[-1])
 
-    def fold(value, axis, place, pairs):
-        sent = lax.dynamic_index_in_dim(value, 1 - place, axis, keepdims=False)
+    def fold(value, axis, place, pairs, sent=None):
+        if sent is None:
+            sent = lax.dynamic_index_in_dim(value, 1 - place, axis, keepdims=False)
         kept = lax.dynamic_index_in_dim(value, place, axis, keepdims=False)
         came = lax.ppermute(sent, "tensor", pairs)
         return (kept.astype(f32) + came.astype(f32)).astype(bf16)
@@ -728,7 +729,9 @@
     up_back = [exchange(after(up_sum[:, :cut], gate_back))]
     up_back.append(exchange(after(up_sum[:, cut:], up_back[0])))
     part_ffn = dot_nt(after(act, up_dw, line2), w_down).astype(bf16)
-    core_ffn = fold(part_ffn.reshape(zs, 2, 2, rows, dim), 2, core, across_core)
+    by_rows = part_ffn.reshape(zs, 2, 2, rows, dim)
+    sent_ffn = lax.dynamic_index_in_dim(by_rows, 1 - core, 2, keepdims=False)
+    core_ffn = fold(by_rows, 2, core, across_core, sent_ffn)
     by_line = fold(after(core_ffn, gate_sum), 1, line, across_line)
 
     def norm_back(route_at, rsb, wide_rows, base, gain, router, gate, gate_at, outs, name, *waited):
@@ -758,7 +761,7 @@
     zero = jnp.zeros((1,), jnp.int32)
     parts_ffn, middle_grad, att_cot = norm_back(
         7, sum_back2, middle, cotangent, gain2, router2, gate2, zero, [f32, bf16], "mid_back",
-        down_back, gate_sum, part_ffn,
+        down_back, gate_sum, sent_ffn,
     )
     group_att_cot = lax.all_gather(att_cot, GROUP, axis=0, tiled=True)
 
@@ -802,14 +805,6 @@
     line1 = sum_line(core1[0], after(core1[1], *att_sent, att_came[0], mixed_rows, up_back[1]))
     sum_back1 = lax.psum_scatter(line1, "zz", scatter_dimension=0, tiled=False)
     att_back = exchange(after(att_sum, up_back[1]))
-    query_grad, kv_grad, out_grad = pl.pallas_call(
-        join_kernel,
-        in_specs=[vmem],
-        out_specs=[vmem] * 3,
-        out_shape=[shape(a.shape, f32) for a in (query_maps, kv_maps, out_maps)],
-        compiler_params=params(),
-        name="join",
-    )(att_back)
     ffn_out = jnp.concatenate([v.astype(f32) for v in (gate_back, jnp.concatenate(up_back, axis=1), down_back)], axis=0)
 
     mixed = (middle + mixed_rows.astype(f32)).astype(bf16)
@@ -822,9 +817,32 @@
     used = EXPERTS + 1
     parts = jnp.concatenate([parts_ffn[:used], parts_att[:used]], axis=0)
     parts = parts.reshape(2 * used, devices, -1).transpose(1, 0, 2).reshape(devices, -1)
-    parts = jnp.sum(lax.all_to_all(parts, ALL, 0, 0, tiled=True), axis=0).reshape(2, used, -1)
+    if xs == 2:
+        parts = parts.reshape(zs, xs, 2, 2, -1)
+
+        def halve(v, axis, place, move):
+            pick = lambda at: lax.dynamic_index_in_dim(v, at, axis, keepdims=False)
+            return pick(place) + move(pick(1 - place))
+
+        parts = halve(parts, 3, core, lambda v: lax.ppermute(v, "tensor", across_core))
+        parts = halve(parts, 2, line, lambda v: lax.ppermute(v, "tensor", across_line))
+        parts = halve(parts, 1, xx, lambda v: shift(v, "xx", 1, 2))
+        turn = lambda k: lax.dynamic_index_in_dim(parts, (zz + k) % zs, 0, keepdims=False)
+        came = [shift(turn(k), "zz", k, zs) for k in range(1, zs)]
+        parts = functools.reduce(lambda a, b: a + b, came, turn(0))
+    else:
+        parts = jnp.sum(lax.all_to_all(parts, ALL, 0, 0, tiled=True), axis=0)
+    parts = parts.reshape(2, used, -1)
     ffn_router_grad, gain2_grad = parts[0, :EXPERTS].T, parts[0, EXPERTS]
     att_router_grad, gain1_grad = parts[1, :EXPERTS].T, parts[1, EXPERTS]
+    query_grad, kv_grad, out_grad = pl.pallas_call(
+        join_kernel,
+        in_specs=[vmem, anywhere],
+        out_specs=[vmem] * 3,
+        out_shape=[shape(a.shape, f32) for a in (query_maps, kv_maps, out_maps)],
+        compiler_params=params(),
+        name="join",
+    )(att_back, parts)
     return (
         mixed,
         input_grad,

time: 1120 us -> 1110 us (level)
  waiting for transfers between devices: 473 us -> 461 us
    all_to_all x12, waiting for transfers between devices: 206 us -> 165 us  [exchange(): return lax.all_to_all(value, 'zz', 0, 0, tiled=True)]
    ppermute x14 -> x18, waiting for transfers between devices: 110 us -> 146 us  [shift(): lax.ppermute(value, axis, [(i, (i + step) % size) for i in range(size)])]
    ppermute x14 -> x18, starting transfers between devices: 18.2 us -> 25.9 us  [shift(): lax.ppermute(value, axis, [(i, (i + step) % size) for i in range(size)])]
    unnamed x76 -> x83, local copies, waits for them, and re-layouts: 24.2 us -> 25.5 us
  transfers between devices with their start and end apart: 45 -> 50, of which waited for: 28 -> 30; matrix products, arithmetic and copies ran while one was open for 21% -> 21% of each run, Pallas kernels for 17% -> 17%
where the time goes in v5:
time: 1110 us; the launch traced here: 1100 us
  waiting for transfers between devices  461 us (42%)
  Pallas kernels  203 us (18%)
  local copies, waits for them, and re-layouts  120 us (11%)
  starting transfers between devices  82.6 us (7%)
  blocking collectives  77.8 us (7%)
  matrix products  70.8 us (6%)
  other arithmetic  69.7 us (6%)
  between operations  16.6 us (1%)
    all_to_all x12, waiting for transfers between devices, exchange(): return lax.all_to_all(value, 'zz', 0, 0, tiled=True)  165 us
    ppermute x18, waiting for transfers between devices, shift(): lax.ppermute(value, axis, [(i, (i + step) % size) for i in range(size)])  146 us
    ppermute x3, waiting for transfers between devices, sum_line(): return add(kept, lax.ppermute(sent, 'tensor', across_line))  64.5 us
    all_to_all x1, blocking collectives, exchange(): return lax.all_to_all(value, 'zz', 0, 0, tiled=True)  63 us
    dot_general x3, matrix products, dot_tn(): lax.dot_general(a, b, (((0,), (0,)), ((), ())), preferred_element_type=f32)  53.6 us
    all_to_all x12, starting transfers between devices, exchange(): return lax.all_to_all(value, 'zz', 0, 0, tiled=True)  48 us
    ppermute x1, waiting for transfers between devices, gather_line(): return (by_zz, lax.ppermute(by_zz, 'tensor', across_line))  42.1 us
    pallas_call x1, Pallas kernels, local(): pl.pallas_call(ffn_back_kernel, grid=steps, in_specs=[smem, rows_of(width...  34.3 us
  transfers between devices with their start and end apart: 50, of which 30 were waited for; matrix products, arithmetic and copies ran while one was open for 21% of the time, Pallas kernels for 17%

profile of v5, /device:TPU:0, one launch (start us, length us, event | category | flops | bytes accessed | tf_op | source)
XLA Modules:
  0.0 1102.1 jit_solution(17922436946806388543)
XLA Ops:
  16.3 14.8 %all_to_all.74 = f32[32,1,640]{2,1,0:T(1,128)S(1)} all-to-all(f32[32,1,640]{2,1,0:T(1,128)S(1)} %copy.109), channel_id=1, replica_groups=mesh['zz'=4,'xx'=2,'tensor'=4] {'zz','xx','tensor'}, dimensions={0} | all-to-all | bytes 163840 | tf_op jit(solution)/shard_map/all_to_all | solution.py:572
  36.6 63.0 %all_to_all.75.refs_1_ = bf16[4,128,1280]{2,1,0:T(8,128)(2,1)} all-to-all(bf16[4,128,1280]{2,1,0:T(8,128)(2,1)} %get-tuple-element.46.refs_3_), channel_id=1, replica_groups=mesh['zz'=4,'xx'=2,'tensor'=4] {'zz'}, dimensions={0} | all-to-all | bytes 2621440 | tf_op jit(solution)/shard_map/all_to_all | solution.py:467
  110.1 9.2 cast.1
  119.3 19.8 %all-to-all-done.2.refs_1_ = bf16[4,128,1280]{2,1,0:T(8,128)(2,1)S(1)} async-done(((bf16[4,128,1280]{2,1,0:T(8,128)(2,1)}), bf16[4,128,1280]{2,1,0:T(8,128)(2,1)S(1)}, u32[]{:S(2)}, u32[]{:S(2)}) %all-to-all-start.2) | async-done | bytes 1310752 | tf_op jit(solution)/shard_map/all_to_all | solution.py:467
  154.3 20.3 %collective-permute-done.1 = bf16[4,128,1280]{2,1,0:T(8,128)(2,1)S(1)} collective-permute-done((bf16[4,128,1280]{2,1,0:T(8,128)(2,1)}, bf16[4,128,1280]{2,1,0:T(8,128)(2,1)S(1)}, u32[]{:S(2)}, u32[]{:S(2)}) %collective-permute-start.1) | collective-permute-done | bytes 1310752 | tf_op jit(solution)/shard_map/ppermute | solution.py:451
  185.2 30.4 %att_fwd.1 = (bf16[2,4,128,2048]{3,2,1,0:T(8,128)(2,1)}, bf16[2,4,128,2048]{3,2,1,0:T(8,128)(2,1)}, bf16[2048,2048]{1,0:T(8,128)(2,1)}, bf16[2048,768]{1,0:T(8,128)(2,1)}, f32[2048,128]{1,0:T(8,128)}) custom-call(s32[1]{0:T(128)} %bitcast.core_ref, bf16[2048,2176]{1,0:T(8,128)(2,1)} %all-gather.6.cloned.1.call-done.tok_ref.side_ref, ...), custom_call_target="tpu_custom_call" | custom-call | flops 199999995904 | bytes 1000000 | tf_op jit(solution)/shard_map/att_fwd/pallas_call | solution.py:637
  236.4 41.1 %collective-permute-done.4 = bf16[4,128,2048]{2,1,0:T(8,128)(2,1)} collective-permute-done((bf16[4,128,2048]{2,1,0:T(8,128)(2,1)}, bf16[4,128,2048]{2,1,0:T(8,128)(2,1)}, u32[]{:S(2)}, u32[]{:S(2)}) %collective-permute-start.4) | collective-permute-done | bytes 2097184 | tf_op jit(solution)/shard_map/ppermute | solution.py:532
  283.1 10.4 all-gather.12.cloned.1.call-done
  306.1 42.1 %collective-permute-done.7.refs_2_ = bf16[4,128,2048]{2,1,0:T(8,128)(2,1)} collective-permute-done((bf16[4,128,2048]{2,1,0:T(8,128)(2,1)}, bf16[4,128,2048]{2,1,0:T(8,128)(2,1)}, u32[]{:S(2)}, u32[]{:S(2)}) %collective-permute-start.7) | collective-permute-done | bytes 2097184 | tf_op jit(solution)/shard_map/ppermute | solution.py:494
  348.1 18.9 %all-to-all-done.6.refs_0_.refs_1_ = bf16[4,128,1408]{2,1,0:T(8,128)(2,1)S(1)} async-done(((bf16[4,128,1408]{2,1,0:T(8,128)(2,1)}), bf16[4,128,1408]{2,1,0:T(8,128)(2,1)S(1)}, u32[]{:S(2)}, u32[]{:S(2)}) %all-to-all-start.6) | async-done | bytes 1441824 | tf_op jit(solution)/shard_map/all_to_all | solution.py:467
  413.1 40.0 %all-to-all-done.7.refs_1_ = bf16[4,128,1408]{2,1,0:T(8,128)(2,1)} async-done(((bf16[4,128,1408]{2,1,0:T(8,128)(2,1)}), bf16[4,128,1408]{2,1,0:T(8,128)(2,1)}, u32[]{:S(2)}, u32[]{:S(2)}) %all-to-all-start.7) | async-done | bytes 1441824 | tf_op jit(solution)/shard_map/all_to_all | solution.py:467
  470.9 20.1 %collective-permute-done.10 = bf16[4,128,1408]{2,1,0:T(8,128)(2,1)S(1)} collective-permute-done((bf16[4,128,1408]{2,1,0:T(8,128)(2,1)}, bf16[4,128,1408]{2,1,0:T(8,128)(2,1)S(1)}, u32[]{:S(2)}, u32[]{:S(2)}) %collective-permute-start.10) | collective-permute-done | bytes 1441824 | tf_op jit(solution)/shard_map/ppermute | solution.py:451
  500.5 33.7 %ffn_fwd.1 = (bf16[2048,1408]{1,0:T(8,128)(2,1)}, bf16[2048,1408]{1,0:T(8,128)(2,1)}, bf16[2048,1408]{1,0:T(8,128)(2,1)}) custom-call(s32[1]{0:T(128)} %bitcast.23.where_ref, bf16[2048,2176]{1,0:T(8,128)(2,1)} %all-gather.8.cloned.1.call-done.x_ref.side_ref, bf16[2048,1408]{1,0:T(8,128)(2,1)} %bitcast.30.wg_ref, bf16[2048,1408]{1,0:T(8,128)(2,1)} %bitcast.37.wu_ref), custom_call_target="tpu_custom_call" | custom-call | flops 199999995904 | bytes 1000000 | tf_op jit(solution)/shard_map/ffn_fwd/pallas_call | solution.py:676
  534.2 17.2 %convolution_convert_fusion.3.wait_ref = bf16[2048,1408]{1,0:T(8,128)(2,1)S(1)} fusion(bf16[2048,2048]{1,0:T(8,128)(2,1)} %bitcast.45.c_ref, bf16[2048,1408]{1,0:T(8,128)(2,1)} %get-tuple-element.56.refs_1_.refs_0_), kind=kOutput, calls=%fused_computation.6 | convolution fusion | flops 11814043648 | bytes 19922944 | tf_op jit(solution)/shard_map/dot_general | solution.py:32
  563.4 26.1 %ffn_act.1 = (bf16[2048,1408]{1,0:T(8,128)(2,1)}, bf16[2048,1408]{1,0:T(8,128)(2,1)}, bf16[2048,128]{1,0:T(8,128)(2,1)}) custom-call(s32[1]{0:T(128)} %bitcast.23.where_ref, bf16[2048,2176]{1,0:T(8,128)(2,1)} %all-gather.8.cloned.1.call-done.x_ref.side_ref, bf16[2048,1408]{1,0:T(8,128)(2,1)} %get-tuple-element.57.gate_ref, ...), custom_call_target="tpu_custom_call" | custom-call | flops 199999995904 | bytes 1000000 | tf_op jit(solution)/shard_map/ffn_act/pallas_call | solution.py:693
  589.9 34.3 %ffn_back.1 = (bf16[2,4,128,2176]{3,2,1,0:T(8,128)(2,1)}, bf16[2,4,128,2176]{3,2,1,0:T(8,128)(2,1)}) custom-call(s32[1]{0:T(128)} %bitcast.core_ref, bf16[2048,1408]{1,0:T(8,128)(2,1)} %get-tuple-element.62.gg_ref.refs_0_, bf16[2048,1408]{1,0:T(8,128)(2,1)} %get-tuple-element.61.ug_ref.refs_0_, bf16[2048,128]{1,0:T(8,128)(2,1)} %get-tuple-element.63.part_ref, ...), custom_call_target="tpu_custom_call" | custom-call | flops 199999995904 | bytes 1000000 | tf_op jit(solution)/shard_map/ffn_back/pallas_call | solution.py:708
  641.3 17.4 %convolution_convert_fusion.2.refs_1_ = bf16[2048,1408]{1,0:T(8,128)(2,1)S(1)} fusion(bf16[2048,1408]{1,0:T(8,128)(2,1)} %after.39, bf16[2048,2176]{1,0:T(8,128)(2,1)} %all-gather.8.cloned.1.call-done.x_ref.side_ref), kind=kOutput, calls=%fused_computation.5 | convolution fusion | flops 11814043648 | bytes 19922944 | tf_op jit(solution)/shard_map/dot_general | solution.py:32
  663.5 23.4 %collective-permute-done.15 = bf16[4,128,2176]{2,1,0:T(8,128)(2,1)} collective-permute-done((bf16[4,128,2176]{2,1,0:T(8,128)(2,1)}, bf16[4,128,2176]{2,1,0:T(8,128)(2,1)}, u32[]{:S(2)}, u32[]{:S(2)}) %collective-permute-start.15) | collective-permute-done | bytes 2228256 | tf_op jit(solution)/shard_map/ppermute | solution.py:532
  692.1 19.1 %convolution_convert_fusion.1.refs_1_ = bf16[2048,1408]{1,0:T(8,128)(2,1)} fusion(bf16[2048,1408]{1,0:T(8,128)(2,1)} %after.40, bf16[2048,2176]{1,0:T(8,128)(2,1)} %all-gather.8.cloned.1.call-done.x_ref.side_ref), kind=kOutput, calls=%fused_computation.4 | convolution fusion | flops 11814043648 | bytes 19922944 | tf_op jit(solution)/shard_map/dot_general | solution.py:32
  711.2 17.2 %convolution_convert_fusion = bf16[2048,2048]{1,0:T(8,128)(2,1)S(1)} fusion(bf16[2048,1408]{1,0:T(8,128)(2,1)} %after.41, bf16[2048,1408]{1,0:T(8,128)(2,1)} %bitcast.54.wd_ref), kind=kOutput, calls=%fused_computation.3 | convolution fusion | flops 11815354368 | bytes 19922944 | tf_op jit(solution)/shard_map/dot_general | solution.py:28
  757.5 7.8 fusion.refs_0_
  767.6 49.3 %collective-permute-done.19 = bf16[4,256,1408]{2,1,0:T(8,128)(2,1)} collective-permute-done((bf16[4,256,1408]{2,1,0:T(8,128)(2,1)}, bf16[4,256,1408]{2,1,0:T(8,128)(2,1)}, u32[]{:S(2)}, u32[]{:S(2)}) %collective-permute-start.19) | collective-permute-done | bytes 2883616 | tf_op jit(solution)/shard_map/ppermute | solution.py:451
  830.0 39.8 %all-to-all-done.10.refs_1_ = bf16[4,256,1408]{2,1,0:T(8,128)(2,1)S(1)} async-done(((bf16[4,256,1408]{2,1,0:T(8,128)(2,1)}), bf16[4,256,1408]{2,1,0:T(8,128)(2,1)S(1)}, u32[]{:S(2)}, u32[]{:S(2)}) %all-to-all-start.10) | async-done | bytes 2883616 | tf_op jit(solution)/shard_map/all_to_all | solution.py:467
  875.8 30.2 %att_bwd.1 = (bf16[2,4,128,2176]{3,2,1,0:T(8,128)(2,1)}, bf16[2,4,128,2176]{3,2,1,0:T(8,128)(2,1)}, bf16[2048,768]{1,0:T(8,128)(2,1)}, bf16[2048,512]{1,0:T(8,128)(2,1)}) custom-call(s32[1]{0:T(128)} %bitcast.core_ref, bf16[2048,2048]{1,0:T(8,128)(2,1)} %after.45.refs_1_.c_ref, bf16[2048,1280]{1,0:T(8,128)(2,1)} %bitcast.16.w_ref, ...), custom_call_target="tpu_custom_call" | custom-call | flops 199999995904 | bytes 1000000 | tf_op jit(solution)/shard_map/att_bwd/pallas_call | solution.py:772
  918.3 6.9 fusion.12
  926.7 16.6 %att_grad.1 = bf16[2048,1280]{1,0:T(8,128)(2,1)} custom-call(bf16[2048,2048]{1,0:T(8,128)(2,1)} %get-tuple-element.72.x_ref, bf16[2048,2048]{1,0:T(8,128)(2,1)} %after.45.refs_1_.c_ref, bf16[2048,768]{1,0:T(8,128)(2,1)} %get-tuple-element.73.grad_ref, bf16[2048,512]{1,0:T(8,128)(2,1)} %get-tuple-element.74.z_ref, ...), custom_call_target="tpu_custom_call" | custom-call | flops 10737418240 | bytes 25165824 | tf_op jit(solution)/shard_map/att_grad/pallas_call | solution.py:790
  950.0 31.3 %all-to-all-done.12.refs_5_.refs_1_ = bf16[4,128,1408]{2,1,0:T(8,128)(2,1)S(1)} async-done(((bf16[4,128,1408]{2,1,0:T(8,128)(2,1)}), bf16[4,128,1408]{2,1,0:T(8,128)(2,1)S(1)}, u32[]{:S(2)}, u32[]{:S(2)}) %all-to-all-start.12) | async-done | bytes 1441824 | tf_op jit(solution)/shard_map/all_to_all | solution.py:467
  989.4 27.9 %collective-permute-done.29 = bf16[2,256,1280]{2,1,0:T(8,128)(2,1)} collective-permute-done((bf16[2,256,1280]{2,1,0:T(8,128)(2,1)S(1)}, bf16[2,256,1280]{2,1,0:T(8,128)(2,1)}, u32[]{:S(2)}, u32[]{:S(2)}) %collective-permute-start.29) | collective-permute-done | bytes 1310752 | tf_op jit(solution)/shard_map/ppermute | solution.py:451
  1026.6 7.4 reduce-scatter.11.cloned.1.call-done
  1046.3 8.7 maximum_convert_fusion
  1062.1 13.4 %collective-permute-done.26 = f32[640]{0:T(1024)S(1)} collective-permute-done((f32[640]{0:T(1024)S(1)}, f32[640]{0:T(1024)S(1)}, u32[]{:S(2)}, u32[]{:S(2)}) %collective-permute-start.26) | collective-permute-done | bytes 2592 | tf_op jit(solution)/shard_map/ppermute | solution.py:451
  1075.5 13.2 %collective-permute-done.27 = f32[640]{0:T(1024)S(1)} collective-permute-done((f32[640]{0:T(1024)S(1)}, f32[640]{0:T(1024)S(1)}, u32[]{:S(2)}, u32[]{:S(2)}) %collective-permute-start.27) | collective-permute-done | bytes 2592 | tf_op jit(solution)/shard_map/ppermute | solution.py:451
  (297 shorter events, 314.4 us)
Async XLA Ops:
  8.0 177.2 %all-gather.6.cloned.1.call-start = ((), (), s32[]{:S(2)}) async-start(), calls=%async_computation.18 | async-start | bytes 9469952 | tf_op jit(solution)/shard_map/all_gather | solution.py:565
  99.6 39.6 %all-to-all-start.2 = ((bf16[4,128,1280]{2,1,0:T(8,128)(2,1)}), bf16[4,128,1280]{2,1,0:T(8,128)(2,1)S(1)}, u32[]{:S(2)}, u32[]{:S(2)}) async-start(bf16[4,128,1280]{2,1,0:T(8,128)(2,1)} %after.27), calls=%async_computation.2 | async-start | bytes 2621440 | tf_op jit(solution)/shard_map/all_to_all | solution.py:467
  106.0 44.7 %collective-permute-start = (bf16[4,128,1280]{2,1,0:T(8,128)(2,1)}, bf16[4,128,1280]{2,1,0:T(8,128)(2,1)}, u32[]{:S(2)}, u32[]{:S(2)}) collective-permute-start(bf16[4,128,1280]{2,1,0:T(8,128)(2,1)} %all_to_all.75.refs_1_), channel_id=1, source_target_pairs={{0,4},{4,0},{1,5},{5,1},{2,6},{6,2},{3,7},{7,3},{8,12},{12,8},{9,1... | collective-permute-start | bytes 3932168 | tf_op jit(solution)/shard_map/ppermute | solution.py:451
  183.6 109.9 %all-gather.12.cloned.1.call-start = ((), (), s32[]{:S(2)}) async-start(), calls=%async_computation.25 | async-start | bytes 2621440 | tf_op jit(solution)/shard_map/all_gather | solution.py:493
  229.6 47.9 %collective-permute-start.4 = (bf16[4,128,2048]{2,1,0:T(8,128)(2,1)}, bf16[4,128,2048]{2,1,0:T(8,128)(2,1)}, u32[]{:S(2)}, u32[]{:S(2)}) collective-permute-start(bf16[4,128,2048]{2,1,0:T(8,128)(2,1)} %fusion.15), channel_id=1, source_target_pairs={{0,2},{1,3},{2,0},{3,1},{4,6},{5,7},{6,4},{7,5},{8,10},{9,11},{10,... | collective-permute-start | bytes 6291464 | tf_op jit(solution)/shard_map/ppermute | solution.py:532
  230.9 62.6 %collective-permute-start.5 = (bf16[4,128,1408]{2,1,0:T(8,128)(2,1)}, bf16[4,128,1408]{2,1,0:T(8,128)(2,1)S(1)}, u32[]{:S(2)}, u32[]{:S(2)}) collective-permute-start(bf16[4,128,1408]{2,1,0:T(8,128)(2,1)} %all-to-all-done.4.refs_2_.refs_1_), channel_id=1, source_target_pairs={{0,4},{4,0},{1,5},{5,1},{2,6},{6,2},{3,7},{7,3},{8,12},{12,8},{9,1... | collective-permute-start | bytes 4325384 | tf_op jit(solution)/shard_map/ppermute | solution.py:451
  232.4 63.3 %all-to-all-start.5 = ((bf16[4,128,1408]{2,1,0:T(8,128)(2,1)}), bf16[4,128,1408]{2,1,0:T(8,128)(2,1)S(1)}, u32[]{:S(2)}, u32[]{:S(2)}) async-start(bf16[4,128,1408]{2,1,0:T(8,128)(2,1)} %after.33), calls=%async_computation.6 | async-start | bytes 2883584 | tf_op jit(solution)/shard_map/all_to_all | solution.py:467
  236.2 130.8 %reduce-scatter.5.cloned.1.call-start = ((), (), s32[]{:S(2)}) async-start(), calls=%async_computation.19 | async-start | bytes 2621440 | tf_op jit(solution)/shard_map/reduce_scatter | solution.py:656
  296.8 70.2 %all-to-all-start.6 = ((bf16[4,128,1408]{2,1,0:T(8,128)(2,1)}), bf16[4,128,1408]{2,1,0:T(8,128)(2,1)S(1)}, u32[]{:S(2)}, u32[]{:S(2)}) async-start(bf16[4,128,1408]{2,1,0:T(8,128)(2,1)} %after.34), calls=%async_computation.7 | async-start | bytes 2883584 | tf_op jit(solution)/shard_map/all_to_all | solution.py:467
  300.4 200.1 %all-gather.8.cloned.1.call-start = ((), (), s32[]{:S(2)}) async-start(), calls=%async_computation.20 | async-start | bytes 9469952 | tf_op jit(solution)/shard_map/all_gather | solution.py:667
  300.4 47.7 %collective-permute-start.7 = (bf16[4,128,2048]{2,1,0:T(8,128)(2,1)}, bf16[4,128,2048]{2,1,0:T(8,128)(2,1)}, u32[]{:S(2)}, u32[]{:S(2)}) collective-permute-start(bf16[4,128,2048]{2,1,0:T(8,128)(2,1)} %bitcast.232), channel_id=1, source_target_pairs={{0,2},{1,3},{2,0},{3,1},{4,6},{5,7},{6,4},{7,5},{8,10},{9,11},{10,... | collective-permute-start | bytes 6291464 | tf_op jit(solution)/shard_map/ppermute | solution.py:494
  302.0 46.2 %collective-permute-start.6 = (bf16[4,128,1408]{2,1,0:T(8,128)(2,1)}, bf16[4,128,1408]{2,1,0:T(8,128)(2,1)}, u32[]{:S(2)}, u32[]{:S(2)}) collective-permute-start(bf16[4,128,1408]{2,1,0:T(8,128)(2,1)} %copy-done.11), channel_id=1, source_target_pairs={{0,4},{4,0},{1,5},{5,1},{2,6},{6,2},{3,7},{7,3},{8,12},{12,8},{9,1... | collective-permute-start | bytes 4325384 | tf_op jit(solution)/shard_map/ppermute | solution.py:451
  385.8 80.4 %collective-permute-start.9 = (bf16[4,2,128,2048]{3,2,1,0:T(8,128)(2,1)}, bf16[4,2,128,2048]{3,2,1,0:T(8,128)(2,1)}, u32[]{:S(2)}, u32[]{:S(2)}) collective-permute-start(bf16[4,2,128,2048]{3,2,1,0:T(8,128)(2,1)} %bitcast_dynamic-update-slice_fusion.2), channel_id=1, source_target_pairs={{0,1},{1,0},{2,3},{3,2},{4,5},{5,4},{6,7},{7,6},{8,9},{9,8},{10,11... | collective-permute-start | bytes 12582920 | tf_op jit(solution)/shard_map/ppermute | solution.py:500
  389.6 63.5 %all-to-all-start.7 = ((bf16[4,128,1408]{2,1,0:T(8,128)(2,1)}), bf16[4,128,1408]{2,1,0:T(8,128)(2,1)}, u32[]{:S(2)}, u32[]{:S(2)}) async-start(bf16[4,128,1408]{2,1,0:T(8,128)(2,1)} %after.35), calls=%async_computation.8 | async-start | bytes 2883584 | tf_op jit(solution)/shard_map/all_to_all | solution.py:467
  398.5 60.7 %collective-permute-start.8 = (bf16[4,128,1408]{2,1,0:T(8,128)(2,1)S(1)}, bf16[4,128,1408]{2,1,0:T(8,128)(2,1)S(1)}, u32[]{:S(2)}, u32[]{:S(2)}) collective-permute-start(bf16[4,128,1408]{2,1,0:T(8,128)(2,1)S(1)} %copy-done.14), channel_id=1, source_target_pairs={{0,4},{4,0},{1,5},{5,1},{2,6},{6,2},{3,7},{7,3},{8,12},{12,8},{9,1... | collective-permute-start | bytes 4325384 | tf_op jit(solution)/shard_map/ppermute | solution.py:451
  453.1 45.9 %all-to-all-start.8 = ((bf16[4,128,1408]{2,1,0:T(8,128)(2,1)}), bf16[4,128,1408]{2,1,0:T(8,128)(2,1)}, u32[]{:S(2)}, u32[]{:S(2)}) async-start(bf16[4,128,1408]{2,1,0:T(8,128)(2,1)} %after.37), calls=%async_computation.9 | async-start | bytes 2883584 | tf_op jit(solution)/shard_map/all_to_all | solution.py:467
  499.0 61.9 %collective-permute-start.11 = (bf16[4,128,1408]{2,1,0:T(8,128)(2,1)}, bf16[4,128,1408]{2,1,0:T(8,128)(2,1)}, u32[]{:S(2)}, u32[]{:S(2)}) collective-permute-start(bf16[4,128,1408]{2,1,0:T(8,128)(2,1)} %all-to-all-done.8), channel_id=1, source_target_pairs={{0,4},{4,0},{1,5},{5,1},{2,6},{6,2},{3,7},{7,3},{8,12},{12,8},{9,1... | collective-permute-start | bytes 4325384 | tf_op jit(solution)/shard_map/ppermute | solution.py:451
  556.9 67.3 %collective-permute-start.13 = (bf16[2,256,1408]{2,1,0:T(8,128)(2,1)}, bf16[2,256,1408]{2,1,0:T(8,128)(2,1)}, u32[]{:S(2)}, u32[]{:S(2)}) collective-permute-start(bf16[2,256,1408]{2,1,0:T(8,128)(2,1)} %dynamic-slice_bitcast_fusion.4), channel_id=1, source_target_pairs={{0,4},{4,0},{1,5},{5,1},{2,6},{6,2},{3,7},{7,3},{8,12},{12,8},{9,1... | collective-permute-start | bytes 4325384 | tf_op jit(solution)/shard_map/ppermute | solution.py:451
  636.1 50.8 %collective-permute-start.15 = (bf16[4,128,2176]{2,1,0:T(8,128)(2,1)}, bf16[4,128,2176]{2,1,0:T(8,128)(2,1)}, u32[]{:S(2)}, u32[]{:S(2)}) collective-permute-start(bf16[4,128,2176]{2,1,0:T(8,128)(2,1)} %fusion.10.refs_1_), channel_id=1, source_target_pairs={{0,2},{1,3},{2,0},{3,1},{4,6},{5,7},{6,4},{7,5},{8,10},{9,11},{10,... | collective-permute-start | bytes 6684680 | tf_op jit(solution)/shard_map/ppermute | solution.py:532
  637.6 100.3 %all-to-all-start.9 = ((bf16[4,256,1408]{2,1,0:T(8,128)(2,1)}), bf16[4,256,1408]{2,1,0:T(8,128)(2,1)S(1)}, u32[]{:S(2)}, u32[]{:S(2)}) async-start(bf16[4,256,1408]{2,1,0:T(8,128)(2,1)} %after.43), calls=%async_computation.11 | async-start | bytes 5767168 | tf_op jit(solution)/shard_map/all_to_all | solution.py:467
  641.3 102.1 %reduce-scatter.7.cloned.1.call-start = ((), (), s32[]{:S(2)}) async-start(), calls=%async_computation.21 | async-start | bytes 2785280 | tf_op jit(solution)/shard_map/reduce_scatter | solution.py:720
  662.9 70.1 %collective-permute-start.17 = (bf16[4,256,1408]{2,1,0:T(8,128)(2,1)}, bf16[4,256,1408]{2,1,0:T(8,128)(2,1)}, u32[]{:S(2)}, u32[]{:S(2)}) collective-permute-start(bf16[4,256,1408]{2,1,0:T(8,128)(2,1)} %dynamic-slice_bitcast_fusion.2), channel_id=1, source_target_pairs={{0,4},{4,0},{1,5},{5,1},{2,6},{6,2},{3,7},{7,3},{8,12},{12,8},{9,1... | collective-permute-start | bytes 8650760 | tf_op jit(solution)/shard_map/ppermute | solution.py:451
  692.1 183.7 %all-gather.10.cloned.1.call-start = ((), (), s32[]{:S(2)}) async-start(), calls=%async_computation.22 | async-start | bytes 8912896 | tf_op jit(solution)/shard_map/all_gather | solution.py:766
  751.7 65.2 %collective-permute-start.19 = (bf16[4,256,1408]{2,1,0:T(8,128)(2,1)}, bf16[4,256,1408]{2,1,0:T(8,128)(2,1)}, u32[]{:S(2)}, u32[]{:S(2)}) collective-permute-start(bf16[4,256,1408]{2,1,0:T(8,128)(2,1)} %dynamic-slice_bitcast_fusion.1), channel_id=1, source_target_pairs={{0,4},{4,0},{1,5},{5,1},{2,6},{6,2},{3,7},{7,3},{8,12},{12,8},{9,1... | collective-permute-start | bytes 8650760 | tf_op jit(solution)/shard_map/ppermute | solution.py:451
  753.8 116.0 %all-to-all-start.10 = ((bf16[4,256,1408]{2,1,0:T(8,128)(2,1)}), bf16[4,256,1408]{2,1,0:T(8,128)(2,1)S(1)}, u32[]{:S(2)}, u32[]{:S(2)}) async-start(bf16[4,256,1408]{2,1,0:T(8,128)(2,1)} %after.44), calls=%async_computation.12 | async-start | bytes 5767168 | tf_op jit(solution)/shard_map/all_to_all | solution.py:467
  767.0 60.9 %collective-permute-start.18 = (bf16[4,128,2048]{2,1,0:T(8,128)(2,1)S(1)}, bf16[4,128,2048]{2,1,0:T(8,128)(2,1)S(1)}, u32[]{:S(2)}, u32[]{:S(2)}) collective-permute-start(bf16[4,128,2048]{2,1,0:T(8,128)(2,1)S(1)} %dynamic-slice_bitcast_fusion.3), channel_id=1, source_target_pairs={{0,2},{1,3},{2,0},{3,1},{4,6},{5,7},{6,4},{7,5},{8,10},{9,11},{10,... | collective-permute-start | bytes 6291464 | tf_op jit(solution)/shard_map/ppermute | solution.py:510
  871.4 39.0 %all-to-all-start.11 = ((bf16[4,128,1408]{2,1,0:T(8,128)(2,1)}), bf16[4,128,1408]{2,1,0:T(8,128)(2,1)}, u32[]{:S(2)}, u32[]{:S(2)}) async-start(bf16[4,128,1408]{2,1,0:T(8,128)(2,1)} %after.47), calls=%async_computation.14 | async-start | bytes 2883584 | tf_op jit(solution)/shard_map/all_to_all | solution.py:467
  875.7 105.7 %reduce-scatter.9.cloned.1.call-start = ((), (), s32[]{:S(2)}) async-start(), calls=%async_computation.23 | async-start | bytes 2621440 | tf_op jit(solution)/shard_map/reduce_scatter | solution.py:769
  910.4 70.9 %all-to-all-start.12 = ((bf16[4,128,1408]{2,1,0:T(8,128)(2,1)}), bf16[4,128,1408]{2,1,0:T(8,128)(2,1)S(1)}, u32[]{:S(2)}, u32[]{:S(2)}) async-start(bf16[4,128,1408]{2,1,0:T(8,128)(2,1)} %after.49), calls=%async_computation.15 | async-start | bytes 2883584 | tf_op jit(solution)/shard_map/all_to_all | solution.py:467
  914.0 120.0 %reduce-scatter.11.cloned.1.call-start = ((), (), s32[]{:S(2)}) async-start(), calls=%async_computation.24 | async-start | bytes 2785280 | tf_op jit(solution)/shard_map/reduce_scatter | solution.py:806
  925.2 57.7 %collective-permute-start.22 = (bf16[4,128,2176]{2,1,0:T(8,128)(2,1)}, bf16[4,128,2176]{2,1,0:T(8,128)(2,1)}, u32[]{:S(2)}, u32[]{:S(2)}) collective-permute-start(bf16[4,128,2176]{2,1,0:T(8,128)(2,1)} %get-tuple-element.89.wait_ref), channel_id=1, source_target_pairs={{0,2},{1,3},{2,0},{3,1},{4,6},{5,7},{6,4},{7,5},{8,10},{9,11},{10,... | collective-permute-start | bytes 6684680 | tf_op jit(solution)/shard_map/ppermute | solution.py:532
  1021.6 68.3 %all-to-all-start.13 = ((bf16[4,256,1280]{2,1,0:T(8,128)(2,1)}), bf16[4,256,1280]{2,1,0:T(8,128)(2,1)}, u32[]{:S(2)}, u32[]{:S(2)}) async-start(bf16[4,256,1280]{2,1,0:T(8,128)(2,1)} %after.51), calls=%async_computation.17 | async-start | bytes 5242880 | tf_op jit(solution)/shard_map/all_to_all | solution.py:467
  (55 other events, 609.9 us)
Sparse Core Ops, SparseCore 0:
  14.0 117.2 all-gather.5
  371.4 119.5 all-gather.7
  747.9 123.6 all-gather.9
Sparse Core Ops, SparseCore 1:
  219.3 74.1 all-gather.11
  296.3 67.9 reduce-scatter.4
  692.2 51.2 reduce-scatter.6
  910.5 67.9 reduce-scatter.8
  987.3 46.6 reduce-scatter.10

commit v6 on v5

--- a/solution.py
+++ b/solution.py
@@ -318,7 +318,7 @@
 
 
 def column_chunks(width):
-    return [slice(n, min(n + 256, width)) for n in range(0, width, 256)]
+    return [slice(0, width)]
 
 
 def sigmoid(v):
@@ -370,7 +370,7 @@
     split_rows(by_core(part_ref, core), kept_ref, sent_ref, slice(dim, dim + SIDE))
 
 
-def split_kernel(query_ref, kv_ref, out_ref, wait_ref, *piece_refs):
+def split_kernel(query_ref, kv_ref, out_ref, *piece_refs):
     cut = piece_refs[0].shape[1]
     for n, piece_ref in enumerate(piece_refs):
         for head in range(piece_ref.shape[0]):
@@ -586,13 +586,13 @@
     cut, width = part // 2, ffn_maps.shape[2]
     by_head = pl.pallas_call(
         split_kernel,
-        in_specs=[vmem, vmem, vmem, anywhere],
+        in_specs=[vmem, vmem, vmem],
         out_specs=[vmem] * 2,
         out_shape=[shape((zs, cut, count * HS), bf16)] * 2,
         compiler_params=params(),
         name="split",
-    )(query_maps, kv_maps, out_maps, small)
-    att_first = exchange(by_head[0])
+    )(query_maps, kv_maps, out_maps)
+    att_first = exchange(after(by_head[0], small))
     att_half = exchange(after(by_head[1], att_first))
     w_att = assemble([att_first, att_half], [swap(att_first), swap(att_half)])
 

time: 1110 us -> 1110 us (level)
  blocking collectives: 77.8 us -> 63.6 us
    all_to_all x1 -> x0, blocking collectives: 14.8 us -> none  [local(): small = lax.all_to_all(small, ALL, 0, 0, tiled=True)]
    unnamed x83 -> x84, local copies, waits for them, and re-layouts: 25.5 us -> 27.9 us
  transfers between devices with their start and end apart: 50 -> 51, of which waited for: 30 -> 31; matrix products, arithmetic and copies ran while one was open for 21% -> 21% of each run, Pallas kernels for 17% -> 17%
where the time goes in v6:
time: 1110 us; the launch traced here: 1100 us
  waiting for transfers between devices  467 us (42%)
  Pallas kernels  202 us (18%)
  local copies, waits for them, and re-layouts  123 us (11%)
  starting transfers between devices  89.5 us (8%)
  matrix products  70.8 us (6%)
  other arithmetic  69.7 us (6%)
  blocking collectives  63.6 us (6%)
  between operations  16.6 us (1%)
    all_to_all x12, waiting for transfers between devices, exchange(): return lax.all_to_all(value, 'zz', 0, 0, tiled=True)  169 us
    ppermute x18, waiting for transfers between devices, shift(): lax.ppermute(value, axis, [(i, (i + step) % size) for i in range(size)])  147 us
    ppermute x3, waiting for transfers between devices, sum_line(): return add(kept, lax.ppermute(sent, 'tensor', across_line))  64.8 us
    all_to_all x1, blocking collectives, exchange(): return lax.all_to_all(value, 'zz', 0, 0, tiled=True)  63.6 us
    dot_general x3, matrix products, dot_tn(): lax.dot_general(a, b, (((0,), (0,)), ((), ())), preferred_element_type=f32)  53.6 us
    all_to_all x12, starting transfers between devices, exchange(): return lax.all_to_all(value, 'zz', 0, 0, tiled=True)  48 us
    ppermute x1, waiting for transfers between devices, gather_line(): return (by_zz, lax.ppermute(by_zz, 'tensor', across_line))  42.1 us
    pallas_call x1, Pallas kernels, local(): pl.pallas_call(ffn_back_kernel, grid=steps, in_specs=[smem, rows_of(width...  34.3 us
  transfers between devices with their start and end apart: 51, of which 31 were waited for; matrix products, arithmetic and copies ran while one was open for 21% of the time, Pallas kernels for 17%

profile of v6, /device:TPU:0, one launch (start us, length us, event | category | flops | bytes accessed | tf_op | source)
XLA Modules:
  0.0 1102.5 jit_solution(4883891064732074359)
XLA Ops:
  16.9 7.3 all-to-all-start
  33.5 63.6 %all_to_all.74.refs_1_ = bf16[4,128,1280]{2,1,0:T(8,128)(2,1)} all-to-all(bf16[4,128,1280]{2,1,0:T(8,128)(2,1)} %after.28), channel_id=1, replica_groups=mesh['zz'=4,'xx'=2,'tensor'=4] {'zz'}, dimensions={0} | all-to-all | bytes 2621440 | tf_op jit(solution)/shard_map/all_to_all | solution.py:467
  100.7 9.3 cast.1
  117.1 22.8 %all-to-all-done.2.refs_1_ = bf16[4,128,1280]{2,1,0:T(8,128)(2,1)S(1)} async-done(((bf16[4,128,1280]{2,1,0:T(8,128)(2,1)}), bf16[4,128,1280]{2,1,0:T(8,128)(2,1)S(1)}, u32[]{:S(2)}, u32[]{:S(2)}) %all-to-all-start.2) | async-done | bytes 1310752 | tf_op jit(solution)/shard_map/all_to_all | solution.py:467
  154.9 20.4 %collective-permute-done.1 = bf16[4,128,1280]{2,1,0:T(8,128)(2,1)S(1)} collective-permute-done((bf16[4,128,1280]{2,1,0:T(8,128)(2,1)}, bf16[4,128,1280]{2,1,0:T(8,128)(2,1)S(1)}, u32[]{:S(2)}, u32[]{:S(2)}) %collective-permute-start.1) | collective-permute-done | bytes 1310752 | tf_op jit(solution)/shard_map/ppermute | solution.py:451
  185.8 30.4 %att_fwd.1 = (bf16[2,4,128,2048]{3,2,1,0:T(8,128)(2,1)}, bf16[2,4,128,2048]{3,2,1,0:T(8,128)(2,1)}, bf16[2048,2048]{1,0:T(8,128)(2,1)}, bf16[2048,768]{1,0:T(8,128)(2,1)}, f32[2048,128]{1,0:T(8,128)}) custom-call(s32[1]{0:T(128)} %bitcast.core_ref, bf16[2048,2176]{1,0:T(8,128)(2,1)} %all-gather.6.cloned.1.call-done.tok_ref.side_ref, ...), custom_call_target="tpu_custom_call" | custom-call | flops 199999995904 | bytes 1000000 | tf_op jit(solution)/shard_map/att_fwd/pallas_call | solution.py:637
  236.9 41.4 %collective-permute-done.4 = bf16[4,128,2048]{2,1,0:T(8,128)(2,1)} collective-permute-done((bf16[4,128,2048]{2,1,0:T(8,128)(2,1)}, bf16[4,128,2048]{2,1,0:T(8,128)(2,1)}, u32[]{:S(2)}, u32[]{:S(2)}) %collective-permute-start.4) | collective-permute-done | bytes 2097184 | tf_op jit(solution)/shard_map/ppermute | solution.py:532
  283.9 10.2 all-gather.12.cloned.1.call-done
  306.8 42.1 %collective-permute-done.7.refs_2_ = bf16[4,128,2048]{2,1,0:T(8,128)(2,1)} collective-permute-done((bf16[4,128,2048]{2,1,0:T(8,128)(2,1)}, bf16[4,128,2048]{2,1,0:T(8,128)(2,1)}, u32[]{:S(2)}, u32[]{:S(2)}) %collective-permute-start.7) | collective-permute-done | bytes 2097184 | tf_op jit(solution)/shard_map/ppermute | solution.py:494
  348.9 19.0 %all-to-all-done.6.refs_0_.refs_1_ = bf16[4,128,1408]{2,1,0:T(8,128)(2,1)S(1)} async-done(((bf16[4,128,1408]{2,1,0:T(8,128)(2,1)}), bf16[4,128,1408]{2,1,0:T(8,128)(2,1)S(1)}, u32[]{:S(2)}, u32[]{:S(2)}) %all-to-all-start.6) | async-done | bytes 1441824 | tf_op jit(solution)/shard_map/all_to_all | solution.py:467
  413.7 40.0 %all-to-all-done.7.refs_1_ = bf16[4,128,1408]{2,1,0:T(8,128)(2,1)} async-done(((bf16[4,128,1408]{2,1,0:T(8,128)(2,1)}), bf16[4,128,1408]{2,1,0:T(8,128)(2,1)}, u32[]{:S(2)}, u32[]{:S(2)}) %all-to-all-start.7) | async-done | bytes 1441824 | tf_op jit(solution)/shard_map/all_to_all | solution.py:467
  471.5 20.2 %collective-permute-done.10 = bf16[4,128,1408]{2,1,0:T(8,128)(2,1)S(1)} collective-permute-done((bf16[4,128,1408]{2,1,0:T(8,128)(2,1)}, bf16[4,128,1408]{2,1,0:T(8,128)(2,1)S(1)}, u32[]{:S(2)}, u32[]{:S(2)}) %collective-permute-start.10) | collective-permute-done | bytes 1441824 | tf_op jit(solution)/shard_map/ppermute | solution.py:451
  501.2 33.5 %ffn_fwd.1 = (bf16[2048,1408]{1,0:T(8,128)(2,1)}, bf16[2048,1408]{1,0:T(8,128)(2,1)}, bf16[2048,1408]{1,0:T(8,128)(2,1)}) custom-call(s32[1]{0:T(128)} %bitcast.23.where_ref, bf16[2048,2176]{1,0:T(8,128)(2,1)} %all-gather.8.cloned.1.call-done.x_ref.side_ref, bf16[2048,1408]{1,0:T(8,128)(2,1)} %bitcast.30.wg_ref, bf16[2048,1408]{1,0:T(8,128)(2,1)} %bitcast.37.wu_ref), custom_call_target="tpu_custom_call" | custom-call | flops 199999995904 | bytes 1000000 | tf_op jit(solution)/shard_map/ffn_fwd/pallas_call | solution.py:676
  534.7 17.2 %convolution_convert_fusion.3.wait_ref = bf16[2048,1408]{1,0:T(8,128)(2,1)S(1)} fusion(bf16[2048,2048]{1,0:T(8,128)(2,1)} %bitcast.45.c_ref, bf16[2048,1408]{1,0:T(8,128)(2,1)} %get-tuple-element.56.refs_1_.refs_0_), kind=kOutput, calls=%fused_computation.6 | convolution fusion | flops 11814043648 | bytes 19922944 | tf_op jit(solution)/shard_map/dot_general | solution.py:32
  563.9 25.0 %ffn_act.1 = (bf16[2048,1408]{1,0:T(8,128)(2,1)}, bf16[2048,1408]{1,0:T(8,128)(2,1)}, bf16[2048,128]{1,0:T(8,128)(2,1)}) custom-call(s32[1]{0:T(128)} %bitcast.23.where_ref, bf16[2048,2176]{1,0:T(8,128)(2,1)} %all-gather.8.cloned.1.call-done.x_ref.side_ref, bf16[2048,1408]{1,0:T(8,128)(2,1)} %get-tuple-element.57.gate_ref, ...), custom_call_target="tpu_custom_call" | custom-call | flops 199999995904 | bytes 1000000 | tf_op jit(solution)/shard_map/ffn_act/pallas_call | solution.py:693
  590.4 34.3 %ffn_back.1 = (bf16[2,4,128,2176]{3,2,1,0:T(8,128)(2,1)}, bf16[2,4,128,2176]{3,2,1,0:T(8,128)(2,1)}) custom-call(s32[1]{0:T(128)} %bitcast.core_ref, bf16[2048,1408]{1,0:T(8,128)(2,1)} %get-tuple-element.62.gg_ref.refs_0_, bf16[2048,1408]{1,0:T(8,128)(2,1)} %get-tuple-element.61.ug_ref.refs_0_, bf16[2048,128]{1,0:T(8,128)(2,1)} %get-tuple-element.63.part_ref, ...), custom_call_target="tpu_custom_call" | custom-call | flops 199999995904 | bytes 1000000 | tf_op jit(solution)/shard_map/ffn_back/pallas_call | solution.py:708
  641.8 17.4 %convolution_convert_fusion.2.refs_1_ = bf16[2048,1408]{1,0:T(8,128)(2,1)S(1)} fusion(bf16[2048,1408]{1,0:T(8,128)(2,1)} %after.41, bf16[2048,2176]{1,0:T(8,128)(2,1)} %all-gather.8.cloned.1.call-done.x_ref.side_ref), kind=kOutput, calls=%fused_computation.5 | convolution fusion | flops 11814043648 | bytes 19922944 | tf_op jit(solution)/shard_map/dot_general | solution.py:32
  664.0 23.4 %collective-permute-done.15 = bf16[4,128,2176]{2,1,0:T(8,128)(2,1)} collective-permute-done((bf16[4,128,2176]{2,1,0:T(8,128)(2,1)}, bf16[4,128,2176]{2,1,0:T(8,128)(2,1)}, u32[]{:S(2)}, u32[]{:S(2)}) %collective-permute-start.15) | collective-permute-done | bytes 2228256 | tf_op jit(solution)/shard_map/ppermute | solution.py:532
  692.6 19.0 %convolution_convert_fusion.1.refs_1_ = bf16[2048,1408]{1,0:T(8,128)(2,1)} fusion(bf16[2048,1408]{1,0:T(8,128)(2,1)} %after.42, bf16[2048,2176]{1,0:T(8,128)(2,1)} %all-gather.8.cloned.1.call-done.x_ref.side_ref), kind=kOutput, calls=%fused_computation.4 | convolution fusion | flops 11814043648 | bytes 19922944 | tf_op jit(solution)/shard_map/dot_general | solution.py:32
  711.7 17.2 %convolution_convert_fusion = bf16[2048,2048]{1,0:T(8,128)(2,1)S(1)} fusion(bf16[2048,1408]{1,0:T(8,128)(2,1)} %after.43, bf16[2048,1408]{1,0:T(8,128)(2,1)} %bitcast.54.wd_ref), kind=kOutput, calls=%fused_computation.3 | convolution fusion | flops 11815354368 | bytes 19922944 | tf_op jit(solution)/shard_map/dot_general | solution.py:28
  758.0 7.8 fusion.refs_0_
  768.1 49.3 %collective-permute-done.19 = bf16[4,256,1408]{2,1,0:T(8,128)(2,1)} collective-permute-done((bf16[4,256,1408]{2,1,0:T(8,128)(2,1)}, bf16[4,256,1408]{2,1,0:T(8,128)(2,1)}, u32[]{:S(2)}, u32[]{:S(2)}) %collective-permute-start.19) | collective-permute-done | bytes 2883616 | tf_op jit(solution)/shard_map/ppermute | solution.py:451
  830.5 39.8 %all-to-all-done.10.refs_1_ = bf16[4,256,1408]{2,1,0:T(8,128)(2,1)S(1)} async-done(((bf16[4,256,1408]{2,1,0:T(8,128)(2,1)}), bf16[4,256,1408]{2,1,0:T(8,128)(2,1)S(1)}, u32[]{:S(2)}, u32[]{:S(2)}) %all-to-all-start.10) | async-done | bytes 2883616 | tf_op jit(solution)/shard_map/all_to_all | solution.py:467
  876.2 30.2 %att_bwd.1 = (bf16[2,4,128,2176]{3,2,1,0:T(8,128)(2,1)}, bf16[2,4,128,2176]{3,2,1,0:T(8,128)(2,1)}, bf16[2048,768]{1,0:T(8,128)(2,1)}, bf16[2048,512]{1,0:T(8,128)(2,1)}) custom-call(s32[1]{0:T(128)} %bitcast.core_ref, bf16[2048,2048]{1,0:T(8,128)(2,1)} %after.47.refs_1_.c_ref, bf16[2048,1280]{1,0:T(8,128)(2,1)} %bitcast.16.w_ref, ...), custom_call_target="tpu_custom_call" | custom-call | flops 199999995904 | bytes 1000000 | tf_op jit(solution)/shard_map/att_bwd/pallas_call | solution.py:772
  918.7 6.9 fusion.12
  927.1 16.6 %att_grad.1 = bf16[2048,1280]{1,0:T(8,128)(2,1)} custom-call(bf16[2048,2048]{1,0:T(8,128)(2,1)} %get-tuple-element.72.x_ref, bf16[2048,2048]{1,0:T(8,128)(2,1)} %after.47.refs_1_.c_ref, bf16[2048,768]{1,0:T(8,128)(2,1)} %get-tuple-element.73.grad_ref, bf16[2048,512]{1,0:T(8,128)(2,1)} %get-tuple-element.74.z_ref, ...), custom_call_target="tpu_custom_call" | custom-call | flops 10737418240 | bytes 25165824 | tf_op jit(solution)/shard_map/att_grad/pallas_call | solution.py:790
  950.4 31.4 %all-to-all-done.12.refs_5_.refs_1_ = bf16[4,128,1408]{2,1,0:T(8,128)(2,1)S(1)} async-done(((bf16[4,128,1408]{2,1,0:T(8,128)(2,1)}), bf16[4,128,1408]{2,1,0:T(8,128)(2,1)S(1)}, u32[]{:S(2)}, u32[]{:S(2)}) %all-to-all-start.12) | async-done | bytes 1441824 | tf_op jit(solution)/shard_map/all_to_all | solution.py:467
  989.9 27.8 %collective-permute-done.29 = bf16[2,256,1280]{2,1,0:T(8,128)(2,1)} collective-permute-done((bf16[2,256,1280]{2,1,0:T(8,128)(2,1)S(1)}, bf16[2,256,1280]{2,1,0:T(8,128)(2,1)}, u32[]{:S(2)}, u32[]{:S(2)}) %collective-permute-start.29) | collective-permute-done | bytes 1310752 | tf_op jit(solution)/shard_map/ppermute | solution.py:451
  1027.0 7.5 reduce-scatter.11.cloned.1.call-done
  1046.7 8.7 maximum_convert_fusion
  1062.6 13.4 %collective-permute-done.26 = f32[640]{0:T(1024)S(1)} collective-permute-done((f32[640]{0:T(1024)S(1)}, f32[640]{0:T(1024)S(1)}, u32[]{:S(2)}, u32[]{:S(2)}) %collective-permute-start.26) | collective-permute-done | bytes 2592 | tf_op jit(solution)/shard_map/ppermute | solution.py:451
  1075.9 13.2 %collective-permute-done.27 = f32[640]{0:T(1024)S(1)} collective-permute-done((f32[640]{0:T(1024)S(1)}, f32[640]{0:T(1024)S(1)}, u32[]{:S(2)}, u32[]{:S(2)}) %collective-permute-start.27) | collective-permute-done | bytes 2592 | tf_op jit(solution)/shard_map/ppermute | solution.py:451
  (300 shorter events, 319.7 us)
Async XLA Ops:
  8.0 177.8 %all-gather.6.cloned.1.call-start = ((), (), s32[]{:S(2)}) async-start(), calls=%async_computation.18 | async-start | bytes 9469952 | tf_op jit(solution)/shard_map/all_gather | solution.py:565
  97.2 42.7 %all-to-all-start.2 = ((bf16[4,128,1280]{2,1,0:T(8,128)(2,1)}), bf16[4,128,1280]{2,1,0:T(8,128)(2,1)S(1)}, u32[]{:S(2)}, u32[]{:S(2)}) async-start(bf16[4,128,1280]{2,1,0:T(8,128)(2,1)} %after.29), calls=%async_computation.2 | async-start | bytes 2621440 | tf_op jit(solution)/shard_map/all_to_all | solution.py:467
  112.8 38.5 %collective-permute-start = (bf16[4,128,1280]{2,1,0:T(8,128)(2,1)}, bf16[4,128,1280]{2,1,0:T(8,128)(2,1)}, u32[]{:S(2)}, u32[]{:S(2)}) collective-permute-start(bf16[4,128,1280]{2,1,0:T(8,128)(2,1)} %all_to_all.74.refs_1_), channel_id=1, source_target_pairs={{0,4},{4,0},{1,5},{5,1},{2,6},{6,2},{3,7},{7,3},{8,12},{12,8},{9,1... | collective-permute-start | bytes 3932168 | tf_op jit(solution)/shard_map/ppermute | solution.py:451
  184.4 109.7 %all-gather.12.cloned.1.call-start = ((), (), s32[]{:S(2)}) async-start(), calls=%async_computation.25 | async-start | bytes 2621440 | tf_op jit(solution)/shard_map/all_gather | solution.py:493
  230.3 47.9 %collective-permute-start.4 = (bf16[4,128,2048]{2,1,0:T(8,128)(2,1)}, bf16[4,128,2048]{2,1,0:T(8,128)(2,1)}, u32[]{:S(2)}, u32[]{:S(2)}) collective-permute-start(bf16[4,128,2048]{2,1,0:T(8,128)(2,1)} %fusion.15), channel_id=1, source_target_pairs={{0,2},{1,3},{2,0},{3,1},{4,6},{5,7},{6,4},{7,5},{8,10},{9,11},{10,... | collective-permute-start | bytes 6291464 | tf_op jit(solution)/shard_map/ppermute | solution.py:532
  231.6 62.5 %collective-permute-start.5 = (bf16[4,128,1408]{2,1,0:T(8,128)(2,1)}, bf16[4,128,1408]{2,1,0:T(8,128)(2,1)S(1)}, u32[]{:S(2)}, u32[]{:S(2)}) collective-permute-start(bf16[4,128,1408]{2,1,0:T(8,128)(2,1)} %all-to-all-done.4.refs_2_.refs_1_), channel_id=1, source_target_pairs={{0,4},{4,0},{1,5},{5,1},{2,6},{6,2},{3,7},{7,3},{8,12},{12,8},{9,1... | collective-permute-start | bytes 4325384 | tf_op jit(solution)/shard_map/ppermute | solution.py:451
  233.1 63.3 %all-to-all-start.5 = ((bf16[4,128,1408]{2,1,0:T(8,128)(2,1)}), bf16[4,128,1408]{2,1,0:T(8,128)(2,1)S(1)}, u32[]{:S(2)}, u32[]{:S(2)}) async-start(bf16[4,128,1408]{2,1,0:T(8,128)(2,1)} %after.35), calls=%async_computation.6 | async-start | bytes 2883584 | tf_op jit(solution)/shard_map/all_to_all | solution.py:467
  236.9 131.0 %reduce-scatter.5.cloned.1.call-start = ((), (), s32[]{:S(2)}) async-start(), calls=%async_computation.19 | async-start | bytes 2621440 | tf_op jit(solution)/shard_map/reduce_scatter | solution.py:656
  297.5 70.4 %all-to-all-start.6 = ((bf16[4,128,1408]{2,1,0:T(8,128)(2,1)}), bf16[4,128,1408]{2,1,0:T(8,128)(2,1)S(1)}, u32[]{:S(2)}, u32[]{:S(2)}) async-start(bf16[4,128,1408]{2,1,0:T(8,128)(2,1)} %after.36), calls=%async_computation.7 | async-start | bytes 2883584 | tf_op jit(solution)/shard_map/all_to_all | solution.py:467
  301.1 200.1 %all-gather.8.cloned.1.call-start = ((), (), s32[]{:S(2)}) async-start(), calls=%async_computation.20 | async-start | bytes 9469952 | tf_op jit(solution)/shard_map/all_gather | solution.py:667
  301.2 47.8 %collective-permute-start.7 = (bf16[4,128,2048]{2,1,0:T(8,128)(2,1)}, bf16[4,128,2048]{2,1,0:T(8,128)(2,1)}, u32[]{:S(2)}, u32[]{:S(2)}) collective-permute-start(bf16[4,128,2048]{2,1,0:T(8,128)(2,1)} %bitcast.232), channel_id=1, source_target_pairs={{0,2},{1,3},{2,0},{3,1},{4,6},{5,7},{6,4},{7,5},{8,10},{9,11},{10,... | collective-permute-start | bytes 6291464 | tf_op jit(solution)/shard_map/ppermute | solution.py:494
  302.7 46.2 %collective-permute-start.6 = (bf16[4,128,1408]{2,1,0:T(8,128)(2,1)}, bf16[4,128,1408]{2,1,0:T(8,128)(2,1)}, u32[]{:S(2)}, u32[]{:S(2)}) collective-permute-start(bf16[4,128,1408]{2,1,0:T(8,128)(2,1)} %copy-done.11), channel_id=1, source_target_pairs={{0,4},{4,0},{1,5},{5,1},{2,6},{6,2},{3,7},{7,3},{8,12},{12,8},{9,1... | collective-permute-start | bytes 4325384 | tf_op jit(solution)/shard_map/ppermute | solution.py:451
  386.5 80.2 %collective-permute-start.9 = (bf16[4,2,128,2048]{3,2,1,0:T(8,128)(2,1)}, bf16[4,2,128,2048]{3,2,1,0:T(8,128)(2,1)}, u32[]{:S(2)}, u32[]{:S(2)}) collective-permute-start(bf16[4,2,128,2048]{3,2,1,0:T(8,128)(2,1)} %bitcast_dynamic-update-slice_fusion.2), channel_id=1, source_target_pairs={{0,1},{1,0},{2,3},{3,2},{4,5},{5,4},{6,7},{7,6},{8,9},{9,8},{10,11... | collective-permute-start | bytes 12582920 | tf_op jit(solution)/shard_map/ppermute | solution.py:500
  390.3 63.4 %all-to-all-start.7 = ((bf16[4,128,1408]{2,1,0:T(8,128)(2,1)}), bf16[4,128,1408]{2,1,0:T(8,128)(2,1)}, u32[]{:S(2)}, u32[]{:S(2)}) async-start(bf16[4,128,1408]{2,1,0:T(8,128)(2,1)} %after.37), calls=%async_computation.8 | async-start | bytes 2883584 | tf_op jit(solution)/shard_map/all_to_all | solution.py:467
  399.2 60.6 %collective-permute-start.8 = (bf16[4,128,1408]{2,1,0:T(8,128)(2,1)S(1)}, bf16[4,128,1408]{2,1,0:T(8,128)(2,1)S(1)}, u32[]{:S(2)}, u32[]{:S(2)}) collective-permute-start(bf16[4,128,1408]{2,1,0:T(8,128)(2,1)S(1)} %copy-done.14), channel_id=1, source_target_pairs={{0,4},{4,0},{1,5},{5,1},{2,6},{6,2},{3,7},{7,3},{8,12},{12,8},{9,1... | collective-permute-start | bytes 4325384 | tf_op jit(solution)/shard_map/ppermute | solution.py:451
  453.7 46.0 %all-to-all-start.8 = ((bf16[4,128,1408]{2,1,0:T(8,128)(2,1)}), bf16[4,128,1408]{2,1,0:T(8,128)(2,1)}, u32[]{:S(2)}, u32[]{:S(2)}) async-start(bf16[4,128,1408]{2,1,0:T(8,128)(2,1)} %after.39), calls=%async_computation.9 | async-start | bytes 2883584 | tf_op jit(solution)/shard_map/all_to_all | solution.py:467
  499.8 61.6 %collective-permute-start.11 = (bf16[4,128,1408]{2,1,0:T(8,128)(2,1)}, bf16[4,128,1408]{2,1,0:T(8,128)(2,1)}, u32[]{:S(2)}, u32[]{:S(2)}) collective-permute-start(bf16[4,128,1408]{2,1,0:T(8,128)(2,1)} %all-to-all-done.8), channel_id=1, source_target_pairs={{0,4},{4,0},{1,5},{5,1},{2,6},{6,2},{3,7},{7,3},{8,12},{12,8},{9,1... | collective-permute-start | bytes 4325384 | tf_op jit(solution)/shard_map/ppermute | solution.py:451
  557.3 67.4 %collective-permute-start.13 = (bf16[2,256,1408]{2,1,0:T(8,128)(2,1)}, bf16[2,256,1408]{2,1,0:T(8,128)(2,1)}, u32[]{:S(2)}, u32[]{:S(2)}) collective-permute-start(bf16[2,256,1408]{2,1,0:T(8,128)(2,1)} %dynamic-slice_bitcast_fusion.4), channel_id=1, source_target_pairs={{0,4},{4,0},{1,5},{5,1},{2,6},{6,2},{3,7},{7,3},{8,12},{12,8},{9,1... | collective-permute-start | bytes 4325384 | tf_op jit(solution)/shard_map/ppermute | solution.py:451
  636.6 50.8 %collective-permute-start.15 = (bf16[4,128,2176]{2,1,0:T(8,128)(2,1)}, bf16[4,128,2176]{2,1,0:T(8,128)(2,1)}, u32[]{:S(2)}, u32[]{:S(2)}) collective-permute-start(bf16[4,128,2176]{2,1,0:T(8,128)(2,1)} %fusion.10.refs_1_), channel_id=1, source_target_pairs={{0,2},{1,3},{2,0},{3,1},{4,6},{5,7},{6,4},{7,5},{8,10},{9,11},{10,... | collective-permute-start | bytes 6684680 | tf_op jit(solution)/shard_map/ppermute | solution.py:532
  638.1 100.4 %all-to-all-start.9 = ((bf16[4,256,1408]{2,1,0:T(8,128)(2,1)}), bf16[4,256,1408]{2,1,0:T(8,128)(2,1)S(1)}, u32[]{:S(2)}, u32[]{:S(2)}) async-start(bf16[4,256,1408]{2,1,0:T(8,128)(2,1)} %after.45), calls=%async_computation.11 | async-start | bytes 5767168 | tf_op jit(solution)/shard_map/all_to_all | solution.py:467
  641.8 102.1 %reduce-scatter.7.cloned.1.call-start = ((), (), s32[]{:S(2)}) async-start(), calls=%async_computation.21 | async-start | bytes 2785280 | tf_op jit(solution)/shard_map/reduce_scatter | solution.py:720
  663.4 70.1 %collective-permute-start.17 = (bf16[4,256,1408]{2,1,0:T(8,128)(2,1)}, bf16[4,256,1408]{2,1,0:T(8,128)(2,1)}, u32[]{:S(2)}, u32[]{:S(2)}) collective-permute-start(bf16[4,256,1408]{2,1,0:T(8,128)(2,1)} %dynamic-slice_bitcast_fusion.2), channel_id=1, source_target_pairs={{0,4},{4,0},{1,5},{5,1},{2,6},{6,2},{3,7},{7,3},{8,12},{12,8},{9,1... | collective-permute-start | bytes 8650760 | tf_op jit(solution)/shard_map/ppermute | solution.py:451
  692.6 183.6 %all-gather.10.cloned.1.call-start = ((), (), s32[]{:S(2)}) async-start(), calls=%async_computation.22 | async-start | bytes 8912896 | tf_op jit(solution)/shard_map/all_gather | solution.py:766
  752.2 65.2 %collective-permute-start.19 = (bf16[4,256,1408]{2,1,0:T(8,128)(2,1)}, bf16[4,256,1408]{2,1,0:T(8,128)(2,1)}, u32[]{:S(2)}, u32[]{:S(2)}) collective-permute-start(bf16[4,256,1408]{2,1,0:T(8,128)(2,1)} %dynamic-slice_bitcast_fusion.1), channel_id=1, source_target_pairs={{0,4},{4,0},{1,5},{5,1},{2,6},{6,2},{3,7},{7,3},{8,12},{12,8},{9,1... | collective-permute-start | bytes 8650760 | tf_op jit(solution)/shard_map/ppermute | solution.py:451
  754.3 116.0 %all-to-all-start.10 = ((bf16[4,256,1408]{2,1,0:T(8,128)(2,1)}), bf16[4,256,1408]{2,1,0:T(8,128)(2,1)S(1)}, u32[]{:S(2)}, u32[]{:S(2)}) async-start(bf16[4,256,1408]{2,1,0:T(8,128)(2,1)} %after.46), calls=%async_computation.12 | async-start | bytes 5767168 | tf_op jit(solution)/shard_map/all_to_all | solution.py:467
  767.5 60.9 %collective-permute-start.18 = (bf16[4,128,2048]{2,1,0:T(8,128)(2,1)S(1)}, bf16[4,128,2048]{2,1,0:T(8,128)(2,1)S(1)}, u32[]{:S(2)}, u32[]{:S(2)}) collective-permute-start(bf16[4,128,2048]{2,1,0:T(8,128)(2,1)S(1)} %dynamic-slice_bitcast_fusion.3), channel_id=1, source_target_pairs={{0,2},{1,3},{2,0},{3,1},{4,6},{5,7},{6,4},{7,5},{8,10},{9,11},{10,... | collective-permute-start | bytes 6291464 | tf_op jit(solution)/shard_map/ppermute | solution.py:510
  871.8 39.0 %all-to-all-start.11 = ((bf16[4,128,1408]{2,1,0:T(8,128)(2,1)}), bf16[4,128,1408]{2,1,0:T(8,128)(2,1)}, u32[]{:S(2)}, u32[]{:S(2)}) async-start(bf16[4,128,1408]{2,1,0:T(8,128)(2,1)} %after.49), calls=%async_computation.14 | async-start | bytes 2883584 | tf_op jit(solution)/shard_map/all_to_all | solution.py:467
  876.1 105.6 %reduce-scatter.9.cloned.1.call-start = ((), (), s32[]{:S(2)}) async-start(), calls=%async_computation.23 | async-start | bytes 2621440 | tf_op jit(solution)/shard_map/reduce_scatter | solution.py:769
  910.9 70.9 %all-to-all-start.12 = ((bf16[4,128,1408]{2,1,0:T(8,128)(2,1)}), bf16[4,128,1408]{2,1,0:T(8,128)(2,1)S(1)}, u32[]{:S(2)}, u32[]{:S(2)}) async-start(bf16[4,128,1408]{2,1,0:T(8,128)(2,1)} %after.51), calls=%async_computation.15 | async-start | bytes 2883584 | tf_op jit(solution)/shard_map/all_to_all | solution.py:467
  914.4 120.0 %reduce-scatter.11.cloned.1.call-start = ((), (), s32[]{:S(2)}) async-start(), calls=%async_computation.24 | async-start | bytes 2785280 | tf_op jit(solution)/shard_map/reduce_scatter | solution.py:806
  925.6 57.7 %collective-permute-start.22 = (bf16[4,128,2176]{2,1,0:T(8,128)(2,1)}, bf16[4,128,2176]{2,1,0:T(8,128)(2,1)}, u32[]{:S(2)}, u32[]{:S(2)}) collective-permute-start(bf16[4,128,2176]{2,1,0:T(8,128)(2,1)} %get-tuple-element.89.wait_ref), channel_id=1, source_target_pairs={{0,2},{1,3},{2,0},{3,1},{4,6},{5,7},{6,4},{7,5},{8,10},{9,11},{10,... | collective-permute-start | bytes 6684680 | tf_op jit(solution)/shard_map/ppermute | solution.py:532
  1022.0 68.3 %all-to-all-start.13 = ((bf16[4,256,1280]{2,1,0:T(8,128)(2,1)}), bf16[4,256,1280]{2,1,0:T(8,128)(2,1)}, u32[]{:S(2)}, u32[]{:S(2)}) async-start(bf16[4,256,1280]{2,1,0:T(8,128)(2,1)} %after.53), calls=%async_computation.17 | async-start | bytes 5242880 | tf_op jit(solution)/shard_map/all_to_all | solution.py:467
  (56 other events, 625.7 us)
Sparse Core Ops, SparseCore 0:
  14.0 119.6 all-gather.5
  372.2 119.5 all-gather.7
  748.4 123.5 all-gather.9
Sparse Core Ops, SparseCore 1:
  220.1 74.0 all-gather.11
  296.8 66.9 reduce-scatter.4
  692.7 51.2 reduce-scatter.6
  910.9 68.0 reduce-scatter.8
  987.8 46.6 reduce-scatter.10
